TPU v7x, 128 devices: a whole 4x4x4 slice. The times are simulated.
128 devices in a mesh: row: 8 (over y, z_hi), col: 16 (over x, z_lo, core).
Axes of the slice: x: 4, y: 4, z: 4 (z_hi: 2, z_lo: 2; z = z_hi * 2 + z_lo), core: 2. Of those that a mesh axis runs over, the one named last changes fastest.
Arguments:
- panel_left: bfloat16 [5000, 128, 128], P(None, ('row', 'col')), may hold values from -0.078125 to 0.078125
- panel_right: bfloat16 [5000, 128, 128], P(None, ('row', 'col')), may hold values from -6 to 6
- amplitudes: bfloat16 [256, 128, 128], P('col', 'row'), may hold values from -0.046875 to 0.046875
- eps_virtual: float32 [1600], replicated, may hold values from 0.2 to 1.5
- eps_occupied: float32 [100], replicated, may hold values from -1.5 to -0.3
- pair_list: int32 [256, 2], replicated, may hold values from 0 to 99
- blocks: int32 [2], replicated, may hold values from 0 to 11
Outputs:
- update: bfloat16 [256, 128, 128], P('col', 'row')
All inputs are finite; a program needn't handle non-finite values.
Results may differ from a plain program's by a relative error of at most 0.0049.
Values may be sent and summed in bfloat16 or wider, within the bound.
No kernel may reach another device: no remote copies, remote signals or barrier semaphores. Data moves between devices by JAX's collectives and lax.ppermute only.
A program may use at most 128 MiB of HBM per device.

v0:
```python
import jax
import jax.numpy as jnp
from jax import lax
from jax.sharding import PartitionSpec as P


def pair_energy(pair_list, eps_occupied):
    levels = jnp.arange(eps_occupied.shape[0], dtype=jnp.int32)
    picked = (pair_list[:, :, None] == levels[None, None, :]).astype(jnp.float32)
    return jnp.sum(picked * eps_occupied[None, None, :], axis=(1, 2))


def select_column(matrix, column_index):
    onehot = (jnp.arange(matrix.shape[1], dtype=jnp.int32) == column_index).astype(jnp.float32)
    return jnp.sum(matrix * onehot[None, :], axis=1)


def ladder_block(left_panel, right_panel, amp_full):
    fit_count = left_panel.shape[0]
    a_count = left_panel.shape[1]
    b_count = right_panel.shape[1]
    block_width = left_panel.shape[2]
    flat_block = lax.dot_general(
        left_panel.reshape(fit_count, a_count * block_width),
        right_panel.reshape(fit_count, b_count * block_width),
        (((0,), (0,)), ((), ())),
        preferred_element_type=jnp.float32,
    )
    integrals = flat_block.astype(jnp.bfloat16).reshape(a_count, block_width, b_count, block_width)
    return jnp.einsum("acbd,pcd->pab", integrals, amp_full, preferred_element_type=jnp.float32)


def shards(panel_left, panel_right, amplitudes, eps_virtual, eps_occupied, pair_list, blocks):
    row_count = lax.axis_size("row")
    col_count = lax.axis_size("col")
    row_index = lax.axis_index("row")
    col_index = lax.axis_index("col")
    window = row_count * col_count
    amp_part = lax.all_gather(amplitudes, "row", axis=1, tiled=True)
    amp_full = lax.all_gather(amp_part, "col", axis=0, tiled=True)
    pair_sum = pair_energy(pair_list, eps_occupied)
    first_all = lax.dynamic_slice_in_dim(eps_virtual, blocks[0] * window, window)
    second_all = lax.dynamic_slice_in_dim(eps_virtual, blocks[1] * window, window)
    left_whole = lax.all_gather(panel_left, "row", axis=1, tiled=True)
    ladder_part = ladder_block(
        left_whole, lax.all_gather(panel_right, "col", axis=1, tiled=True), amp_full
    )
    first_energy = select_column(first_all.reshape(row_count, col_count), col_index)
    second_energy = lax.dynamic_slice_in_dim(second_all, row_index * col_count, col_count)
    denominator = (
        first_energy[None, :, None] + second_energy[None, None, :] - pair_sum[:, None, None]
    )
    update = (ladder_part / denominator).astype(jnp.bfloat16)
    pair_layout = lax.all_to_all(
        lax.all_to_all(update[:, :, None, :], "row", split_axis=1, concat_axis=2, tiled=True),
        "col",
        split_axis=0,
        concat_axis=1,
        tiled=True,
    )
    return pair_layout.reshape(pair_layout.shape[0], col_count, window)


def solution(mesh):
    return jax.shard_map(
        shards,
        mesh=mesh,
        in_specs=(
            P(None, ("row", "col"), None),
            P(None, ("row", "col"), None),
            P("col", "row", None),
            P(),
            P(),
            P(),
            P(),
        ),
        out_specs=P("col", "row", None),
        check_vma=False,
    )
```

profile of v0, /device:TPU:1, one launch (start us, length us, event | category | flops | bytes accessed | tf_op | source)
XLA Modules:
  0.0 355.8 jit_solution(10827159034960426650)
XLA Ops:
  6.5 0.7 all-gather.4.cloned.1.call-update
  7.3 0.7 all-gather.6.cloned.1.call-update
  8.1 0.9 copy.25
  8.9 33.7 %all_gather.14 = bf16[16,128,128]{2,0,1:T(8,128)(2,1)} all-gather(bf16[16,16,128]{2,0,1:T(8,128)(2,1)S(1)} %copy.25), channel_id=1, replica_groups=mesh['row'=8,'col'=16] {'row'}, dimensions={1}, use_global_device_ids=true | all-gather | bytes 589824 | tf_op jit(solution)/shard_map/all_gather | solution.py:39
  42.6 1.4 fusion.24
  45.3 0.8 dynamic_slice.11
  46.1 0.8 dynamic_slice.9
  47.0 0.1 multiply_reduce_fusion
  47.1 0.9 fusion.23
  48.1 95.8 %all-gather.4.cloned.1.call-done = bf16[5000,8,128]{2,0,1:T(8,128)(2,1)} async-done(((bf16[5000,1,128]{2,0,1:T(8,128)(2,1)}), bf16[5000,8,128]{2,0,1:T(8,128)(2,1)}) %all-gather.4.cloned.1.call-update) | async-done | bytes 10240016 | tf_op jit(solution)/shard_map/all_gather | solution.py:44
  143.8 13.9 %copy.23 = bf16[5000,8,128]{0,2,1:T(8,128)(2,1)} copy(bf16[5000,8,128]{2,0,1:T(8,128)(2,1)} %all-gather.4.cloned.1.call-done) | data formatting | bytes 20480000 | tf_op jit(solution)/shard_map/all_gather | solution.py:44
  157.7 95.5 %all-gather.6.cloned.1.call-done = bf16[5000,16,128]{2,0,1:T(8,128)(2,1)} async-done(((bf16[5000,1,128]{2,0,1:T(8,128)(2,1)}), bf16[5000,16,128]{2,0,1:T(8,128)(2,1)}) %all-gather.6.cloned.1.call-update) | async-done | bytes 20480016 | tf_op jit(solution)/shard_map/all_gather | solution.py:46
  253.2 26.0 %copy.24 = bf16[5000,16,128]{0,2,1:T(8,128)(2,1)} copy(bf16[5000,16,128]{2,0,1:T(8,128)(2,1)} %all-gather.6.cloned.1.call-done) | data formatting | bytes 40960000 | tf_op jit(solution)/shard_map/all_gather | solution.py:46
  279.2 26.8 %convert_bitcast_fusion = bf16[128,8,16,128]{3,1,2,0:T(8,128)(2,1)S(1)} fusion(bf16[5000,1024]{0,1:T(8,128)(2,1)} %bitcast.58, bf16[5000,2048]{0,1:T(8,128)(2,1)} %bitcast.56), kind=kOutput, calls=%fused_computation.3 | convolution fusion | flops 20973617152 | bytes 34914304 | tf_op jit(solution)/shard_map/dot_general | solution.py:23
  306.0 3.4 copy.31
  309.4 6.7 %all-gather.8.cloned.1.call-done = bf16[256,128,128]{2,0,1:T(8,128)(2,1)} async-done(((bf16[16,128,128]{2,0,1:T(8,128)(2,1)}), bf16[256,128,128]{2,0,1:T(8,128)(2,1)}) %all-gather.8.cloned.1.call-update) | async-done | bytes 8388624 | tf_op jit(solution)/shard_map/all_gather | solution.py:40
  316.1 7.5 %fusion.18 = bf16[256,8,1,16]{0,3,2,1:T(8,128)(2,1)S(1)} fusion(bf16[256,128,128]{2,0,1:T(8,128)(2,1)} %all-gather.8.cloned.1.call-done, f32[256]{0:T(256)S(1)} %fusion.23, f32[8,16]{1,0:T(8,128)S(1)} %broadcast_add_fusion, bf16[8,128,16,128]{3,2,1,0:T(8,128)(2,1)} %bitcast.57), kind=kOutput, calls=%fused_computation.7 | convolution fusion | flops 1073840128 | bytes 12649984 | tf_op jit(solution)/shard_map/acbd,pcd->pab/dot_general | solution.py:30
  323.6 12.4 %all_to_all.27 = bf16[256,8,1,16]{0,3,2,1:T(8,128)(2,1)S(1)} all-to-all(bf16[256,8,1,16]{0,3,2,1:T(8,128)(2,1)S(1)} %fusion.18), channel_id=1, replica_groups=mesh['row'=8,'col'=16] {'row'}, dimensions={1} | all-to-all | bytes 131072 | tf_op jit(solution)/shard_map/all_to_all | solution.py:55
  336.0 0.3 copy.27
  336.3 0.6 reshape.71
  336.9 11.0 %all_to_all.28 = bf16[16,2,1024]{2,1,0:T(2,128)(2,1)S(1)} all-to-all(bf16[16,2,1024]{2,1,0:T(2,128)(2,1)S(1)} %reshape.71), channel_id=1, replica_groups=mesh['row'=8,'col'=16] {'col'}, dimensions={0} | all-to-all | bytes 131072 | tf_op jit(solution)/shard_map/all_to_all | solution.py:54
  347.9 0.4 reshape.72
  348.3 0.3 reshape.70
  348.6 0.6 copy.30
  (7 shorter events, 0.2 us)
Async XLA Ops:
  6.5 137.3 %all-gather.4.cloned.1.call-start = ((), (), s32[]{:S(2)}) async-start(), calls=%async_computation.2 | async-start | bytes 11520000 | tf_op jit(solution)/shard_map/all_gather | solution.py:44
  7.3 245.9 %all-gather.6.cloned.1.call-start = ((), (), s32[]{:S(2)}) async-start(), calls=%async_computation.3 | async-start | bytes 21760000 | tf_op jit(solution)/shard_map/all_gather | solution.py:46
  8.0 308.1 %all-gather.8.cloned.1.call-start = ((), (), s32[]{:S(2)}) async-start(), calls=%async_computation.4 | async-start | bytes 8912896 | tf_op jit(solution)/shard_map/all_gather | solution.py:40
Sparse Core Ops, SparseCore 0:
  9.6 134.1 all-gather.3
  145.5 107.6 all-gather.5
  254.8 61.2 all-gather.7
where the time goes:
time: 357 us; the launch traced here: 356 us
  waiting for transfers between devices  199 us (56%)
  blocking collectives  57.1 us (16%)
  local copies, waits for them, and re-layouts  49.4 us (14%)
  matrix products  34.3 us (10%)
  between operations  14.5 us (4%)
    all_gather x1, waiting for transfers between devices, shards(): left_whole = lax.all_gather(panel_left, 'row', axis=1, tiled=True)  95.8 us
    all_gather x1, waiting for transfers between devices, shards(): lax.all_gather(panel_right, 'col', axis=1, tiled=True)  95.5 us
    all_gather x1, blocking collectives, shards(): amp_part = lax.all_gather(amplitudes, 'row', axis=1, tiled=True)  33.7 us
    dot_general x1, matrix products, ladder_block(): lax.dot_general(left_panel.reshape(fit_count, a_count * block_width), rig...  26.8 us
    all_gather x1, local copies, waits for them, and re-layouts, shards(): lax.all_gather(panel_right, 'col', axis=1, tiled=True)  26 us
    all_gather x1, local copies, waits for them, and re-layouts, shards(): left_whole = lax.all_gather(panel_left, 'row', axis=1, tiled=True)  13.9 us
    all_to_all x1, blocking collectives, shards(): lax.all_to_all(update[:, :, None, :], 'row', split_axis=1, concat_axis=2,...  12.4 us
    all_to_all x1, blocking collectives, shards(): lax.all_to_all(lax.all_to_all(update[:, :, None, :], 'row', split_axis=1,...  11 us
  transfers between devices with their start and end apart: 3, of which 3 were waited for; matrix products, arithmetic and copies ran while one was open for 21% of the time, Pallas kernels for 0%

commit v1 on v0

v1 whole, which is shorter than its diff:
```python
import jax
import jax.numpy as jnp
from jax import lax
from jax.experimental import pallas as pl
from jax.experimental.pallas import tpu as pltpu
from jax.sharding import Mesh, PartitionSpec as P

Z = ("zh", "zl")
ALL = ("y", "zh", "x", "zl", "c")
QP = 1280
W = 128
ROWS = 512
STRIDE = 520
CH = 64


def shift(value, axis, step):
    return lax.ppermute(value, axis, [(i, (i + step) % 4) for i in range(4)])


def ladder_kernel(place, left, r_own, r_m, r_p, r_h0, r_h1, t0, t1, t2, t3, u0, u1, u2, u3, out, lbuf, rbuf, tbuf, scr, acc, sems):
    copies_r = [
        pltpu.make_async_copy(r_own, rbuf.at[pl.ds(0, 4)], sems.at[0]),
        pltpu.make_async_copy(r_m, rbuf.at[pl.ds(4, 4)], sems.at[1]),
        pltpu.make_async_copy(r_p, rbuf.at[pl.ds(8, 4)], sems.at[2]),
        pltpu.make_async_copy(r_h0, rbuf.at[pl.ds(12, 2)], sems.at[3]),
        pltpu.make_async_copy(r_h1, rbuf.at[pl.ds(14, 2)], sems.at[4]),
    ]
    copies_l = [pltpu.make_async_copy(left.at[pl.ds(8 * k, 8)], lbuf.at[pl.ds(8 * k, 8)], sems.at[5 + k]) for k in range(4)]
    copies_t = []
    for k, ref in enumerate((t0, t1, t2, t3)):
        copies_t.append(pltpu.make_async_copy(ref, tbuf.at[place[k], place[4]], sems.at[9 + k]))
    for k, ref in enumerate((u0, u1, u2, u3)):
        copies_t.append(pltpu.make_async_copy(ref, tbuf.at[place[k], place[5]], sems.at[13 + k]))
    copies_l[0].start()
    for copy in copies_r:
        copy.start()
    for copy in copies_l[1:]:
        copy.start()
    for copy in copies_t:
        copy.start()
    for copy in copies_r:
        copy.wait()
    acc[...] = jnp.zeros_like(acc)
    for phase in range(2):
        for part in range(4):
            if phase == 0:
                copies_l[part].wait()
            rows = lbuf[pl.ds(part * 8, 8), pl.ds(phase * CH, CH), :].reshape(8 * CH, QP)

            def integrals(group, carry):
                weights = rbuf[pl.ds(group * 4, 4)].reshape(4 * W, QP)
                m = lax.dot_general(rows, weights, (((1,), (1,)), ((), ())), preferred_element_type=jnp.float32)
                for k in range(8):
                    c_core, zh, zl = k // 4, (k // 2) % 2, k % 2
                    slot = zh * 256 + ((part * 2 + zl) * 2 + c_core) * 16
                    for b in range(4):
                        scr[pl.ds(slot + group * 4 + b, CH, stride=STRIDE), :] = m[k * CH : (k + 1) * CH, b * W : (b + 1) * W]
                return carry

            lax.fori_loop(0, 4, integrals, 0)
        if phase == 0:
            for copy in copies_t:
                copy.wait()

        def contract(step, carry):
            x = []
            t = []
            for k in range(8):
                cc = step * 8 + k
                x.append(scr[pl.ds(pl.multiple_of(cc * STRIDE, 8), ROWS), :].astype(jnp.bfloat16))
                c = phase * CH + cc
                y, zh, low = c // 32, (c // 16) % 2, c % 16
                t.append(
                    jnp.concatenate(
                        [tbuf[zh * 2 + zl, core, y * 4 + xx, low] for xx in range(4) for zl in range(2) for core in range(2)],
                        axis=0,
                    )
                )
            acc[...] += lax.dot_general(
                jnp.concatenate(t, axis=1),
                jnp.concatenate(x, axis=1),
                (((1,), (1,)), ((), ())),
                preferred_element_type=jnp.float32,
            )
            return carry

        lax.fori_loop(0, CH // 8, contract, 0)
    for half in range(2):
        out[half] = acc[:, half * 256 : (half + 1) * 256]


def ladder(place, left, rights, ts):
    anywhere = pl.BlockSpec(memory_space=pl.ANY)
    return pl.pallas_call(
        ladder_kernel,
        out_shape=jax.ShapeDtypeStruct((2, 256, 256), jnp.float32),
        in_specs=[pl.BlockSpec(memory_space=pltpu.SMEM)] + [anywhere] * 14,
        out_specs=pl.BlockSpec(memory_space=pltpu.VMEM),
        scratch_shapes=[
            pltpu.VMEM((32, W, QP), jnp.bfloat16),
            pltpu.VMEM((16, W, QP), jnp.bfloat16),
            pltpu.VMEM((4, 2, 16, 16, 16, W), jnp.bfloat16),
            pltpu.VMEM((CH * STRIDE, W), jnp.float32),
            pltpu.VMEM((256, ROWS), jnp.float32),
            pltpu.SemaphoreType.DMA((17,)),
        ],
        compiler_params=pltpu.CompilerParams(vmem_limit_bytes=58 * 2**20),
        cost_estimate=pl.CostEstimate(flops=26 * 10**9, bytes_accessed=25 * 10**6, transcendentals=0),
    )(place, left, *rights, *ts)


def shards(panel_left, panel_right, amplitudes, eps_virtual, eps_occupied, pair_list, blocks):
    y, zh, x, zl, core = (lax.axis_index(name) for name in ALL)
    z = zh * 2 + zl
    panels = jnp.stack([panel_left[:, 0, :], panel_right[:, 0, :]])
    panels = jnp.pad(panels, ((0, 0), (0, 4 * QP - panels.shape[1]), (0, 0)))
    panels = jnp.transpose(panels.reshape(2, 4, QP, W), (1, 0, 3, 2))
    panels = lax.all_to_all(panels, Z, 0, 0, tiled=True)
    left_part, right_part = panels[:, 0], panels[:, 1]
    left = lax.all_gather(left_part, ("x", "c"), axis=0, tiled=True)
    r_m = shift(right_part, "y", 1)
    r_p = shift(right_part, "y", -1)
    r_h0 = shift(r_m[:2], "y", 1)
    r_h1 = shift(r_p[2:], "y", -1)
    own_t = jnp.transpose(amplitudes, (1, 0, 2))
    t0 = lax.all_to_all(jnp.broadcast_to(own_t[None], (16,) + own_t.shape), ("y", "x"), 0, 0, tiled=True)
    ts = [t0, shift(t0, Z, 1), shift(t0, Z, -1), shift(t0, Z, 2)]
    ts = ts + [lax.ppermute(t, "c", [(0, 1), (1, 0)]) for t in ts]
    place = jnp.stack([z, (z + 3) % 4, (z + 1) % 4, (z + 2) % 4, core, 1 - core]).astype(jnp.int32)
    partial = ladder(place, left, (right_part, r_m, r_p, r_h0, r_h1), ts)
    gathered = lax.all_to_all(partial.reshape(32, 16, 256), ("zh", "x", "zl", "c"), 0, 0, tiled=True)
    summed = jnp.sum(gathered.reshape(2, 4, 2, 2, 16, 256), axis=(0, 2))
    summed = summed.reshape(4, 2, 16, 16, 4, 4)
    order = (jnp.array([0, 1, 3, 2], jnp.int32))
    relative = jnp.take(summed, jnp.array([0, 2, 3, 1]), axis=4)
    doubled = jnp.concatenate([relative, relative], axis=4)
    absolute = lax.dynamic_slice_in_dim(doubled, (4 - y) % 4, 4, axis=4)
    absolute = absolute.reshape(4, 2, 16, 16, 4, 2, 2)
    block = jnp.transpose(absolute, (2, 3, 4, 5, 0, 6, 1)).reshape(16, 16, W)
    first = lax.dynamic_slice_in_dim(eps_virtual, blocks[0] * W + (y * 2 + zh) * 16, 16)
    second = lax.dynamic_slice_in_dim(eps_virtual, blocks[1] * W, W)
    pairs = lax.dynamic_slice_in_dim(pair_list, ((x * 2 + zl) * 2 + core) * 16, 16, axis=0)
    levels = jnp.arange(eps_occupied.shape[0], dtype=jnp.int32)
    picked = jnp.where(pairs[:, :, None] == levels[None, None, :], eps_occupied[None, None, :], 0.0)
    pair_sum = jnp.sum(picked, axis=(1, 2))
    denominator = first[None, :, None] + second[None, None, :] - pair_sum[:, None, None]
    return (block / denominator).astype(jnp.bfloat16)


def solution(mesh):
    fine = Mesh(mesh.devices.reshape(4, 2, 4, 2, 2), ALL)
    return jax.shard_map(
        shards,
        mesh=fine,
        in_specs=(
            P(None, ALL, None),
            P(None, ALL, None),
            P(("x", "zl", "c"), ("y", "zh"), None),
            P(),
            P(),
            P(),
            P(),
        ),
        out_specs=P(("x", "zl", "c"), ("y", "zh"), None),
        check_vma=False,
    )
```

time: 357 us -> 215 us (0.60)
  waiting for transfers between devices: 199 us -> 40.1 us
  Pallas kernels: 0 us -> 42.3 us
  starting transfers between devices: 0.08 us -> 40.1 us
  local copies, waits for them, and re-layouts: 49.4 us -> 10.4 us
  matrix products: 34.3 us -> 0 us
  blocking collectives: 57.1 us -> 62.4 us
    all_gather x3 -> x1, waiting for transfers between devices: 198 us -> 0.01 us  [shards(): left = lax.all_gather(left_part, ('x', 'c'), axis=0, tiled=True)]
    pallas_call x0 -> x1, Pallas kernels: none -> 42.3 us  [ladder(): pl.pallas_call(ladder_kernel, out_shape=jax.ShapeDtypeStruct((2, 256, 256...]
    all_gather x2 -> x0, local copies, waits for them, and re-layouts: 39.9 us -> none  [the longest x1 26 us: shards(): lax.all_gather(panel_right, 'col', axis=1, tiled=True)]
    all_to_all x2, blocking collectives: 23.4 us -> 62.4 us  [the longest x1 36.7 us: shards(): panels = lax.all_to_all(panels, Z, 0, 0, tiled=True)]
    ppermute x0 -> x11, starting transfers between devices: none -> 35.3 us  [the longest x4 29.9 us: shards(): ts = ts + [lax.ppermute(t, 'c', [(0, 1), (1, 0)]) for t in ts]]
    dot_general x2 -> x0, matrix products: 34.3 us -> none  [the longest x1 26.8 us: ladder_block(): lax.dot_general(left_panel.reshape(fit_count, a_count * block_width), rig...]
    all_gather x1 -> x0, blocking collectives: 33.7 us -> none  [shards(): amp_part = lax.all_gather(amplitudes, 'row', axis=1, tiled=True)]
    ppermute x0 -> x11, waiting for transfers between devices: none -> 28.6 us  [the longest x7 25.7 us: shift(): return lax.ppermute(value, axis, [(i, (i + step) % 4) for i in range(4)])]
  transfers between devices with their start and end apart: 3 -> 13, of which waited for: 3 -> 5; matrix products, arithmetic and copies ran while one was open for 21% -> 2% of each run, Pallas kernels for 0% -> 0%
where the time goes in v1:
time: 215 us
  blocking collectives  62.4 us (29%)
  Pallas kernels  42.3 us (20%)
  starting transfers between devices  40.1 us (19%)
  waiting for transfers between devices  40.1 us (19%)
  between operations  14.8 us (7%)
  local copies, waits for them, and re-layouts  10.4 us (5%)
  other arithmetic  4.64 us (2%)
    pallas_call x1, Pallas kernels, ladder(): pl.pallas_call(ladder_kernel, out_shape=jax.ShapeDtypeStruct((2, 256, 256...  42.3 us
    all_to_all x1, blocking collectives, shards(): panels = lax.all_to_all(panels, Z, 0, 0, tiled=True)  36.7 us
    ppermute x4, starting transfers between devices, shards(): ts = ts + [lax.ppermute(t, 'c', [(0, 1), (1, 0)]) for t in ts]  29.9 us
    all_to_all x1, blocking collectives, shards(): lax.all_to_all(jnp.broadcast_to(own_t[None], (16,) + own_t.shape), ('y',...  25.7 us
    ppermute x7, waiting for transfers between devices, shift(): return lax.ppermute(value, axis, [(i, (i + step) % 4) for i in range(4)])  25.7 us
    all_to_all x1, waiting for transfers between devices, shards(): lax.all_to_all(partial.reshape(32, 16, 256), ('zh', 'x', 'zl', 'c'), 0, 0...  11.5 us
    ppermute x7, starting transfers between devices, shift(): return lax.ppermute(value, axis, [(i, (i + step) % 4) for i in range(4)])  5.43 us
    all_to_all x1, starting transfers between devices, shards(): lax.all_to_all(partial.reshape(32, 16, 256), ('zh', 'x', 'zl', 'c'), 0, 0...  4.76 us
  transfers between devices with their start and end apart: 13, of which 5 were waited for; matrix products, arithmetic and copies ran while one was open for 2% of the time, Pallas kernels for 0%

profile of v1, /device:TPU:1, one launch (start us, length us, event | category | flops | bytes accessed | tf_op | source)
XLA Modules:
  0.0 214.8 jit_solution(16839371665890964727)
XLA Ops:
  6.5 3.4 %fusion.2 = bf16[2,5120,128]{2,1,0:T(8,128)(2,1)} fusion(bf16[1,5000,128]{2,1,0:T(8,128)(2,1)} %bitcast.33, bf16[1,5000,128]{2,1,0:T(8,128)(2,1)} %bitcast.34), kind=kLoop, calls=%fused_computation.4 | loop fusion | flops 9175040 | bytes 5181440 | tf_op jit(solution)/shard_map/stack | solution.py:116
  9.9 3.0 %copy.35 = bf16[4,2,128,1280]{3,2,1,0:T(8,128)(2,1)S(1)} copy(bf16[4,2,128,1280]{2,3,0,1:T(8,128)(2,1)} %bitcast.28) | data formatting | bytes 5242880 | tf_op jit(solution)/shard_map/transpose | solution.py:118
  12.9 36.7 %all_to_all.15 = bf16[4,2,128,1280]{3,2,1,0:T(8,128)(2,1)S(1)} all-to-all(bf16[4,2,128,1280]{3,2,1,0:T(8,128)(2,1)S(1)} %copy.35), channel_id=1, replica_groups=mesh['y'=4,'zh'=2,'x'=4,'zl'=2,'c'=2] {'zh','zl'}, dimensions={0} | all-to-all | bytes 5242880 | tf_op jit(solution)/shard_map/all_to_all | solution.py:119
  49.6 1.3 slice_bitcast_fusion
  51.1 25.7 %all_to_all.16.t0 = bf16[16,16,16,128]{3,2,1,0:T(8,128)(2,1)S(1)} all-to-all(bf16[16,16,16,128]{3,2,1,0:T(8,128)(2,1)S(1)} %broadcast_in_dim.37), channel_id=1, replica_groups=mesh['y'=4,'zh'=2,'x'=4,'zl'=2,'c'=2] {'y','x'}, dimensions={0} | all-to-all | bytes 2097152 | tf_op jit(solution)/shard_map/all_to_all | solution.py:127
  76.9 2.7 %collective-permute-start.5 = (bf16[16,16,16,128]{3,2,1,0:T(8,128)(2,1)S(1)}, bf16[16,16,16,128]{3,2,1,0:T(8,128)(2,1)}, u32[]{:S(2)}, u32[]{:S(2)}) collective-permute-start(bf16[16,16,16,128]{3,2,1,0:T(8,128)(2,1)S(1)} %all_to_all.16.t0), channel_id=1, source_target_pairs={{0,18},{2,0},{16,2},{18,16},{1,19},{3,1},{17,3},{19,17},{4,22},{6,... | collective-permute-start | bytes 3145736 | tf_op jit(solution)/shard_map/ppermute | solution.py:18
  79.5 2.7 %collective-permute-start.1 = (bf16[4,128,1280]{2,1,0:T(8,128)(2,1)S(1)}, bf16[4,128,1280]{2,1,0:T(8,128)(2,1)S(1)}, u32[]{:S(2)}, u32[]{:S(2)}) collective-permute-start(bf16[4,128,1280]{2,1,0:T(8,128)(2,1)S(1)} %get-tuple-element.5.r_own), channel_id=1, source_target_pairs={{0,96},{32,0},{64,32},{96,64},{1,97},{33,1},{65,33},{97,65},{2,98}... | collective-permute-start | bytes 3932168 | tf_op jit(solution)/shard_map/ppermute | solution.py:18
  82.2 14.7 %collective-permute-done.4.t1 = bf16[16,16,16,128]{3,2,1,0:T(8,128)(2,1)} collective-permute-done((bf16[16,16,16,128]{3,2,1,0:T(8,128)(2,1)S(1)}, bf16[16,16,16,128]{3,2,1,0:T(8,128)(2,1)}, u32[]{:S(2)}, u32[]{:S(2)}) %collective-permute-start.4) | collective-permute-done | bytes 1048608 | tf_op jit(solution)/shard_map/ppermute | solution.py:18
  96.9 29.3 %collective-permute-start.7 = (bf16[16,16,16,128]{3,2,1,0:T(8,128)(2,1)S(1)}, bf16[16,16,16,128]{3,2,1,0:T(8,128)(2,1)S(1)}, u32[]{:S(2)}, u32[]{:S(2)}) collective-permute-start(bf16[16,16,16,128]{3,2,1,0:T(8,128)(2,1)S(1)} %all_to_all.16.t0), channel_id=1, source_target_pairs={{0,1},{1,0},{2,3},{3,2},{4,5},{5,4},{6,7},{7,6},{8,9},{9,8},{10,11... | collective-permute-start | bytes 3145736 | tf_op jit(solution)/shard_map/ppermute | solution.py:129
  126.2 0.5 collective-permute-start.9
  127.1 2.9 %collective-permute-done.7.u0 = bf16[16,16,16,128]{3,2,1,0:T(8,128)(2,1)S(1)} collective-permute-done((bf16[16,16,16,128]{3,2,1,0:T(8,128)(2,1)S(1)}, bf16[16,16,16,128]{3,2,1,0:T(8,128)(2,1)S(1)}, u32[]{:S(2)}, u32[]{:S(2)}) %collective-permute-start.7) | collective-permute-done | bytes 1048608 | tf_op jit(solution)/shard_map/ppermute | solution.py:129
  129.9 1.0 copy-done.9
  130.9 0.6 fusion.4
  132.8 0.8 dynamic_slice.14
  133.6 0.8 dynamic_slice.13
  134.4 0.6 stack.30.place
  135.0 9.2 %collective-permute-done.2.r_h0 = bf16[2,128,1280]{2,1,0:T(8,128)(2,1)} collective-permute-done((bf16[2,128,1280]{2,1,0:T(8,128)(2,1)S(1)}, bf16[2,128,1280]{2,1,0:T(8,128)(2,1)}, u32[]{:S(2)}, u32[]{:S(2)}) %collective-permute-start.2) | collective-permute-done | bytes 655392 | tf_op jit(solution)/shard_map/ppermute | solution.py:18
  144.2 1.8 collective-permute-done.3.r_h1
  146.0 42.3 %shard_map.82 = f32[2,256,256]{2,1,0:T(8,128)} custom-call(s32[6]{0:T(128)} %stack.30.place, bf16[32,128,1280]{2,1,0:T(8,128)(2,1)} %bitcast.37, bf16[4,128,1280]{2,1,0:T(8,128)(2,1)} %copy-done.1, bf16[4,128,1280]{2,1,0:T(8,128)(2,1)} %copy-done.3, bf16[4,128,1280]{2,1,0:T(8,128)(2,1)} %copy-done.4, bf16[2,128,1280]{2,1,0:T(8,128)(2,1)} %collective-permute-done.2.r_h0, ...), custom_call_target="tpu_custom_call" | custom-call | flops 25999998976 | bytes 25000000 | tf_op jit(solution)/shard_map/pallas_call | solution.py:95
  188.3 4.8 %all-to-all-start.2 = ((f32[32,16,256]{2,1,0:T(8,128)}), f32[32,16,256]{2,1,0:T(8,128)S(1)}, u32[]{:S(2)}, u32[]{:S(2)}) async-start(f32[32,16,256]{2,1,0:T(8,128)} %bitcast.35), calls=%async_computation.2 | async-start | bytes 1048576 | tf_op jit(solution)/shard_map/all_to_all | solution.py:132
  193.4 11.5 %all-to-all-done.2 = f32[32,16,256]{2,1,0:T(8,128)S(1)} async-done(((f32[32,16,256]{2,1,0:T(8,128)}), f32[32,16,256]{2,1,0:T(8,128)S(1)}, u32[]{:S(2)}, u32[]{:S(2)}) %all-to-all-start.2) | async-done | bytes 524320 | tf_op jit(solution)/shard_map/all_to_all | solution.py:132
  205.3 0.5 copy.39
  205.8 0.6 gather_fusion
  207.3 0.7 divide_convert_fusion
  (49 shorter events, 2.1 us)
Async XLA Ops:
  6.5 186.5 %copy-start = (s32[256,2]{0,1:T(2,128)S(1)}, s32[256,2]{0,1:T(2,128)}, u32[]{:S(2)}) copy-start(s32[256,2]{0,1:T(2,128)} %param.13) | copy-start | bytes 6148
  6.5 139.5 %all-gather.3.cloned.1.call-start = ((), (), s32[]{:S(2)}) async-start(), calls=%async_computation.3 | async-start | bytes 11796480 | tf_op jit(solution)/shard_map/all_gather | solution.py:121
  49.6 1.3 copy-start.5
  50.9 76.0 %copy-start.1 = (bf16[4,128,1280]{2,1,0:T(8,128)(2,1)}, bf16[4,128,1280]{2,1,0:T(8,128)(2,1)S(1)}, u32[]{:S(2)}) copy-start(bf16[4,128,1280]{2,1,0:T(8,128)(2,1)S(1)} %get-tuple-element.5.r_own) | copy-start | bytes 3932164
  51.1 79.8 %copy-start.6 = (s32[2]{0:T(128)S(1)}, s32[2]{0:T(128)}, u32[]{:S(2)}) copy-start(s32[2]{0:T(128)} %param.14) | copy-start | bytes 28
  76.9 69.1 %copy-start.2 = (bf16[16,16,16,128]{3,2,1,0:T(8,128)(2,1)}, bf16[16,16,16,128]{3,2,1,0:T(8,128)(2,1)S(1)}, u32[]{:S(2)}) copy-start(bf16[16,16,16,128]{3,2,1,0:T(8,128)(2,1)S(1)} %all_to_all.16.t0) | copy-start | bytes 3145732
  76.9 20.1 %collective-permute-start.4 = (bf16[16,16,16,128]{3,2,1,0:T(8,128)(2,1)S(1)}, bf16[16,16,16,128]{3,2,1,0:T(8,128)(2,1)}, u32[]{:S(2)}, u32[]{:S(2)}) collective-permute-start(bf16[16,16,16,128]{3,2,1,0:T(8,128)(2,1)S(1)} %all_to_all.16.t0), channel_id=1, source_target_pairs={{0,2},{2,16},{16,18},{18,0},{1,3},{3,17},{17,19},{19,1},{4,6},{6,2... | collective-permute-start | bytes 3145736 | tf_op jit(solution)/shard_map/ppermute | solution.py:18
  76.9 49.9 %collective-permute-start = (bf16[4,128,1280]{2,1,0:T(8,128)(2,1)S(1)}, bf16[4,128,1280]{2,1,0:T(8,128)(2,1)S(1)}, u32[]{:S(2)}, u32[]{:S(2)}) collective-permute-start(bf16[4,128,1280]{2,1,0:T(8,128)(2,1)S(1)} %get-tuple-element.5.r_own), channel_id=1, source_target_pairs={{0,32},{32,64},{64,96},{96,0},{1,33},{33,65},{65,97},{97,1},{2,34}... | collective-permute-start | bytes 3932168 | tf_op jit(solution)/shard_map/ppermute | solution.py:18
  76.9 49.4 %collective-permute-start.5 = (bf16[16,16,16,128]{3,2,1,0:T(8,128)(2,1)S(1)}, bf16[16,16,16,128]{3,2,1,0:T(8,128)(2,1)}, u32[]{:S(2)}, u32[]{:S(2)}) collective-permute-start(bf16[16,16,16,128]{3,2,1,0:T(8,128)(2,1)S(1)} %all_to_all.16.t0), channel_id=1, source_target_pairs={{0,18},{2,0},{16,2},{18,16},{1,19},{3,1},{17,3},{19,17},{4,22},{6,... | collective-permute-start | bytes 3145736 | tf_op jit(solution)/shard_map/ppermute | solution.py:18
  79.5 46.7 %collective-permute-start.6 = (bf16[16,16,16,128]{3,2,1,0:T(8,128)(2,1)S(1)}, bf16[16,16,16,128]{3,2,1,0:T(8,128)(2,1)}, u32[]{:S(2)}, u32[]{:S(2)}) collective-permute-start(bf16[16,16,16,128]{3,2,1,0:T(8,128)(2,1)S(1)} %all_to_all.16.t0), channel_id=1, source_target_pairs={{0,16},{2,18},{16,0},{18,2},{1,17},{3,19},{17,1},{19,3},{4,20},{6,... | collective-permute-start | bytes 3145736 | tf_op jit(solution)/shard_map/ppermute | solution.py:18
  79.5 47.4 %collective-permute-start.1 = (bf16[4,128,1280]{2,1,0:T(8,128)(2,1)S(1)}, bf16[4,128,1280]{2,1,0:T(8,128)(2,1)S(1)}, u32[]{:S(2)}, u32[]{:S(2)}) collective-permute-start(bf16[4,128,1280]{2,1,0:T(8,128)(2,1)S(1)} %get-tuple-element.5.r_own), channel_id=1, source_target_pairs={{0,96},{32,0},{64,32},{96,64},{1,97},{33,1},{65,33},{97,65},{2,98}... | collective-permute-start | bytes 3932168 | tf_op jit(solution)/shard_map/ppermute | solution.py:18
  96.9 33.0 %collective-permute-start.7 = (bf16[16,16,16,128]{3,2,1,0:T(8,128)(2,1)S(1)}, bf16[16,16,16,128]{3,2,1,0:T(8,128)(2,1)S(1)}, u32[]{:S(2)}, u32[]{:S(2)}) collective-permute-start(bf16[16,16,16,128]{3,2,1,0:T(8,128)(2,1)S(1)} %all_to_all.16.t0), channel_id=1, source_target_pairs={{0,1},{1,0},{2,3},{3,2},{4,5},{5,4},{6,7},{7,6},{8,9},{9,8},{10,11... | collective-permute-start | bytes 3145736 | tf_op jit(solution)/shard_map/ppermute | solution.py:129
  126.2 8.7 %collective-permute-start.8 = (bf16[16,16,16,128]{3,2,1,0:T(8,128)(2,1)}, bf16[16,16,16,128]{3,2,1,0:T(8,128)(2,1)}, u32[]{:S(2)}, u32[]{:S(2)}) collective-permute-start(bf16[16,16,16,128]{3,2,1,0:T(8,128)(2,1)} %collective-permute-done.4.t1), channel_id=1, source_target_pairs={{0,1},{1,0},{2,3},{3,2},{4,5},{5,4},{6,7},{7,6},{8,9},{9,8},{10,11... | collective-permute-start | bytes 3145736 | tf_op jit(solution)/shard_map/ppermute | solution.py:129
  126.2 8.7 %collective-permute-start.9 = (bf16[16,16,16,128]{3,2,1,0:T(8,128)(2,1)}, bf16[16,16,16,128]{3,2,1,0:T(8,128)(2,1)}, u32[]{:S(2)}, u32[]{:S(2)}) collective-permute-start(bf16[16,16,16,128]{3,2,1,0:T(8,128)(2,1)} %collective-permute-done.5.t2), channel_id=1, source_target_pairs={{0,1},{1,0},{2,3},{3,2},{4,5},{5,4},{6,7},{7,6},{8,9},{9,8},{10,11... | collective-permute-start | bytes 3145736 | tf_op jit(solution)/shard_map/ppermute | solution.py:129
  126.7 3.2 %copy-start.3 = (bf16[4,128,1280]{2,1,0:T(8,128)(2,1)}, bf16[4,128,1280]{2,1,0:T(8,128)(2,1)S(1)}, u32[]{:S(2)}) copy-start(bf16[4,128,1280]{2,1,0:T(8,128)(2,1)S(1)} %collective-permute-done.r_m) | copy-start | bytes 3932164
  126.7 8.2 %collective-permute-start.10 = (bf16[16,16,16,128]{3,2,1,0:T(8,128)(2,1)}, bf16[16,16,16,128]{3,2,1,0:T(8,128)(2,1)}, u32[]{:S(2)}, u32[]{:S(2)}) collective-permute-start(bf16[16,16,16,128]{3,2,1,0:T(8,128)(2,1)} %collective-permute-done.6.t3), channel_id=1, source_target_pairs={{0,1},{1,0},{2,3},{3,2},{4,5},{5,4},{6,7},{7,6},{8,9},{9,8},{10,11... | collective-permute-start | bytes 3145736 | tf_op jit(solution)/shard_map/ppermute | solution.py:129
  126.9 3.0 %copy-start.4 = (bf16[4,128,1280]{2,1,0:T(8,128)(2,1)}, bf16[4,128,1280]{2,1,0:T(8,128)(2,1)S(1)}, u32[]{:S(2)}) copy-start(bf16[4,128,1280]{2,1,0:T(8,128)(2,1)S(1)} %collective-permute-done.1.r_p) | copy-start | bytes 3932164
  126.9 17.3 %collective-permute-start.2 = (bf16[2,128,1280]{2,1,0:T(8,128)(2,1)S(1)}, bf16[2,128,1280]{2,1,0:T(8,128)(2,1)}, u32[]{:S(2)}, u32[]{:S(2)}) collective-permute-start(bf16[2,128,1280]{2,1,0:T(8,128)(2,1)S(1)} %slice.28), channel_id=1, source_target_pairs={{0,32},{32,64},{64,96},{96,0},{1,33},{33,65},{65,97},{97,1},{2,34}... | collective-permute-start | bytes 1966088 | tf_op jit(solution)/shard_map/ppermute | solution.py:18
  129.9 1.0 copy-start.9
  129.9 16.1 %collective-permute-start.3 = (bf16[2,128,1280]{2,1,0:T(8,128)(2,1)S(1)}, bf16[2,128,1280]{2,1,0:T(8,128)(2,1)}, u32[]{:S(2)}, u32[]{:S(2)}) collective-permute-start(bf16[2,128,1280]{2,1,0:T(8,128)(2,1)S(1)} %slice.29), channel_id=1, source_target_pairs={{0,96},{32,0},{64,32},{96,64},{1,97},{33,1},{65,33},{97,65},{2,98}... | collective-permute-start | bytes 1966088 | tf_op jit(solution)/shard_map/ppermute | solution.py:18
  146.0 47.2 %copy-start.7 = (s32[4]{0:T(128)S(1)}, s32[4]{0:T(128)}, u32[]{:S(2)}) copy-start(s32[4]{0:T(128)} %constant.94) | copy-start | bytes 52
  146.0 47.2 %copy-start.8 = (f32[100]{0:T(128)S(1)}, f32[100]{0:T(128)}, u32[]{:S(2)}) copy-start(f32[100]{0:T(128)} %param.12) | copy-start | bytes 1204
  188.3 16.6 %all-to-all-start.2 = ((f32[32,16,256]{2,1,0:T(8,128)}), f32[32,16,256]{2,1,0:T(8,128)S(1)}, u32[]{:S(2)}, u32[]{:S(2)}) async-start(f32[32,16,256]{2,1,0:T(8,128)} %bitcast.35), calls=%async_computation.2 | async-start | bytes 1048576 | tf_op jit(solution)/shard_map/all_to_all | solution.py:132
Sparse Core Ops, SparseCore 0:
  51.0 66.2 all-gather.2

commit v2 on v0

v2 whole, which is shorter than its diff:
```python
import jax
import jax.numpy as jnp
from jax import lax
from jax.experimental import pallas as pl
from jax.experimental.pallas import tpu as pltpu
from jax.sharding import Mesh, PartitionSpec as P

Z = ("zh", "zl")
ALL = ("y", "zh", "x", "zl", "c")
RING = (0, 3, 1, 2)
QP = 1280
W = 128
NEAR = 96
FAR = 32
ANYWHERE = pl.BlockSpec(memory_space=pl.ANY)
SCALARS = pl.BlockSpec(memory_space=pltpu.SMEM)
LIMIT = 58 * 2**20


def gate(values, after):
    count = len(values)

    def nothing(*refs):
        pass

    return pl.pallas_call(
        nothing,
        out_shape=[jax.ShapeDtypeStruct(v.shape, v.dtype) for v in values],
        in_specs=[ANYWHERE] * (count + len(after)),
        out_specs=[ANYWHERE] * count,
        input_output_aliases={k: k for k in range(count)},
        name="gate",
    )(*values, *after)


def block_integrals(place, left, right, core, scr, base, stride, first):
    m = lax.dot_general(
        left.reshape(4 * W, QP), right.reshape(4 * W, QP), (((1,), (1,)), ((), ())), preferred_element_type=jnp.float32
    )
    for za in range(4):
        for zb in range(4):
            row = base + first + place[za] * 8 + place[zb] * 2 + core
            scr[pl.ds(row, W, stride=stride), :] = m[za * W : (za + 1) * W, zb * W : (zb + 1) * W]


def near_kernel(place, l0, l1, l2, r0, r1, r2, r3, r4, r5, xs, lbuf, rbuf, scr, xbuf, sems):
    copies_l = [pltpu.make_async_copy(ref, lbuf.at[u], sems.at[8 + u]) for u, ref in enumerate((l0, l1, l2))]
    rights = (r0, r1, r2, r3, r4, r5)
    copies_r = [pltpu.make_async_copy(ref, rbuf.at[g], sems.at[g]) for g, ref in enumerate(rights)]
    copies_l[0].start()
    for copy in copies_r:
        copy.start()
    for copy in copies_l[1:]:
        copy.start()
    stride = NEAR + 8
    stores = [pltpu.make_async_copy(xbuf.at[u], xs.at[u], sems.at[11 + u]) for u in range(3)]
    for u in range(3):
        copies_l[u].wait()

        def block(g, carry):
            if u == 0:
                pltpu.make_async_copy(r0, rbuf.at[g], sems.at[g]).wait()
            block_integrals(place, lbuf[u], rbuf[g], place[4 + g], scr, u * W * stride, stride, (g // 2) * 32)
            return carry

        lax.fori_loop(0, 6, block, 0)

        def convert(c, carry):
            start = pl.multiple_of((u * W + c) * stride, 8)
            xbuf[u, c] = scr[pl.ds(start, NEAR), :].astype(jnp.bfloat16)
            return carry

        lax.fori_loop(0, W, convert, 0, unroll=8)
        stores[u].start()
    for copy in stores:
        copy.wait()


def near_integrals(place, lefts, rights):
    return pl.pallas_call(
        near_kernel,
        out_shape=jax.ShapeDtypeStruct((3, W, NEAR, W), jnp.bfloat16),
        in_specs=[SCALARS] + [ANYWHERE] * 9,
        out_specs=ANYWHERE,
        scratch_shapes=[
            pltpu.VMEM((3, 4, W, QP), jnp.bfloat16),
            pltpu.VMEM((6, 4, W, QP), jnp.bfloat16),
            pltpu.VMEM((3 * W * (NEAR + 8), W), jnp.float32),
            pltpu.VMEM((3, W, NEAR, W), jnp.bfloat16),
            pltpu.SemaphoreType.DMA((14,)),
        ],
        compiler_params=pltpu.CompilerParams(vmem_limit_bytes=LIMIT),
        cost_estimate=pl.CostEstimate(flops=15 * 10**9, bytes_accessed=10**7, transcendentals=0),
        name="near_integrals",
    )(place, *lefts, *rights)


def far_kernel(place, xs, l0, l1, l2, l3, amps, *refs):
    rights, (out, lbuf, rbuf, tbuf, xbuf, scr, scr3, acc, sems, t_sem) = refs[:8], refs[8:]
    copies_l = [pltpu.make_async_copy(ref, lbuf.at[u], sems.at[8 + u]) for u, ref in enumerate((l0, l1, l2, l3))]
    copies_r = [pltpu.make_async_copy(ref, rbuf.at[g], sems.at[g]) for g, ref in enumerate(rights)]
    copy_x = pltpu.make_async_copy(xs, xbuf.at[:, :, pl.ds(0, NEAR), :], sems.at[12])
    copies_t = [
        pltpu.make_async_copy(amps.at[:, jy, jx], tbuf.at[:, place[16 + jy] * 4 + place[20 + jx]], t_sem)
        for jy in range(4)
        for jx in range(4)
    ]
    for g in (6, 7):
        copies_r[g].start()
    for copy in copies_l:
        copy.start()
    for copy in copies_r[:6]:
        copy.start()
    copy_x.start()
    for copy in copies_t:
        copy.start()
    for copy in copies_l + copies_r[6:]:
        copy.wait()
    stride = FAR + 8

    def opposite(u, carry):
        for g in (6, 7):
            block_integrals(place, lbuf[u], rbuf[g], place[4 + g], scr, u * W * stride, stride, 0)
        return carry

    lax.fori_loop(0, 3, opposite, 0)
    stride3 = NEAR + FAR + 8

    def last(g, carry):
        @pl.when(g < 6)
        def _():
            pltpu.make_async_copy(l0, rbuf.at[g], sems.at[g]).wait()

        block_integrals(place, lbuf[3], rbuf[g], place[4 + g], scr3, 0, stride3, (g // 2) * 32)
        return carry

    lax.fori_loop(0, 8, last, 0)
    copy_x.wait()
    for copy in copies_t:
        copy.wait()
    acc[...] = jnp.zeros_like(acc)

    def contract(step, carry):
        x = []
        t = []
        for k in range(16):
            c = step * 16 + k
            last = scr3[pl.ds(pl.multiple_of(c * stride3, 8), NEAR + FAR), :].astype(jnp.bfloat16)
            pieces = []
            for u in range(3):
                start = pl.multiple_of((u * W + c) * stride, 8)
                far = scr[pl.ds(start, FAR), :].astype(jnp.bfloat16)
                near = xbuf[u, c, :NEAR]
                pieces.append([near[s * 32 : s * 32 + 32] for s in range(3)] + [far])
            pieces.append([last[s * 32 : s * 32 + 32] for s in range(4)])
            rows = [pieces[u][s][zh * 16 : zh * 16 + 16] for zh in range(2) for u in range(4) for s in range(4)]
            x.append(jnp.concatenate(rows, axis=0))
            y, zh, low = c // 32, (c // 16) % 2, c % 16
            t.append(
                jnp.concatenate(
                    [tbuf[(zh * 2 + zl) * 2 + core, y * 4 + xx, low] for xx in range(4) for zl in range(2) for core in range(2)],
                    axis=0,
                )
            )
        acc[...] += lax.dot_general(
            jnp.concatenate(t, axis=1),
            jnp.concatenate(x, axis=1),
            (((1,), (1,)), ((), ())),
            preferred_element_type=jnp.float32,
        )
        return carry

    lax.fori_loop(0, W // 16, contract, 0)
    for zh in range(2):
        out[zh] = acc[:, zh * 256 : (zh + 1) * 256].astype(out.dtype).reshape(16, 16, 256)


def far_ladder(place, xs, lefts, amps, rights):
    return pl.pallas_call(
        far_kernel,
        out_shape=jax.ShapeDtypeStruct((2, 16, 16, 256), jnp.bfloat16),
        in_specs=[SCALARS] + [ANYWHERE] * 14,
        out_specs=pl.BlockSpec(memory_space=pltpu.VMEM),
        scratch_shapes=[
            pltpu.VMEM((4, 4, W, QP), jnp.bfloat16),
            pltpu.VMEM((8, 4, W, QP), jnp.bfloat16),
            pltpu.VMEM((8, 16, 16, 16, W), jnp.bfloat16),
            pltpu.VMEM((3, W, NEAR, W), jnp.bfloat16),
            pltpu.VMEM((3 * W * (FAR + 8), W), jnp.float32),
            pltpu.VMEM((W * (NEAR + FAR + 8), W), jnp.float32),
            pltpu.VMEM((256, 512), jnp.float32),
            pltpu.SemaphoreType.DMA((13,)),
            pltpu.SemaphoreType.DMA,
        ],
        compiler_params=pltpu.CompilerParams(vmem_limit_bytes=LIMIT),
        cost_estimate=pl.CostEstimate(flops=15 * 10**9, bytes_accessed=10**7, transcendentals=0),
        name="far_ladder",
    )(place, xs, *lefts, amps, *rights)


def swap(value):
    return lax.ppermute(value, "c", [(0, 1), (1, 0)])


def shift(value, axis, step):
    return lax.ppermute(value, axis, [(i, (i + step) % 4) for i in range(4)])


def onward(value, axis):
    pairs = [(i * 2 + c, (i + 1 - 2 * c) % 4 * 2 + c) for i in range(4) for c in range(2)]
    return lax.ppermute(value, (axis, "c"), pairs)


def over_ring(value, axis):
    return jnp.stack([value, shift(value, axis, 1), shift(value, axis, -1), shift(value, axis, 2)])


def place_units():
    table = []
    for x in range(4):
        for other in range(4):
            for c in range(2):
                step = (other - x) % 4
                if step in (0, 2):
                    core, unit = c, (0 if step == 0 else 3)
                else:
                    core = 0 if step == 3 else 1
                    unit = 1 if core == c else 2
                table.append(x * 8 + core * 4 + unit)
    return table


def shards(panel_left, panel_right, amplitudes, eps_virtual, eps_occupied, pair_list, blocks):
    y, zh, x, zl, core = (lax.axis_index(name) for name in ALL)
    z = zh * 2 + zl
    panels = jnp.stack([panel_left[:, 0, :], panel_right[:, 0, :]])
    panels = jnp.pad(panels, ((0, 0), (0, 4 * QP - panels.shape[1]), (0, 0)))
    panels = jnp.transpose(panels.reshape(2, 4, QP, W), (1, 0, 3, 2))
    part = lambda k: lax.dynamic_index_in_dim(panels, (z + k) % 4, 0, keepdims=False)
    pieces = [part(0), shift(part(1), Z, 1), shift(part(3), Z, -1), shift(part(2), Z, 2)]
    left = jnp.stack([piece[0] for piece in pieces])
    right = jnp.stack([piece[1] for piece in pieces])
    amps = over_ring(over_ring(jnp.transpose(amplitudes, (1, 0, 2)), "x"), "y")
    left, right, amps = gate([left, right, amps], [])
    amps = lax.all_gather(amps, ("zh", "zl", "c"), axis=0)
    left_s, right_s = swap(left), swap(right)
    left_1, right_1 = onward(left, "x"), onward(right, "y")
    left_1, right_1, left_s, right_s = gate([left_1, right_1, left_s, right_s], [])
    left_1s, right_1s = onward(left_s, "x"), onward(right_s, "y")
    right_1p = swap(right_1)
    left_1, right_1, left_1s, right_1s = gate([left_1, right_1, left_1s, right_1s], [right_1p])
    left_2, right_2 = onward(left_1, "x"), onward(right_1, "y")
    right_1sp = swap(right_1s)
    near = (right, right_s, right_1, right_1s, right_1p, right_1sp)
    cores = [core, 1 - core, core, 1 - core, 1 - core, core, core, 1 - core]
    back = jnp.where(core == 0, 3, 1)
    ys = [y, (y + back) % 4, (y + 4 - back) % 4, (y + 2) % 4]
    slot_of = [sum(jnp.where(ys[s] == k, s, 0) for s in range(4)) for k in range(4)]
    place = [(z + k) % 4 for k in RING] + cores + slot_of + [(base + k) % 4 for base in (y, x) for k in RING]
    place = jnp.stack(place).astype(jnp.int32)
    xs = near_integrals(place, (left, left_1, left_1s), near)
    right_2, xs = gate([right_2, xs], [])
    far = (right_2, swap(right_2))
    partial = far_ladder(place, xs, (left, left_1, left_1s, left_2), amps, near + far)
    gathered = lax.all_to_all(partial.reshape(32, 16, 256), ("zh", "x", "zl", "c"), 0, 0, tiled=True)
    summed = jnp.sum(gathered.reshape(2, 4, 2, 2, 16, 4, 4, 2, 8).astype(jnp.float32), axis=(0, 2))
    upward = [summed[:, 0][:, :, :, s] for s in (0, 2, 3, 1)]
    downward = [summed[:, 1][:, :, :, s] for s in (0, 1, 3, 2)]
    steps = jnp.stack([jnp.stack([u, d], axis=1) for u, d in zip(upward, downward)])
    steps = lax.dynamic_slice_in_dim(jnp.concatenate([steps, steps]), (4 - y) % 4, 4)
    units = jnp.transpose(steps, (1, 2, 4, 0, 3, 5, 6)).reshape(32, 4, 16, 2, 8)
    block = jnp.take(units, jnp.array(place_units(), jnp.int32), axis=0)
    block = block.reshape(4, 4, 2, 4, 16, 2, 2, 2, 2)
    block = jnp.transpose(block, (4, 1, 5, 2, 3, 6, 0, 7, 8)).reshape(16, 16, W)
    first = lax.dynamic_slice_in_dim(eps_virtual, blocks[0] * W + (y * 2 + zh) * 16, 16)
    second = lax.dynamic_slice_in_dim(eps_virtual, blocks[1] * W, W)
    pairs = lax.dynamic_slice_in_dim(pair_list, ((x * 2 + zl) * 2 + core) * 16, 16, axis=0)
    levels = jnp.arange(eps_occupied.shape[0], dtype=jnp.int32)
    picked = jnp.where(pairs[:, :, None] == levels[None, None, :], eps_occupied[None, None, :], 0.0)
    pair_sum = jnp.sum(picked, axis=(1, 2))
    denominator = first[None, :, None] + second[None, None, :] - pair_sum[:, None, None]
    return (block / denominator).astype(jnp.bfloat16)


def solution(mesh):
    fine = Mesh(mesh.devices.reshape(4, 2, 4, 2, 2), ALL)
    return jax.shard_map(
        shards,
        mesh=fine,
        in_specs=(
            P(None, ALL, None),
            P(None, ALL, None),
            P(("x", "zl", "c"), ("y", "zh"), None),
            P(),
            P(),
            P(),
            P(),
        ),
        out_specs=P(("x", "zl", "c"), ("y", "zh"), None),
        check_vma=False,
    )
```

time: 357 us -> 183 us (0.51)
  waiting for transfers between devices: 199 us -> 54.1 us
  blocking collectives: 57.1 us -> 0 us
  Pallas kernels: 0 us -> 49.5 us
  starting transfers between devices: 0.08 us -> 35.8 us
  matrix products: 34.3 us -> 0 us
  local copies, waits for them, and re-layouts: 49.4 us -> 19.3 us
  other arithmetic: 1.08 us -> 9.22 us
    all_gather x3 -> x1, waiting for transfers between devices: 198 us -> 0.01 us  [shards(): amps = lax.all_gather(amps, ('zh', 'zl', 'c'), axis=0)]
    pallas_call x0 -> x6, Pallas kernels: none -> 49.5 us  [the longest x1 25.9 us: far_ladder(): pl.pallas_call(far_kernel, out_shape=jax.ShapeDtypeStruct((2, 16, 16, 256...]
    ppermute x0 -> x20, waiting for transfers between devices: none -> 48.2 us  [the longest x6 29.2 us: onward(): return lax.ppermute(value, (axis, 'c'), pairs)]
    all_gather x2 -> x0, local copies, waits for them, and re-layouts: 39.9 us -> none  [the longest x1 26 us: shards(): lax.all_gather(panel_right, 'col', axis=1, tiled=True)]
    dot_general x2 -> x0, matrix products: 34.3 us -> none  [the longest x1 26.8 us: ladder_block(): lax.dot_general(left_panel.reshape(fit_count, a_count * block_width), rig...]
    all_gather x1 -> x0, blocking collectives: 33.7 us -> none  [shards(): amp_part = lax.all_gather(amplitudes, 'row', axis=1, tiled=True)]
    ppermute x0 -> x20, starting transfers between devices: none -> 29.8 us  [the longest x9 14.5 us: shift(): return lax.ppermute(value, axis, [(i, (i + step) % 4) for i in range(4)])]
    all_to_all x2 -> x0, blocking collectives: 23.4 us -> none  [the longest x1 12.4 us: shards(): lax.all_to_all(update[:, :, None, :], 'row', split_axis=1, concat_axis=2,...]
  transfers between devices with their start and end apart: 3 -> 22, of which waited for: 3 -> 9; matrix products, arithmetic and copies ran while one was open for 21% -> 8% of each run, Pallas kernels for 0% -> 13%
where the time goes in v2:
time: 183 us
  waiting for transfers between devices  54.1 us (30%)
  Pallas kernels  49.5 us (27%)
  starting transfers between devices  35.8 us (20%)
  local copies, waits for them, and re-layouts  19.3 us (11%)
  between operations  15.1 us (8%)
  other arithmetic  9.22 us (5%)
    ppermute x6, waiting for transfers between devices, onward(): return lax.ppermute(value, (axis, 'c'), pairs)  29.2 us
    pallas_call x1, Pallas kernels, far_ladder(): pl.pallas_call(far_kernel, out_shape=jax.ShapeDtypeStruct((2, 16, 16, 256...  25.9 us
    pallas_call x1, Pallas kernels, near_integrals(): pl.pallas_call(near_kernel, out_shape=jax.ShapeDtypeStruct((3, W, NEAR, W...  23.5 us
    ppermute x9, waiting for transfers between devices, shift(): return lax.ppermute(value, axis, [(i, (i + step) % 4) for i in range(4)])  16.6 us
    ppermute x9, starting transfers between devices, shift(): return lax.ppermute(value, axis, [(i, (i + step) % 4) for i in range(4)])  14.5 us
    ppermute x6, starting transfers between devices, onward(): return lax.ppermute(value, (axis, 'c'), pairs)  12.6 us
    unnamed x30, local copies, waits for them, and re-layouts  11.9 us
    all_to_all x1, starting transfers between devices, shards(): lax.all_to_all(partial.reshape(32, 16, 256), ('zh', 'x', 'zl', 'c'), 0, 0...  5.99 us
  transfers between devices with their start and end apart: 22, of which 9 were waited for; matrix products, arithmetic and copies ran while one was open for 8% of the time, Pallas kernels for 13%

profile of v2, /device:TPU:1, one launch (start us, length us, event | category | flops | bytes accessed | tf_op | source)
XLA Modules:
  0.0 183.0 jit_solution(8914067469443948760)
XLA Ops:
  8.0 3.6 %collective-permute-start.5 = (bf16[16,16,128]{2,1,0:T(8,128)(2,1)}, bf16[16,16,128]{2,1,0:T(8,128)(2,1)}, u32[]{:S(2)}, u32[]{:S(2)}) collective-permute-start(bf16[16,16,128]{2,1,0:T(8,128)(2,1)} %bitcast.109.clone.2), channel_id=1, source_target_pairs={{0,8},{4,12},{8,0},{12,4},{1,9},{5,13},{9,1},{13,5},{2,10},{6,14},... | collective-permute-start | bytes 196616 | tf_op jit(solution)/shard_map/ppermute | solution.py:206
  13.1 1.9 %fusion.2 = bf16[2,5120,128]{2,1,0:T(8,128)(2,1)S(1)} fusion(bf16[1,5000,128]{2,1,0:T(8,128)(2,1)} %bitcast.120, bf16[1,5000,128]{2,1,0:T(8,128)(2,1)} %bitcast.121), kind=kLoop, calls=%fused_computation.5 | loop fusion | flops 9175040 | bytes 5181440 | tf_op jit(solution)/shard_map/stack | solution.py:236
  16.3 2.2 %copy.87 = bf16[2,1,1280,128]{2,3,0,1:T(8,128)(2,1)} copy(bf16[2,1,1280,128]{3,2,1,0:T(8,128)(2,1)} %get-tuple-element.34) | data formatting | bytes 1310720
  18.6 3.6 %collective-permute-start.2 = (bf16[2,128,1280]{2,1,0:T(8,128)(2,1)}, bf16[2,128,1280]{2,1,0:T(8,128)(2,1)S(1)}, u32[]{:S(2)}, u32[]{:S(2)}) collective-permute-start(bf16[2,128,1280]{2,1,0:T(8,128)(2,1)} %bitcast.28), channel_id=1, source_target_pairs={{0,16},{2,18},{16,0},{18,2},{1,17},{3,19},{17,1},{19,3},{4,20},{6,... | collective-permute-start | bytes 1966088 | tf_op jit(solution)/shard_map/ppermute | solution.py:206
  22.2 2.2 %copy.86 = bf16[2,1,1280,128]{2,3,0,1:T(8,128)(2,1)} copy(bf16[2,1,1280,128]{3,2,1,0:T(8,128)(2,1)} %get-tuple-element.32) | data formatting | bytes 1310720
  26.8 2.9 %collective-permute-start.8 = (bf16[4,16,16,128]{3,2,1,0:T(8,128)(2,1)}, bf16[4,16,16,128]{3,2,1,0:T(8,128)(2,1)}, u32[]{:S(2)}, u32[]{:S(2)}) collective-permute-start(bf16[4,16,16,128]{3,2,1,0:T(8,128)(2,1)} %get-tuple-element.54), channel_id=1, source_target_pairs={{0,64},{32,96},{64,0},{96,32},{1,65},{33,97},{65,1},{97,33},{2,66}... | collective-permute-start | bytes 786440 | tf_op jit(solution)/shard_map/ppermute | solution.py:206
  31.5 2.8 %collective-permute-done.8 = bf16[4,16,16,128]{3,2,1,0:T(8,128)(2,1)} collective-permute-done((bf16[4,16,16,128]{3,2,1,0:T(8,128)(2,1)}, bf16[4,16,16,128]{3,2,1,0:T(8,128)(2,1)}, u32[]{:S(2)}, u32[]{:S(2)}) %collective-permute-start.8) | collective-permute-done | bytes 262176 | tf_op jit(solution)/shard_map/ppermute | solution.py:206
  35.4 6.3 %collective-permute-done.7 = bf16[4,16,16,128]{3,2,1,0:T(8,128)(2,1)} collective-permute-done((bf16[4,16,16,128]{3,2,1,0:T(8,128)(2,1)}, bf16[4,16,16,128]{3,2,1,0:T(8,128)(2,1)}, u32[]{:S(2)}, u32[]{:S(2)}) %collective-permute-start.7) | collective-permute-done | bytes 262176 | tf_op jit(solution)/shard_map/ppermute | solution.py:206
  41.7 2.2 %pad_maximum_fusion.2.refs_2_ = bf16[4,4,16,16,128]{4,3,2,1,0:T(8,128)(2,1)} fusion(bf16[1,4,16,16,128]{4,3,2,1,0:T(8,128)(2,1)} %bitcast.38, bf16[1,4,16,16,128]{4,3,2,1,0:T(8,128)(2,1)} %bitcast.37, bf16[1,4,16,16,128]{4,3,2,1,0:T(8,128)(2,1)} %bitcast.36, bf16[1,4,16,16,128]{4,3,2,1,0:T(8,128)(2,1)S(1)} %get-tuple-element.53), kind=kLoop, calls=%fused_computation.8 | loop fusion | flops 1572864 | bytes 2097152 | tf_op jit(solution)/shard_map/stack | solution.py:215
  43.9 7.5 %collective-permute-done.1 = bf16[2,128,1280]{2,1,0:T(8,128)(2,1)S(1)} collective-permute-done((bf16[2,128,1280]{2,1,0:T(8,128)(2,1)}, bf16[2,128,1280]{2,1,0:T(8,128)(2,1)S(1)}, u32[]{:S(2)}, u32[]{:S(2)}) %collective-permute-start.1) | collective-permute-done | bytes 655392 | tf_op jit(solution)/shard_map/ppermute | solution.py:206
  51.5 1.8 pad_maximum_fusion
  53.4 2.1 %collective-permute-start.9 = (bf16[4,128,1280]{2,1,0:T(8,128)(2,1)}, bf16[4,128,1280]{2,1,0:T(8,128)(2,1)S(1)}, u32[]{:S(2)}, u32[]{:S(2)}) collective-permute-start(bf16[4,128,1280]{2,1,0:T(8,128)(2,1)} %get-tuple-element.18.l0), channel_id=1, source_target_pairs={{0,4},{1,13},{4,8},{5,1},{8,12},{9,5},{12,0},{13,9},{2,6},{3,15},{... | collective-permute-start | bytes 3932168 | tf_op jit(solution)/shard_map/ppermute | solution.py:211
  55.5 2.7 %collective-permute-start.10 = (bf16[4,128,1280]{2,1,0:T(8,128)(2,1)}, bf16[4,128,1280]{2,1,0:T(8,128)(2,1)S(1)}, u32[]{:S(2)}, u32[]{:S(2)}) collective-permute-start(bf16[4,128,1280]{2,1,0:T(8,128)(2,1)} %get-tuple-element.19.r0.refs_0_), channel_id=1, source_target_pairs={{0,32},{1,97},{32,64},{33,1},{64,96},{65,33},{96,0},{97,65},{2,34}... | collective-permute-start | bytes 3932168 | tf_op jit(solution)/shard_map/ppermute | solution.py:211
  58.8 11.8 %collective-permute-done.9.refs_0_ = bf16[4,128,1280]{2,1,0:T(8,128)(2,1)S(1)} collective-permute-done((bf16[4,128,1280]{2,1,0:T(8,128)(2,1)}, bf16[4,128,1280]{2,1,0:T(8,128)(2,1)S(1)}, u32[]{:S(2)}, u32[]{:S(2)}) %collective-permute-start.9) | collective-permute-done | bytes 1310752 | tf_op jit(solution)/shard_map/ppermute | solution.py:211
  70.5 2.6 %collective-permute-done.10.refs_1_ = bf16[4,128,1280]{2,1,0:T(8,128)(2,1)S(1)} collective-permute-done((bf16[4,128,1280]{2,1,0:T(8,128)(2,1)}, bf16[4,128,1280]{2,1,0:T(8,128)(2,1)S(1)}, u32[]{:S(2)}, u32[]{:S(2)}) %collective-permute-start.10) | collective-permute-done | bytes 1310752 | tf_op jit(solution)/shard_map/ppermute | solution.py:211
  75.3 2.8 %collective-permute-start.14 = (bf16[4,128,1280]{2,1,0:T(8,128)(2,1)}, bf16[4,128,1280]{2,1,0:T(8,128)(2,1)}, u32[]{:S(2)}, u32[]{:S(2)}) collective-permute-start(bf16[4,128,1280]{2,1,0:T(8,128)(2,1)} %get-tuple-element.23.r1.refs_1_), channel_id=1, source_target_pairs={{0,32},{1,97},{32,64},{33,1},{64,96},{65,33},{96,0},{97,65},{2,34}... | collective-permute-start | bytes 3932168 | tf_op jit(solution)/shard_map/ppermute | solution.py:211
  78.0 13.2 %collective-permute-done.13.refs_2_ = bf16[4,128,1280]{2,1,0:T(8,128)(2,1)S(1)} collective-permute-done((bf16[4,128,1280]{2,1,0:T(8,128)(2,1)}, bf16[4,128,1280]{2,1,0:T(8,128)(2,1)S(1)}, u32[]{:S(2)}, u32[]{:S(2)}) %collective-permute-start.13) | collective-permute-done | bytes 1310752 | tf_op jit(solution)/shard_map/ppermute | solution.py:211
  94.0 2.2 %collective-permute-start.17 = (bf16[4,128,1280]{2,1,0:T(8,128)(2,1)}, bf16[4,128,1280]{2,1,0:T(8,128)(2,1)S(1)}, u32[]{:S(2)}, u32[]{:S(2)}) collective-permute-start(bf16[4,128,1280]{2,1,0:T(8,128)(2,1)} %get-tuple-element.27.r3.refs_3_), channel_id=1, source_target_pairs={{0,1},{1,0},{2,3},{3,2},{4,5},{5,4},{6,7},{7,6},{8,9},{9,8},{10,11... | collective-permute-start | bytes 3932168 | tf_op jit(solution)/shard_map/ppermute | solution.py:202
  96.8 2.6 %collective-permute-start.16 = (bf16[4,128,1280]{2,1,0:T(8,128)(2,1)}, bf16[4,128,1280]{2,1,0:T(8,128)(2,1)S(1)}, u32[]{:S(2)}, u32[]{:S(2)}) collective-permute-start(bf16[4,128,1280]{2,1,0:T(8,128)(2,1)} %get-tuple-element.24.r2.refs_2_), channel_id=1, source_target_pairs={{0,32},{1,97},{32,64},{33,1},{64,96},{65,33},{96,0},{97,65},{2,34}... | collective-permute-start | bytes 3932168 | tf_op jit(solution)/shard_map/ppermute | solution.py:211
  101.8 23.5 %near_integrals.1.refs_1_ = bf16[3,128,96,128]{3,2,1,0:T(8,128)(2,1)} custom-call(s32[24]{0:T(128)} %stack.145.place, bf16[4,128,1280]{2,1,0:T(8,128)(2,1)} %get-tuple-element.18.l0, bf16[4,128,1280]{2,1,0:T(8,128)(2,1)} %get-tuple-element.25.l1, bf16[4,128,1280]{2,1,0:T(8,128)(2,1)} %get-tuple-element.26.l2, ...), custom_call_target="tpu_custom_call" | custom-call | flops 15000000512 | bytes 10000000 | tf_op jit(solution)/shard_map/near_integrals/pallas_call | solution.py:80
  127.4 2.3 %collective-permute-done.19.refs_7_ = bf16[4,128,1280]{2,1,0:T(8,128)(2,1)S(1)} collective-permute-done((bf16[4,128,1280]{2,1,0:T(8,128)(2,1)}, bf16[4,128,1280]{2,1,0:T(8,128)(2,1)S(1)}, u32[]{:S(2)}, u32[]{:S(2)}) %collective-permute-start.19) | collective-permute-done | bytes 1310752 | tf_op jit(solution)/shard_map/ppermute | solution.py:202
  130.8 25.9 %far_ladder.1 = bf16[2,16,16,256]{3,2,1,0:T(8,128)(2,1)} custom-call(s32[24]{0:T(128)} %stack.145.place, bf16[3,128,96,128]{3,2,1,0:T(8,128)(2,1)} %get-tuple-element.28.xs, bf16[4,128,1280]{2,1,0:T(8,128)(2,1)} %get-tuple-element.18.l0, bf16[4,128,1280]{2,1,0:T(8,128)(2,1)} %get-tuple-element.25.l1, bf16[4,128,1280]{2,1,0:T(8,128)(2,1)} %get-tuple-element.26.l2, ...), custom_call_target="tpu_custom_call" | custom-call | flops 15000000512 | bytes 10000000 | tf_op jit(solution)/shard_map/far_ladder/pallas_call | solution.py:179
  156.7 6.0 %all-to-all-start = ((bf16[32,16,256]{2,1,0:T(8,128)(2,1)}), bf16[32,16,256]{2,1,0:T(8,128)(2,1)S(1)}, u32[]{:S(2)}, u32[]{:S(2)}) async-start(bf16[32,16,256]{2,1,0:T(8,128)(2,1)} %bitcast.123), calls=%async_computation | async-start | bytes 524288 | tf_op jit(solution)/shard_map/all_to_all | solution.py:265
  165.7 5.9 %all-to-all-done = bf16[32,16,256]{2,1,0:T(8,128)(2,1)S(1)} async-done(((bf16[32,16,256]{2,1,0:T(8,128)(2,1)}), bf16[32,16,256]{2,1,0:T(8,128)(2,1)S(1)}, u32[]{:S(2)}, u32[]{:S(2)}) %all-to-all-start) | async-done | bytes 262176 | tf_op jit(solution)/shard_map/all_to_all | solution.py:265
  (93 shorter events, 27.2 us)
Async XLA Ops:
  6.5 120.0 %copy-start = (s32[256,2]{0,1:T(2,128)S(1)}, s32[256,2]{0,1:T(2,128)}, u32[]{:S(2)}) copy-start(s32[256,2]{0,1:T(2,128)} %param.13) | copy-start | bytes 6148
  6.5 123.2 %all-gather.3.cloned.1.call-start = ((), (), s32[]{:S(2)}) async-start(), calls=%async_computation.1 | async-start | bytes 9437184 | tf_op jit(solution)/shard_map/all_gather | solution.py:245
  8.0 17.0 %collective-permute-start.5 = (bf16[16,16,128]{2,1,0:T(8,128)(2,1)}, bf16[16,16,128]{2,1,0:T(8,128)(2,1)}, u32[]{:S(2)}, u32[]{:S(2)}) collective-permute-start(bf16[16,16,128]{2,1,0:T(8,128)(2,1)} %bitcast.109.clone.2), channel_id=1, source_target_pairs={{0,8},{4,12},{8,0},{12,4},{1,9},{5,13},{9,1},{13,5},{2,10},{6,14},... | collective-permute-start | bytes 196616 | tf_op jit(solution)/shard_map/ppermute | solution.py:206
  11.6 13.5 %collective-permute-start.4 = (bf16[16,16,128]{2,1,0:T(8,128)(2,1)}, bf16[16,16,128]{2,1,0:T(8,128)(2,1)}, u32[]{:S(2)}, u32[]{:S(2)}) collective-permute-start(bf16[16,16,128]{2,1,0:T(8,128)(2,1)} %bitcast.109.clone.2), channel_id=1, source_target_pairs={{0,12},{4,0},{8,4},{12,8},{1,13},{5,1},{9,5},{13,9},{2,14},{6,2},{... | collective-permute-start | bytes 196616 | tf_op jit(solution)/shard_map/ppermute | solution.py:206
  12.5 12.6 %collective-permute-start.3 = (bf16[16,16,128]{2,1,0:T(8,128)(2,1)}, bf16[16,16,128]{2,1,0:T(8,128)(2,1)}, u32[]{:S(2)}, u32[]{:S(2)}) collective-permute-start(bf16[16,16,128]{2,1,0:T(8,128)(2,1)} %bitcast.109.clone.2), channel_id=1, source_target_pairs={{0,4},{4,8},{8,12},{12,0},{1,5},{5,9},{9,13},{13,1},{2,6},{6,10},{... | collective-permute-start | bytes 196616 | tf_op jit(solution)/shard_map/ppermute | solution.py:206
  18.6 25.3 %collective-permute-start.2 = (bf16[2,128,1280]{2,1,0:T(8,128)(2,1)}, bf16[2,128,1280]{2,1,0:T(8,128)(2,1)S(1)}, u32[]{:S(2)}, u32[]{:S(2)}) collective-permute-start(bf16[2,128,1280]{2,1,0:T(8,128)(2,1)} %bitcast.28), channel_id=1, source_target_pairs={{0,16},{2,18},{16,0},{18,2},{1,17},{3,19},{17,1},{19,3},{4,20},{6,... | collective-permute-start | bytes 1966088 | tf_op jit(solution)/shard_map/ppermute | solution.py:206
  24.4 27.1 %collective-permute-start.1 = (bf16[2,128,1280]{2,1,0:T(8,128)(2,1)}, bf16[2,128,1280]{2,1,0:T(8,128)(2,1)S(1)}, u32[]{:S(2)}, u32[]{:S(2)}) collective-permute-start(bf16[2,128,1280]{2,1,0:T(8,128)(2,1)} %bitcast.26), channel_id=1, source_target_pairs={{0,18},{2,0},{16,2},{18,16},{1,19},{3,1},{17,3},{19,17},{4,22},{6,... | collective-permute-start | bytes 1966088 | tf_op jit(solution)/shard_map/ppermute | solution.py:206
  26.8 7.5 %collective-permute-start.8 = (bf16[4,16,16,128]{3,2,1,0:T(8,128)(2,1)}, bf16[4,16,16,128]{3,2,1,0:T(8,128)(2,1)}, u32[]{:S(2)}, u32[]{:S(2)}) collective-permute-start(bf16[4,16,16,128]{3,2,1,0:T(8,128)(2,1)} %get-tuple-element.54), channel_id=1, source_target_pairs={{0,64},{32,96},{64,0},{96,32},{1,65},{33,97},{65,1},{97,33},{2,66}... | collective-permute-start | bytes 786440 | tf_op jit(solution)/shard_map/ppermute | solution.py:206
  29.7 11.9 %collective-permute-start.7 = (bf16[4,16,16,128]{3,2,1,0:T(8,128)(2,1)}, bf16[4,16,16,128]{3,2,1,0:T(8,128)(2,1)}, u32[]{:S(2)}, u32[]{:S(2)}) collective-permute-start(bf16[4,16,16,128]{3,2,1,0:T(8,128)(2,1)} %get-tuple-element.54), channel_id=1, source_target_pairs={{0,96},{32,0},{64,32},{96,64},{1,97},{33,1},{65,33},{97,65},{2,98}... | collective-permute-start | bytes 786440 | tf_op jit(solution)/shard_map/ppermute | solution.py:206
  30.5 11.2 %collective-permute-start.6 = (bf16[4,16,16,128]{3,2,1,0:T(8,128)(2,1)}, bf16[4,16,16,128]{3,2,1,0:T(8,128)(2,1)}, u32[]{:S(2)}, u32[]{:S(2)}) collective-permute-start(bf16[4,16,16,128]{3,2,1,0:T(8,128)(2,1)} %get-tuple-element.54), channel_id=1, source_target_pairs={{0,32},{32,64},{64,96},{96,0},{1,33},{33,65},{65,97},{97,1},{2,34}... | collective-permute-start | bytes 786440 | tf_op jit(solution)/shard_map/ppermute | solution.py:206
  34.3 17.1 %collective-permute-start = (bf16[2,128,1280]{2,1,0:T(8,128)(2,1)S(1)}, bf16[2,128,1280]{2,1,0:T(8,128)(2,1)S(1)}, u32[]{:S(2)}, u32[]{:S(2)}) collective-permute-start(bf16[2,128,1280]{2,1,0:T(8,128)(2,1)S(1)} %bitcast.122), channel_id=1, source_target_pairs={{0,2},{2,16},{16,18},{18,0},{1,3},{3,17},{17,19},{19,1},{4,6},{6,2... | collective-permute-start | bytes 1966088 | tf_op jit(solution)/shard_map/ppermute | solution.py:206
  53.4 17.1 %collective-permute-start.9 = (bf16[4,128,1280]{2,1,0:T(8,128)(2,1)}, bf16[4,128,1280]{2,1,0:T(8,128)(2,1)S(1)}, u32[]{:S(2)}, u32[]{:S(2)}) collective-permute-start(bf16[4,128,1280]{2,1,0:T(8,128)(2,1)} %get-tuple-element.18.l0), channel_id=1, source_target_pairs={{0,4},{1,13},{4,8},{5,1},{8,12},{9,5},{12,0},{13,9},{2,6},{3,15},{... | collective-permute-start | bytes 3932168 | tf_op jit(solution)/shard_map/ppermute | solution.py:211
  55.5 17.6 %collective-permute-start.10 = (bf16[4,128,1280]{2,1,0:T(8,128)(2,1)}, bf16[4,128,1280]{2,1,0:T(8,128)(2,1)S(1)}, u32[]{:S(2)}, u32[]{:S(2)}) collective-permute-start(bf16[4,128,1280]{2,1,0:T(8,128)(2,1)} %get-tuple-element.19.r0.refs_0_), channel_id=1, source_target_pairs={{0,32},{1,97},{32,64},{33,1},{64,96},{65,33},{96,0},{97,65},{2,34}... | collective-permute-start | bytes 3932168 | tf_op jit(solution)/shard_map/ppermute | solution.py:211
  58.3 14.9 %collective-permute-start.11 = (bf16[4,128,1280]{2,1,0:T(8,128)(2,1)}, bf16[4,128,1280]{2,1,0:T(8,128)(2,1)}, u32[]{:S(2)}, u32[]{:S(2)}) collective-permute-start(bf16[4,128,1280]{2,1,0:T(8,128)(2,1)} %get-tuple-element.18.l0), channel_id=1, source_target_pairs={{0,1},{1,0},{2,3},{3,2},{4,5},{5,4},{6,7},{7,6},{8,9},{9,8},{10,11... | collective-permute-start | bytes 3932168 | tf_op jit(solution)/shard_map/ppermute | solution.py:202
  58.3 14.9 %collective-permute-start.12 = (bf16[4,128,1280]{2,1,0:T(8,128)(2,1)}, bf16[4,128,1280]{2,1,0:T(8,128)(2,1)}, u32[]{:S(2)}, u32[]{:S(2)}) collective-permute-start(bf16[4,128,1280]{2,1,0:T(8,128)(2,1)} %get-tuple-element.19.r0.refs_0_), channel_id=1, source_target_pairs={{0,1},{1,0},{2,3},{3,2},{4,5},{5,4},{6,7},{7,6},{8,9},{9,8},{10,11... | collective-permute-start | bytes 3932168 | tf_op jit(solution)/shard_map/ppermute | solution.py:202
  74.2 17.1 %collective-permute-start.13 = (bf16[4,128,1280]{2,1,0:T(8,128)(2,1)}, bf16[4,128,1280]{2,1,0:T(8,128)(2,1)S(1)}, u32[]{:S(2)}, u32[]{:S(2)}) collective-permute-start(bf16[4,128,1280]{2,1,0:T(8,128)(2,1)} %get-tuple-element.22), channel_id=1, source_target_pairs={{0,4},{1,13},{4,8},{5,1},{8,12},{9,5},{12,0},{13,9},{2,6},{3,15},{... | collective-permute-start | bytes 3932168 | tf_op jit(solution)/shard_map/ppermute | solution.py:211
  75.3 17.6 %collective-permute-start.14 = (bf16[4,128,1280]{2,1,0:T(8,128)(2,1)}, bf16[4,128,1280]{2,1,0:T(8,128)(2,1)}, u32[]{:S(2)}, u32[]{:S(2)}) collective-permute-start(bf16[4,128,1280]{2,1,0:T(8,128)(2,1)} %get-tuple-element.23.r1.refs_1_), channel_id=1, source_target_pairs={{0,32},{1,97},{32,64},{33,1},{64,96},{65,33},{96,0},{97,65},{2,34}... | collective-permute-start | bytes 3932168 | tf_op jit(solution)/shard_map/ppermute | solution.py:211
  78.0 14.9 %collective-permute-start.15 = (bf16[4,128,1280]{2,1,0:T(8,128)(2,1)}, bf16[4,128,1280]{2,1,0:T(8,128)(2,1)S(1)}, u32[]{:S(2)}, u32[]{:S(2)}) collective-permute-start(bf16[4,128,1280]{2,1,0:T(8,128)(2,1)} %get-tuple-element.21.refs_1_), channel_id=1, source_target_pairs={{0,1},{1,0},{2,3},{3,2},{4,5},{5,4},{6,7},{7,6},{8,9},{9,8},{10,11... | collective-permute-start | bytes 3932168 | tf_op jit(solution)/shard_map/ppermute | solution.py:202
  94.0 6.7 %collective-permute-start.17 = (bf16[4,128,1280]{2,1,0:T(8,128)(2,1)}, bf16[4,128,1280]{2,1,0:T(8,128)(2,1)S(1)}, u32[]{:S(2)}, u32[]{:S(2)}) collective-permute-start(bf16[4,128,1280]{2,1,0:T(8,128)(2,1)} %get-tuple-element.27.r3.refs_3_), channel_id=1, source_target_pairs={{0,1},{1,0},{2,3},{3,2},{4,5},{5,4},{6,7},{7,6},{8,9},{9,8},{10,11... | collective-permute-start | bytes 3932168 | tf_op jit(solution)/shard_map/ppermute | solution.py:202
  96.8 28.6 %collective-permute-start.16 = (bf16[4,128,1280]{2,1,0:T(8,128)(2,1)}, bf16[4,128,1280]{2,1,0:T(8,128)(2,1)S(1)}, u32[]{:S(2)}, u32[]{:S(2)}) collective-permute-start(bf16[4,128,1280]{2,1,0:T(8,128)(2,1)} %get-tuple-element.24.r2.refs_2_), channel_id=1, source_target_pairs={{0,32},{1,97},{32,64},{33,1},{64,96},{65,33},{96,0},{97,65},{2,34}... | collective-permute-start | bytes 3932168 | tf_op jit(solution)/shard_map/ppermute | solution.py:211
  99.3 28.1 %collective-permute-start.18 = (bf16[4,128,1280]{2,1,0:T(8,128)(2,1)}, bf16[4,128,1280]{2,1,0:T(8,128)(2,1)}, u32[]{:S(2)}, u32[]{:S(2)}) collective-permute-start(bf16[4,128,1280]{2,1,0:T(8,128)(2,1)} %get-tuple-element.25.l1), channel_id=1, source_target_pairs={{0,4},{1,13},{4,8},{5,1},{8,12},{9,5},{12,0},{13,9},{2,6},{3,15},{... | collective-permute-start | bytes 3932168 | tf_op jit(solution)/shard_map/ppermute | solution.py:211
  126.5 3.2 %collective-permute-start.19 = (bf16[4,128,1280]{2,1,0:T(8,128)(2,1)}, bf16[4,128,1280]{2,1,0:T(8,128)(2,1)S(1)}, u32[]{:S(2)}, u32[]{:S(2)}) collective-permute-start(bf16[4,128,1280]{2,1,0:T(8,128)(2,1)} %get-tuple-element.30.refs_6_), channel_id=1, source_target_pairs={{0,1},{1,0},{2,3},{3,2},{4,5},{5,4},{6,7},{7,6},{8,9},{9,8},{10,11... | collective-permute-start | bytes 3932168 | tf_op jit(solution)/shard_map/ppermute | solution.py:202
  130.8 31.9 %copy-start.8 = (s32[32]{0:T(128)S(1)}, s32[32]{0:T(128)}, u32[]{:S(2)}) copy-start(s32[32]{0:T(128)} %constant.161) | copy-start | bytes 388
  156.7 14.8 %all-to-all-start = ((bf16[32,16,256]{2,1,0:T(8,128)(2,1)}), bf16[32,16,256]{2,1,0:T(8,128)(2,1)S(1)}, u32[]{:S(2)}, u32[]{:S(2)}) async-start(bf16[32,16,256]{2,1,0:T(8,128)(2,1)} %bitcast.123), calls=%async_computation | async-start | bytes 524288 | tf_op jit(solution)/shard_map/all_to_all | solution.py:265
  (10 other events, 21.2 us)
Sparse Core Ops, SparseCore 0:
  53.5 51.4 all-gather.2

commit v3 on v2

v3 whole, which is shorter than its diff:
```python
import jax
import jax.numpy as jnp
import numpy as np
from jax import lax
from jax.experimental import pallas as pl
from jax.experimental.pallas import tpu as pltpu
from jax.sharding import Mesh, PartitionSpec as P

Z = ("zh", "zl")
ALL = ("y", "zh", "x", "zl", "c")
RING = (0, 3, 1, 2)
QP = 1280
W = 128
CC = 16
ROWS1, ROWS2, ROWS3 = 128, 160, 224
FIRST = ((0, 1, 2, 4), (3, 5), (6, 7))
ANYWHERE = pl.BlockSpec(memory_space=pl.ANY)
SCALARS = pl.BlockSpec(memory_space=pltpu.SMEM)
LIMIT = 58 * 2**20


def gate(values, after):
    count = len(values)

    def nothing(*refs):
        pass

    return pl.pallas_call(
        nothing,
        out_shape=[jax.ShapeDtypeStruct(v.shape, v.dtype) for v in values],
        in_specs=[ANYWHERE] * (count + len(after)),
        out_specs=[ANYWHERE] * count,
        input_output_aliases={k: k for k in range(count)},
        name="gate",
    )(*values, *after)


def times(left, right):
    rows = left.shape[0] * W if left.ndim == 3 else left.shape[0] * left.shape[1] * W
    return lax.dot_general(
        left.reshape(rows, QP), right.reshape(4 * W, QP), (((1,), (1,)), ((), ())), preferred_element_type=jnp.float32
    )


def pair_integrals(place, lefts, right, scr, stride, first):
    m = times(lefts, right)
    for u in range(2):
        for za in range(4):
            for zb in range(4):
                row = first + place[12 + za] + u * 8 + place[zb]
                k = u * 4 + za
                scr[pl.ds(row, W, stride=stride), :] = m[k * W : (k + 1) * W, zb * W : (zb + 1) * W]


def single_integrals(place, left, right, core, scr, stride, first):
    m = times(left, right)
    for za in range(4):
        for zb in range(4):
            row = first + place[za] * 8 + place[zb] * 2 + core
            scr[pl.ds(row, W, stride=stride), :] = m[za * W : (za + 1) * W, zb * W : (zb + 1) * W]


def round_out(scr, xbuf, xs, rows, sems):
    quarter = W // 4
    stores = [
        pltpu.make_async_copy(xbuf.at[pl.ds(k * quarter, quarter)], xs.at[pl.ds(k * quarter, quarter)], sems.at[k]) for k in range(4)
    ]
    for k in range(4):

        def convert(c, carry):
            start = pl.multiple_of(c * (rows + 8), 8)
            xbuf[c] = scr[pl.ds(start, rows), :].astype(jnp.bfloat16)
            return carry

        lax.fori_loop(k * quarter, (k + 1) * quarter, convert, 0, unroll=8)
        stores[k].start()
    for store in stores:
        store.wait()


def first_kernel(place, l0, l1, *refs):
    rights, (xs, lbuf, rbuf, scr, xbuf, sems, out_sems) = refs[:4], refs[4:]
    copies = [pltpu.make_async_copy(ref, lbuf.at[u], sems.at[4 + u]) for u, ref in enumerate((l0, l1))]
    copies += [pltpu.make_async_copy(ref, rbuf.at[g], sems.at[g]) for g, ref in enumerate(rights)]
    for copy in copies:
        copy.start()
    for copy in copies[:2]:
        copy.wait()

    def block(g, carry):
        pltpu.make_async_copy(l0, rbuf.at[g], sems.at[g]).wait()
        pair_integrals(place, lbuf[...], rbuf[g], scr, ROWS1 + 8, g * 32)
        return carry

    lax.fori_loop(0, 4, block, 0)
    round_out(scr, xbuf, xs, ROWS1, out_sems)


def second_kernel(place, l0, l1, l2, *refs):
    rights, (xs, lbuf, rbuf, scr, xbuf, sems, out_sems) = refs[:6], refs[6:]
    copies = [pltpu.make_async_copy(ref, lbuf.at[u], sems.at[6 + u]) for u, ref in enumerate((l0, l1, l2))]
    copies += [pltpu.make_async_copy(rights[g], rbuf.at[g], sems.at[g]) for g in (3, 5, 0, 1, 2, 4)]
    for copy in copies:
        copy.start()
    for copy in copies[:5]:
        copy.wait()

    def pairs(k, carry):
        pair_integrals(place, lbuf[:2], rbuf[3 + 2 * k], scr, ROWS2 + 8, k * 32)
        return carry

    lax.fori_loop(0, 2, pairs, 0)
    for copy in copies[5:]:
        copy.wait()

    def singles(g, carry):
        single_integrals(place, lbuf[2], rbuf[g], place[4 + g], scr, ROWS2 + 8, 64 + (g // 2) * 32)
        return carry

    lax.fori_loop(0, 6, singles, 0)
    round_out(scr, xbuf, xs, ROWS2, out_sems)


def integrals(kernel, rows, place, lefts, rights):
    units, count = len(lefts), len(rights)
    return pl.pallas_call(
        kernel,
        out_shape=jax.ShapeDtypeStruct((W, rows, W), jnp.bfloat16),
        in_specs=[SCALARS] + [ANYWHERE] * (units + count),
        out_specs=ANYWHERE,
        scratch_shapes=[
            pltpu.VMEM((units, 4, W, QP), jnp.bfloat16),
            pltpu.VMEM((count, 4, W, QP), jnp.bfloat16),
            pltpu.VMEM((W * (rows + 8), W), jnp.float32),
            pltpu.VMEM((W, rows, W), jnp.bfloat16),
            pltpu.SemaphoreType.DMA((units + count,)),
            pltpu.SemaphoreType.DMA((4,)),
        ],
        compiler_params=pltpu.CompilerParams(vmem_limit_bytes=LIMIT),
        cost_estimate=pl.CostEstimate(flops=10 * 10**9, bytes_accessed=10**7, transcendentals=0),
        name="integrals%d" % units,
    )(place, *lefts, *rights)


def far_kernel(place, x1, x2, l0, l1, l2, l3, amps, *refs):
    rights, (out, lbuf, rbuf, tbuf, xbuf1, xbuf2, scr, acc, sems) = refs[:8], refs[8:]
    copies_l = [pltpu.make_async_copy(ref, lbuf.at[u], sems.at[8 + u]) for u, ref in enumerate((l0, l1, l2, l3))]
    copies_r = [pltpu.make_async_copy(ref, rbuf.at[g], sems.at[g]) for g, ref in enumerate(rights)]
    later = [
        pltpu.make_async_copy(amps, tbuf, sems.at[12]),
        pltpu.make_async_copy(x1, xbuf1, sems.at[13]),
        pltpu.make_async_copy(x2, xbuf2, sems.at[14]),
    ]
    soon = copies_l[:2] + copies_r[6:] + copies_l[2:]
    for copy in soon + copies_r[:6] + later:
        copy.start()
    stride = ROWS3 + 8
    for copy in soon[:4]:
        copy.wait()

    def pairs(k, carry):
        pair_integrals(place, lbuf[:2], rbuf[6 + k], scr, stride, k * 32)
        return carry

    lax.fori_loop(0, 2, pairs, 0)
    for copy in soon[4:]:
        copy.wait()

    def opposite(g, carry):
        single_integrals(place, lbuf[2], rbuf[g], place[4 + g], scr, stride, 64)
        return carry

    lax.fori_loop(6, 8, opposite, 0)

    def last(g, carry):
        @pl.when(g < 6)
        def _():
            pltpu.make_async_copy(l0, rbuf.at[g], sems.at[g]).wait()

        single_integrals(place, lbuf[3], rbuf[g], place[4 + g], scr, stride, 96 + (g // 2) * 32)
        return carry

    lax.fori_loop(0, 8, last, 0)
    for copy in later:
        copy.wait()
    acc[...] = jnp.zeros_like(acc)

    def contract(step, carry):
        x = []
        t = []
        for k in range(CC):
            c = step * CC + k
            groups = []
            for values in (
                xbuf1[c],
                xbuf2[c],
                scr[pl.ds(pl.multiple_of(c * stride, 8), ROWS3), :].astype(jnp.bfloat16),
            ):
                groups += [values[g * 32 : g * 32 + 32] for g in range(values.shape[0] // 32)]
            x.append(jnp.concatenate([group[zh * 16 : zh * 16 + 16] for zh in range(2) for group in groups], axis=0))
            y, zh, low = c // 32, (c // 16) % 2, c % 16
            t.append(
                jnp.concatenate(
                    [tbuf[(zh * 2 + zl) * 2 + core, y, xx, low] for xx in range(4) for zl in range(2) for core in range(2)],
                    axis=0,
                )
            )
        acc[...] += lax.dot_general(
            jnp.concatenate(t, axis=1),
            jnp.concatenate(x, axis=1),
            (((1,), (1,)), ((), ())),
            preferred_element_type=jnp.float32,
        )
        return carry

    lax.fori_loop(0, W // CC, contract, 0)
    for zh in range(2):
        out[zh] = acc[:, zh * 256 : (zh + 1) * 256].astype(out.dtype).reshape(16, 16, 256)


def far_ladder(place, x1, x2, lefts, amps, rights):
    return pl.pallas_call(
        far_kernel,
        out_shape=jax.ShapeDtypeStruct((2, 16, 16, 256), jnp.bfloat16),
        in_specs=[SCALARS] + [ANYWHERE] * 15,
        out_specs=pl.BlockSpec(memory_space=pltpu.VMEM),
        scratch_shapes=[
            pltpu.VMEM((4, 4, W, QP), jnp.bfloat16),
            pltpu.VMEM((8, 4, W, QP), jnp.bfloat16),
            pltpu.VMEM((8, 4, 4, 16, 16, W), jnp.bfloat16),
            pltpu.VMEM((W, ROWS1, W), jnp.bfloat16),
            pltpu.VMEM((W, ROWS2, W), jnp.bfloat16),
            pltpu.VMEM((W * (ROWS3 + 8), W), jnp.float32),
            pltpu.VMEM((256, 512), jnp.float32),
            pltpu.SemaphoreType.DMA((15,)),
        ],
        compiler_params=pltpu.CompilerParams(vmem_limit_bytes=LIMIT),
        cost_estimate=pl.CostEstimate(flops=15 * 10**9, bytes_accessed=10**7, transcendentals=0),
        name="far_ladder",
    )(place, x1, x2, *lefts, amps, *rights)


def swap(value):
    return lax.ppermute(value, "c", [(0, 1), (1, 0)])


def shift(value, axis, step):
    return lax.ppermute(value, axis, [(i, (i + step) % 4) for i in range(4)])


def onward(value, axis):
    pairs = [(i * 2 + c, (i + 1 - 2 * c) % 4 * 2 + c) for i in range(4) for c in range(2)]
    return lax.ppermute(value, (axis, "c"), pairs)


def lane_table():
    table = np.full((4, 4, 2, 512), -1, np.int32)
    group_of = {block: k for k, block in enumerate(FIRST[0])}
    group_of.update({FIRST[1][k]: 4 + k for k in range(2)})
    group_of.update({FIRST[2][k]: 9 + k for k in range(2)})
    for y, x, far, zl, c, yb, zb, cb in np.ndindex(4, 4, 4, 2, 2, 4, 4, 2):
        step = (far - x) % 4
        if step in (0, 2):
            core, unit = c, (0 if step == 0 else 3)
        else:
            core = 0 if step == 3 else 1
            unit = 1 if core == c else 2
        slot = ({0: 0, 3: 1, 1: 2, 2: 3} if core == 0 else {0: 0, 1: 1, 3: 2, 2: 3})[(yb - y) % 4]
        own = (cb == core) != (slot == 2)
        if unit < 2:
            lane = group_of[slot * 2 + (0 if own else 1)] * 16 + unit * 8 + zl * 4 + zb
        else:
            group = (6, 7, 8, 11)[slot] if unit == 2 else 12 + slot
            lane = group * 16 + zl * 8 + zb * 2 + cb
        table[y, x, core, ((far * 2 + zl) * 2 + c) * 32 + (yb * 4 + zb) * 2 + cb] = lane
    return table


def shards(panel_left, panel_right, amplitudes, eps_virtual, eps_occupied, pair_list, blocks):
    y, zh, x, zl, core = (lax.axis_index(name) for name in ALL)
    z = zh * 2 + zl
    panels = jnp.stack([panel_left[:, 0, :], panel_right[:, 0, :]])
    panels = jnp.pad(panels, ((0, 0), (0, 4 * QP - panels.shape[1]), (0, 0)))
    panels = jnp.transpose(panels.reshape(2, 4, QP, W), (1, 0, 3, 2))
    part = lambda k: lax.dynamic_index_in_dim(panels, (z + k) % 4, 0, keepdims=False)
    near_z = [shift(part(1), Z, 1), shift(part(3), Z, -1)]
    amps = lax.all_gather(jnp.transpose(amplitudes, (1, 0, 2)), "x", axis=0)
    opposite = gate([part(2)], near_z)[0]
    pieces = [part(0)] + near_z + [shift(opposite, Z, 2)]
    amps = lax.all_gather(amps, "y", axis=0)
    left = jnp.stack([piece[0] for piece in pieces])
    right = jnp.stack([piece[1] for piece in pieces])
    left_s, right_s = swap(left), swap(right)
    amps = lax.all_gather(gate([amps], [left_s, right_s])[0], ("zh", "zl", "c"), axis=0)
    left_1, right_1 = onward(left, "x"), onward(right, "y")
    left_1s, right_1s = onward(left_s, "x"), onward(right_s, "y")
    right_1p = swap(right_1)
    left_2, right_2 = onward(left_1, "x"), onward(right_1, "y")
    cores = [core, 1 - core, core, 1 - core, 1 - core, core, core, 1 - core]
    zs = [(z + k) % 4 for k in RING]
    place = jnp.stack(zs + cores + [(k // 2) * 16 + (k % 2) * 4 for k in zs]).astype(jnp.int32)
    x1 = integrals(first_kernel, ROWS1, place, (left, left_1), (right, right_s, right_1, right_1p))
    right_1s = gate([right_1s], [x1])[0]
    rights = (right, right_s, right_1, right_1s, right_1p, swap(right_1s))
    x2 = integrals(second_kernel, ROWS2, place, (left, left_1, left_1s), rights)
    right_2, x2 = gate([right_2, x2], [])
    rights = rights + (right_2, swap(right_2))
    partial = far_ladder(place, x1, x2, (left, left_1, left_1s, left_2), amps, rights)
    gathered = lax.all_to_all(partial.reshape(32, 16, 256), ("zh", "x", "zl", "c"), 0, 0, tiled=True)
    lanes = lax.dynamic_index_in_dim(jnp.array(lane_table()), y, 0, keepdims=False)
    pick = (lanes[:, :, None, :] == jnp.arange(256, dtype=jnp.int32)[None, None, :, None]).astype(jnp.bfloat16)
    parts = jnp.einsum("hxlkpj,xkjm->hlxpm", gathered.reshape(2, 4, 2, 2, 16, 256), pick, preferred_element_type=jnp.float32)
    block = jnp.sum(parts, axis=(0, 1)).reshape(4, 16, 16, 8, 4)
    block = jnp.transpose(block, (1, 2, 3, 0, 4)).reshape(16, 16, W)
    first = lax.dynamic_slice_in_dim(eps_virtual, blocks[0] * W + (y * 2 + zh) * 16, 16)
    second = lax.dynamic_slice_in_dim(eps_virtual, blocks[1] * W, W)
    pairs = lax.dynamic_slice_in_dim(pair_list, ((x * 2 + zl) * 2 + core) * 16, 16, axis=0)
    levels = jnp.arange(eps_occupied.shape[0], dtype=jnp.int32)
    picked = jnp.where(pairs[:, :, None] == levels[None, None, :], eps_occupied[None, None, :], 0.0)
    pair_sum = jnp.sum(picked, axis=(1, 2))
    denominator = first[None, :, None] + second[None, None, :] - pair_sum[:, None, None]
    return (block / denominator).astype(jnp.bfloat16)


def solution(mesh):
    fine = Mesh(mesh.devices.reshape(4, 2, 4, 2, 2), ALL)
    return jax.shard_map(
        shards,
        mesh=fine,
        in_specs=(
            P(None, ALL, None),
            P(None, ALL, None),
            P(("x", "zl", "c"), ("y", "zh"), None),
            P(),
            P(),
            P(),
            P(),
        ),
        out_specs=P(("x", "zl", "c"), ("y", "zh"), None),
        check_vma=False,
    )
```

time: 183 us -> 171 us (0.934)
  waiting for transfers between devices: 54.1 us -> 35.6 us
  blocking collectives: 0 us -> 10.8 us
  other arithmetic: 9.22 us -> 5.31 us
  Pallas kernels: 49.5 us -> 52.7 us
  starting transfers between devices: 35.8 us -> 32.7 us
    ppermute x6, waiting for transfers between devices: 29.2 us -> 12.4 us  [onward(): return lax.ppermute(value, (axis, 'c'), pairs)]
    all_gather x0 -> x1, blocking collectives: none -> 10.8 us  [shards(): amps = lax.all_gather(jnp.transpose(amplitudes, (1, 0, 2)), 'x', axis=0)]
    ppermute x9 -> x3, starting transfers between devices: 14.5 us -> 7.48 us  [shift(): return lax.ppermute(value, axis, [(i, (i + step) % 4) for i in range(4)])]
    pallas_call x1 -> x2, Pallas kernels: 23.5 us -> 28.6 us  [integrals(): pl.pallas_call(kernel, out_shape=jax.ShapeDtypeStruct((W, rows, W), jnp.b...]
    ppermute x9 -> x3, waiting for transfers between devices: 16.6 us -> 11.9 us  [shift(): return lax.ppermute(value, axis, [(i, (i + step) % 4) for i in range(4)])]
    ppermute x5, starting transfers between devices: 2.71 us -> 5.86 us  [swap(): return lax.ppermute(value, 'c', [(0, 1), (1, 0)])]
    another operation x2 -> x1, other arithmetic: 3.92 us -> 1.24 us  [shards(): right = jnp.stack([piece[1] for piece in pieces])]
    ppermute x5, waiting for transfers between devices: 2.34 us -> 4.86 us  [swap(): return lax.ppermute(value, 'c', [(0, 1), (1, 0)])]
  transfers between devices with their start and end apart: 22 -> 17, of which waited for: 9 -> 9; matrix products, arithmetic and copies ran while one was open for 8% -> 6% of each run, Pallas kernels for 13% -> 17%
where the time goes in v3:
time: 171 us
  Pallas kernels  52.7 us (31%)
  waiting for transfers between devices  35.6 us (21%)
  starting transfers between devices  32.7 us (19%)
  local copies, waits for them, and re-layouts  18.2 us (11%)
  between operations  14.8 us (9%)
  blocking collectives  10.8 us (6%)
  other arithmetic  5.31 us (3%)
    pallas_call x2, Pallas kernels, integrals(): pl.pallas_call(kernel, out_shape=jax.ShapeDtypeStruct((W, rows, W), jnp.b...  28.6 us
    pallas_call x1, Pallas kernels, far_ladder(): pl.pallas_call(far_kernel, out_shape=jax.ShapeDtypeStruct((2, 16, 16, 256...  24.1 us
    ppermute x6, waiting for transfers between devices, onward(): return lax.ppermute(value, (axis, 'c'), pairs)  12.4 us
    ppermute x6, starting transfers between devices, onward(): return lax.ppermute(value, (axis, 'c'), pairs)  12.2 us
    ppermute x3, waiting for transfers between devices, shift(): return lax.ppermute(value, axis, [(i, (i + step) % 4) for i in range(4)])  11.9 us
    all_gather x1, blocking collectives, shards(): amps = lax.all_gather(jnp.transpose(amplitudes, (1, 0, 2)), 'x', axis=0)  10.8 us
    unnamed x34, local copies, waits for them, and re-layouts  10.6 us
    ppermute x3, starting transfers between devices, shift(): return lax.ppermute(value, axis, [(i, (i + step) % 4) for i in range(4)])  7.48 us
  transfers between devices with their start and end apart: 17, of which 9 were waited for; matrix products, arithmetic and copies ran while one was open for 6% of the time, Pallas kernels for 17%

profile of v3, /device:TPU:1, one launch (start us, length us, event | category | flops | bytes accessed | tf_op | source)
XLA Modules:
  0.0 170.9 jit_solution(7922161951215030542)
XLA Ops:
  6.5 1.9 %fusion.5 = bf16[2,5120,128]{2,1,0:T(8,128)(2,1)S(1)} fusion(bf16[1,5000,128]{2,1,0:T(8,128)(2,1)} %bitcast.62, bf16[1,5000,128]{2,1,0:T(8,128)(2,1)} %bitcast.63), kind=kLoop, calls=%fused_computation.6 | loop fusion | flops 9175040 | bytes 5181440 | tf_op jit(solution)/shard_map/stack | solution.py:282
  9.7 2.5 %collective-permute-start = (bf16[2,128,1280]{2,1,0:T(8,128)(2,1)}, bf16[2,128,1280]{2,1,0:T(8,128)(2,1)S(1)}, u32[]{:S(2)}, u32[]{:S(2)}) collective-permute-start(bf16[2,128,1280]{2,1,0:T(8,128)(2,1)} %bitcast.19), channel_id=1, source_target_pairs={{0,2},{2,16},{16,18},{18,0},{1,3},{3,17},{17,19},{19,1},{4,6},{6,2... | collective-permute-start | bytes 1966088 | tf_op jit(solution)/shard_map/ppermute | solution.py:248
  13.3 2.1 %collective-permute-start.1 = (bf16[2,128,1280]{2,1,0:T(8,128)(2,1)}, bf16[2,128,1280]{2,1,0:T(8,128)(2,1)S(1)}, u32[]{:S(2)}, u32[]{:S(2)}) collective-permute-start(bf16[2,128,1280]{2,1,0:T(8,128)(2,1)} %bitcast.21), channel_id=1, source_target_pairs={{0,18},{2,0},{16,2},{18,16},{1,19},{3,1},{17,3},{19,17},{4,22},{6,... | collective-permute-start | bytes 1966088 | tf_op jit(solution)/shard_map/ppermute | solution.py:248
  15.4 10.8 %all-gather = bf16[64,16,128]{2,0,1:T(8,128)(2,1)S(1)} all-gather(bf16[16,16,128]{2,0,1:T(8,128)(2,1)S(1)} %bitcast.68), channel_id=2, replica_groups=mesh['y'=4,'zh'=2,'x'=4,'zl'=2,'c'=2] {'x'}, dimensions={0}, use_global_device_ids=true | all-gather | bytes 327680 | tf_op jit(solution)/shard_map/all_gather | solution.py:287
  30.1 2.9 %collective-permute-start.2 = (bf16[2,128,1280]{2,1,0:T(8,128)(2,1)}, bf16[2,128,1280]{2,1,0:T(8,128)(2,1)S(1)}, u32[]{:S(2)}, u32[]{:S(2)}) collective-permute-start(bf16[2,128,1280]{2,1,0:T(8,128)(2,1)} %gate.4), channel_id=1, source_target_pairs={{0,16},{2,18},{16,0},{18,2},{1,17},{3,19},{17,1},{19,3},{4,20},{6,... | collective-permute-start | bytes 1966088 | tf_op jit(solution)/shard_map/ppermute | solution.py:248
  34.1 11.4 %collective-permute-done.2 = bf16[2,128,1280]{2,1,0:T(8,128)(2,1)S(1)} collective-permute-done((bf16[2,128,1280]{2,1,0:T(8,128)(2,1)}, bf16[2,128,1280]{2,1,0:T(8,128)(2,1)S(1)}, u32[]{:S(2)}, u32[]{:S(2)}) %collective-permute-start.2) | collective-permute-done | bytes 655392 | tf_op jit(solution)/shard_map/ppermute | solution.py:248
  45.6 1.2 pad_maximum_fusion.1.refs_0_
  46.9 3.3 %collective-permute-start.4 = (bf16[4,128,1280]{2,1,0:T(8,128)(2,1)}, bf16[4,128,1280]{2,1,0:T(8,128)(2,1)S(1)}, u32[]{:S(2)}, u32[]{:S(2)}) collective-permute-start(bf16[4,128,1280]{2,1,0:T(8,128)(2,1)} %pad_maximum_fusion.1.refs_0_), channel_id=1, source_target_pairs={{0,1},{1,0},{2,3},{3,2},{4,5},{5,4},{6,7},{7,6},{8,9},{9,8},{10,11... | collective-permute-start | bytes 3932168 | tf_op jit(solution)/shard_map/ppermute | solution.py:244
  50.2 1.2 pad_maximum_fusion.l0
  53.1 1.9 %collective-permute-done.8.refs_1_ = bf16[4,128,1280]{2,1,0:T(8,128)(2,1)S(1)} collective-permute-done((bf16[4,128,1280]{2,1,0:T(8,128)(2,1)}, bf16[4,128,1280]{2,1,0:T(8,128)(2,1)S(1)}, u32[]{:S(2)}, u32[]{:S(2)}) %collective-permute-start.8) | collective-permute-done | bytes 1310752 | tf_op jit(solution)/shard_map/ppermute | solution.py:244
  56.1 2.8 %collective-permute-start.5 = (bf16[4,128,1280]{2,1,0:T(8,128)(2,1)}, bf16[4,128,1280]{2,1,0:T(8,128)(2,1)S(1)}, u32[]{:S(2)}, u32[]{:S(2)}) collective-permute-start(bf16[4,128,1280]{2,1,0:T(8,128)(2,1)} %pad_maximum_fusion.1.refs_0_), channel_id=1, source_target_pairs={{0,32},{1,97},{32,64},{33,1},{64,96},{65,33},{96,0},{97,65},{2,34}... | collective-permute-start | bytes 3932168 | tf_op jit(solution)/shard_map/ppermute | solution.py:253
  58.9 2.5 %collective-permute-start.3 = (bf16[4,128,1280]{2,1,0:T(8,128)(2,1)}, bf16[4,128,1280]{2,1,0:T(8,128)(2,1)S(1)}, u32[]{:S(2)}, u32[]{:S(2)}) collective-permute-start(bf16[4,128,1280]{2,1,0:T(8,128)(2,1)} %pad_maximum_fusion.l0), channel_id=1, source_target_pairs={{0,4},{1,13},{4,8},{5,1},{8,12},{9,5},{12,0},{13,9},{2,6},{3,15},{... | collective-permute-start | bytes 3932168 | tf_op jit(solution)/shard_map/ppermute | solution.py:253
  61.4 12.4 %collective-permute-done.5.refs_2_ = bf16[4,128,1280]{2,1,0:T(8,128)(2,1)S(1)} collective-permute-done((bf16[4,128,1280]{2,1,0:T(8,128)(2,1)}, bf16[4,128,1280]{2,1,0:T(8,128)(2,1)S(1)}, u32[]{:S(2)}, u32[]{:S(2)}) %collective-permute-start.5) | collective-permute-done | bytes 1310752 | tf_op jit(solution)/shard_map/ppermute | solution.py:253
  73.8 1.8 %collective-permute-start.6 = (bf16[4,128,1280]{2,1,0:T(8,128)(2,1)S(1)}, bf16[4,128,1280]{2,1,0:T(8,128)(2,1)}, u32[]{:S(2)}, u32[]{:S(2)}) collective-permute-start(bf16[4,128,1280]{2,1,0:T(8,128)(2,1)S(1)} %collective-permute-done.5.refs_2_), channel_id=1, source_target_pairs={{0,1},{1,0},{2,3},{3,2},{4,5},{5,4},{6,7},{7,6},{8,9},{9,8},{10,11... | collective-permute-start | bytes 3932168 | tf_op jit(solution)/shard_map/ppermute | solution.py:244
  75.6 1.6 collective-permute-start.10
  77.8 2.5 %collective-permute-start.9 = (bf16[4,128,1280]{2,1,0:T(8,128)(2,1)}, bf16[4,128,1280]{2,1,0:T(8,128)(2,1)}, u32[]{:S(2)}, u32[]{:S(2)}) collective-permute-start(bf16[4,128,1280]{2,1,0:T(8,128)(2,1)} %copy-done.5), channel_id=1, source_target_pairs={{0,4},{1,13},{4,8},{5,1},{8,12},{9,5},{12,0},{13,9},{2,6},{3,15},{... | collective-permute-start | bytes 3932168 | tf_op jit(solution)/shard_map/ppermute | solution.py:253
  80.3 1.1 copy-done.12
  81.5 12.5 %integrals2.1.refs_1_.x1 = bf16[128,128,128]{2,1,0:T(8,128)(2,1)} custom-call(s32[16]{0:T(128)} %stack.58.place, bf16[4,128,1280]{2,1,0:T(8,128)(2,1)} %pad_maximum_fusion.l0, bf16[4,128,1280]{2,1,0:T(8,128)(2,1)} %copy-done.12, bf16[4,128,1280]{2,1,0:T(8,128)(2,1)} %pad_maximum_fusion.1.refs_0_, bf16[4,128,1280]{2,1,0:T(8,128)(2,1)} %copy-done.4, ...), custom_call_target="tpu_custom_call" | custom-call | flops 10000000000 | bytes 10000000 | tf_op jit(solution)/shard_map/integrals2/pallas_call | solution.py:126
  95.8 2.3 %collective-permute-start.12 = (bf16[4,128,1280]{2,1,0:T(8,128)(2,1)}, bf16[4,128,1280]{2,1,0:T(8,128)(2,1)}, u32[]{:S(2)}, u32[]{:S(2)}) collective-permute-start(bf16[4,128,1280]{2,1,0:T(8,128)(2,1)} %copy-done.12), channel_id=1, source_target_pairs={{0,4},{1,13},{4,8},{5,1},{8,12},{9,5},{12,0},{13,9},{2,6},{3,15},{... | collective-permute-start | bytes 3932168 | tf_op jit(solution)/shard_map/ppermute | solution.py:253
  99.2 16.1 %integrals3.1.refs_1_ = bf16[128,160,128]{2,1,0:T(8,128)(2,1)} custom-call(s32[16]{0:T(128)} %stack.58.place, bf16[4,128,1280]{2,1,0:T(8,128)(2,1)} %pad_maximum_fusion.l0, bf16[4,128,1280]{2,1,0:T(8,128)(2,1)} %copy-done.12, bf16[4,128,1280]{2,1,0:T(8,128)(2,1)} %collective-permute-done.9.l2, bf16[4,128,1280]{2,1,0:T(8,128)(2,1)} %pad_maximum_fusion.1.refs_0_, ...), custom_call_target="tpu_custom_call" | custom-call | flops 10000000000 | bytes 10000000 | tf_op jit(solution)/shard_map/integrals3/pallas_call | solution.py:126
  117.4 2.3 %collective-permute-done.13.refs_7_ = bf16[4,128,1280]{2,1,0:T(8,128)(2,1)S(1)} collective-permute-done((bf16[4,128,1280]{2,1,0:T(8,128)(2,1)}, bf16[4,128,1280]{2,1,0:T(8,128)(2,1)S(1)}, u32[]{:S(2)}, u32[]{:S(2)}) %collective-permute-start.13) | collective-permute-done | bytes 1310752 | tf_op jit(solution)/shard_map/ppermute | solution.py:244
  120.8 24.1 %far_ladder.1 = bf16[2,16,16,256]{3,2,1,0:T(8,128)(2,1)} custom-call(s32[16]{0:T(128)} %stack.58.place, bf16[128,128,128]{2,1,0:T(8,128)(2,1)} %integrals2.1.refs_1_.x1, bf16[128,160,128]{2,1,0:T(8,128)(2,1)} %get-tuple-element.7.x2, bf16[4,128,1280]{2,1,0:T(8,128)(2,1)} %pad_maximum_fusion.l0, bf16[4,128,1280]{2,1,0:T(8,128)(2,1)} %copy-done.12, ...), custom_call_target="tpu_custom_call" | custom-call | flops 15000000512 | bytes 10000000 | tf_op jit(solution)/shard_map/far_ladder/pallas_call | solution.py:222
  144.8 7.2 %all-to-all-start = ((bf16[32,16,256]{2,1,0:T(8,128)(2,1)}), bf16[32,16,256]{2,1,0:T(8,128)(2,1)S(1)}, u32[]{:S(2)}, u32[]{:S(2)}) async-start(bf16[32,16,256]{2,1,0:T(8,128)(2,1)} %bitcast.65), calls=%async_computation | async-start | bytes 524288 | tf_op jit(solution)/shard_map/all_to_all | solution.py:309
  155.4 5.4 %all-to-all-done = bf16[32,16,256]{2,1,0:T(8,128)(2,1)S(1)} async-done(((bf16[32,16,256]{2,1,0:T(8,128)(2,1)}), bf16[32,16,256]{2,1,0:T(8,128)(2,1)S(1)}, u32[]{:S(2)}, u32[]{:S(2)}) %all-to-all-start) | async-done | bytes 262176 | tf_op jit(solution)/shard_map/all_to_all | solution.py:309
  (76 shorter events, 22.2 us)
Async XLA Ops:
  6.5 109.9 %copy-start = (s32[256,2]{0,1:T(2,128)S(1)}, s32[256,2]{0,1:T(2,128)}, u32[]{:S(2)}) copy-start(s32[256,2]{0,1:T(2,128)} %param.13) | copy-start | bytes 6148
  6.5 45.8 %all-gather.6.cloned.1.call-start = ((), (), s32[]{:S(2)}) async-start(), calls=%async_computation.1 | async-start | bytes 1310720 | tf_op jit(solution)/shard_map/all_gather | solution.py:290
  8.6 6.8 %copy-start.7 = (bf16[16,16,128]{2,1,0:T(8,128)(2,1)S(1)}, bf16[16,16,128]{2,1,0:T(8,128)(2,1)}, u32[]{:S(2)}) copy-start(bf16[16,16,128]{2,1,0:T(8,128)(2,1)} %param.10) | copy-start | bytes 196612
  9.7 19.3 %collective-permute-start = (bf16[2,128,1280]{2,1,0:T(8,128)(2,1)}, bf16[2,128,1280]{2,1,0:T(8,128)(2,1)S(1)}, u32[]{:S(2)}, u32[]{:S(2)}) collective-permute-start(bf16[2,128,1280]{2,1,0:T(8,128)(2,1)} %bitcast.19), channel_id=1, source_target_pairs={{0,2},{2,16},{16,18},{18,0},{1,3},{3,17},{17,19},{19,1},{4,6},{6,2... | collective-permute-start | bytes 1966088 | tf_op jit(solution)/shard_map/ppermute | solution.py:248
  13.3 15.9 %collective-permute-start.1 = (bf16[2,128,1280]{2,1,0:T(8,128)(2,1)}, bf16[2,128,1280]{2,1,0:T(8,128)(2,1)S(1)}, u32[]{:S(2)}, u32[]{:S(2)}) collective-permute-start(bf16[2,128,1280]{2,1,0:T(8,128)(2,1)} %bitcast.21), channel_id=1, source_target_pairs={{0,18},{2,0},{16,2},{18,16},{1,19},{3,1},{17,3},{19,17},{4,22},{6,... | collective-permute-start | bytes 1966088 | tf_op jit(solution)/shard_map/ppermute | solution.py:248
  27.2 92.5 %all-gather.8.cloned.1.call-start = ((), (), s32[]{:S(2)}) async-start(), calls=%async_computation.2 | async-start | bytes 9437184 | tf_op jit(solution)/shard_map/all_gather | solution.py:294
  30.1 4.0 %copy-start.3 = (bf16[2,128,1280]{2,1,0:T(8,128)(2,1)S(1)}, bf16[2,128,1280]{2,1,0:T(8,128)(2,1)}, u32[]{:S(2)}) copy-start(bf16[2,128,1280]{2,1,0:T(8,128)(2,1)} %copy-done.2) | copy-start | bytes 1966084
  30.1 15.5 %collective-permute-start.2 = (bf16[2,128,1280]{2,1,0:T(8,128)(2,1)}, bf16[2,128,1280]{2,1,0:T(8,128)(2,1)S(1)}, u32[]{:S(2)}, u32[]{:S(2)}) collective-permute-start(bf16[2,128,1280]{2,1,0:T(8,128)(2,1)} %gate.4), channel_id=1, source_target_pairs={{0,16},{2,18},{16,0},{18,2},{1,17},{3,19},{17,1},{19,3},{4,20},{6,... | collective-permute-start | bytes 1966088 | tf_op jit(solution)/shard_map/ppermute | solution.py:248
  46.9 6.2 %collective-permute-start.4 = (bf16[4,128,1280]{2,1,0:T(8,128)(2,1)}, bf16[4,128,1280]{2,1,0:T(8,128)(2,1)S(1)}, u32[]{:S(2)}, u32[]{:S(2)}) collective-permute-start(bf16[4,128,1280]{2,1,0:T(8,128)(2,1)} %pad_maximum_fusion.1.refs_0_), channel_id=1, source_target_pairs={{0,1},{1,0},{2,3},{3,2},{4,5},{5,4},{6,7},{7,6},{8,9},{9,8},{10,11... | collective-permute-start | bytes 3932168 | tf_op jit(solution)/shard_map/ppermute | solution.py:244
  51.5 3.5 %collective-permute-start.8 = (bf16[4,128,1280]{2,1,0:T(8,128)(2,1)}, bf16[4,128,1280]{2,1,0:T(8,128)(2,1)S(1)}, u32[]{:S(2)}, u32[]{:S(2)}) collective-permute-start(bf16[4,128,1280]{2,1,0:T(8,128)(2,1)} %pad_maximum_fusion.l0), channel_id=1, source_target_pairs={{0,1},{1,0},{2,3},{3,2},{4,5},{5,4},{6,7},{7,6},{8,9},{9,8},{10,11... | collective-permute-start | bytes 3932168 | tf_op jit(solution)/shard_map/ppermute | solution.py:244
  53.1 1.9 %copy-start.4 = (bf16[4,128,1280]{2,1,0:T(8,128)(2,1)}, bf16[4,128,1280]{2,1,0:T(8,128)(2,1)S(1)}, u32[]{:S(2)}) copy-start(bf16[4,128,1280]{2,1,0:T(8,128)(2,1)S(1)} %collective-permute-done.4.refs_1_.refs_2_) | copy-start | bytes 3932164
  56.1 17.7 %collective-permute-start.5 = (bf16[4,128,1280]{2,1,0:T(8,128)(2,1)}, bf16[4,128,1280]{2,1,0:T(8,128)(2,1)S(1)}, u32[]{:S(2)}, u32[]{:S(2)}) collective-permute-start(bf16[4,128,1280]{2,1,0:T(8,128)(2,1)} %pad_maximum_fusion.1.refs_0_), channel_id=1, source_target_pairs={{0,32},{1,97},{32,64},{33,1},{64,96},{65,33},{96,0},{97,65},{2,34}... | collective-permute-start | bytes 3932168 | tf_op jit(solution)/shard_map/ppermute | solution.py:253
  58.9 21.4 %collective-permute-start.3 = (bf16[4,128,1280]{2,1,0:T(8,128)(2,1)}, bf16[4,128,1280]{2,1,0:T(8,128)(2,1)S(1)}, u32[]{:S(2)}, u32[]{:S(2)}) collective-permute-start(bf16[4,128,1280]{2,1,0:T(8,128)(2,1)} %pad_maximum_fusion.l0), channel_id=1, source_target_pairs={{0,4},{1,13},{4,8},{5,1},{8,12},{9,5},{12,0},{13,9},{2,6},{3,15},{... | collective-permute-start | bytes 3932168 | tf_op jit(solution)/shard_map/ppermute | solution.py:253
  73.8 6.6 %copy-start.10 = (bf16[4,128,1280]{2,1,0:T(8,128)(2,1)}, bf16[4,128,1280]{2,1,0:T(8,128)(2,1)S(1)}, u32[]{:S(2)}) copy-start(bf16[4,128,1280]{2,1,0:T(8,128)(2,1)S(1)} %collective-permute-done.5.refs_2_) | copy-start | bytes 3932164
  73.8 6.5 %collective-permute-start.6 = (bf16[4,128,1280]{2,1,0:T(8,128)(2,1)S(1)}, bf16[4,128,1280]{2,1,0:T(8,128)(2,1)}, u32[]{:S(2)}, u32[]{:S(2)}) collective-permute-start(bf16[4,128,1280]{2,1,0:T(8,128)(2,1)S(1)} %collective-permute-done.5.refs_2_), channel_id=1, source_target_pairs={{0,1},{1,0},{2,3},{3,2},{4,5},{5,4},{6,7},{7,6},{8,9},{9,8},{10,11... | collective-permute-start | bytes 3932168 | tf_op jit(solution)/shard_map/ppermute | solution.py:244
  75.6 18.4 %collective-permute-start.10 = (bf16[4,128,1280]{2,1,0:T(8,128)(2,1)}, bf16[4,128,1280]{2,1,0:T(8,128)(2,1)}, u32[]{:S(2)}, u32[]{:S(2)}) collective-permute-start(bf16[4,128,1280]{2,1,0:T(8,128)(2,1)} %copy-done.4), channel_id=1, source_target_pairs={{0,32},{1,97},{32,64},{33,1},{64,96},{65,33},{96,0},{97,65},{2,34}... | collective-permute-start | bytes 3932168 | tf_op jit(solution)/shard_map/ppermute | solution.py:253
  77.8 20.3 %collective-permute-start.9 = (bf16[4,128,1280]{2,1,0:T(8,128)(2,1)}, bf16[4,128,1280]{2,1,0:T(8,128)(2,1)}, u32[]{:S(2)}, u32[]{:S(2)}) collective-permute-start(bf16[4,128,1280]{2,1,0:T(8,128)(2,1)} %copy-done.5), channel_id=1, source_target_pairs={{0,4},{1,13},{4,8},{5,1},{8,12},{9,5},{12,0},{13,9},{2,6},{3,15},{... | collective-permute-start | bytes 3932168 | tf_op jit(solution)/shard_map/ppermute | solution.py:253
  94.0 4.1 %collective-permute-start.11 = (bf16[4,128,1280]{2,1,0:T(8,128)(2,1)}, bf16[4,128,1280]{2,1,0:T(8,128)(2,1)S(1)}, u32[]{:S(2)}, u32[]{:S(2)}) collective-permute-start(bf16[4,128,1280]{2,1,0:T(8,128)(2,1)} %gate.5.refs_3_), channel_id=1, source_target_pairs={{0,1},{1,0},{2,3},{3,2},{4,5},{5,4},{6,7},{7,6},{8,9},{9,8},{10,11... | collective-permute-start | bytes 3932168 | tf_op jit(solution)/shard_map/ppermute | solution.py:244
  95.3 20.1 %collective-permute-start.7 = (bf16[4,128,1280]{2,1,0:T(8,128)(2,1)S(1)}, bf16[4,128,1280]{2,1,0:T(8,128)(2,1)S(1)}, u32[]{:S(2)}, u32[]{:S(2)}) collective-permute-start(bf16[4,128,1280]{2,1,0:T(8,128)(2,1)S(1)} %copy-done.11), channel_id=1, source_target_pairs={{0,32},{1,97},{32,64},{33,1},{64,96},{65,33},{96,0},{97,65},{2,34}... | collective-permute-start | bytes 3932168 | tf_op jit(solution)/shard_map/ppermute | solution.py:253
  95.8 21.7 %collective-permute-start.12 = (bf16[4,128,1280]{2,1,0:T(8,128)(2,1)}, bf16[4,128,1280]{2,1,0:T(8,128)(2,1)}, u32[]{:S(2)}, u32[]{:S(2)}) collective-permute-start(bf16[4,128,1280]{2,1,0:T(8,128)(2,1)} %copy-done.12), channel_id=1, source_target_pairs={{0,4},{1,13},{4,8},{5,1},{8,12},{9,5},{12,0},{13,9},{2,6},{3,15},{... | collective-permute-start | bytes 3932168 | tf_op jit(solution)/shard_map/ppermute | solution.py:253
  115.3 1.9 %copy-start.9 = (f32[100]{0:T(128)S(1)}, f32[100]{0:T(128)}, u32[]{:S(2)}) copy-start(f32[100]{0:T(128)} %param.12) | copy-start | bytes 1204
  116.4 3.2 %collective-permute-start.13 = (bf16[4,128,1280]{2,1,0:T(8,128)(2,1)}, bf16[4,128,1280]{2,1,0:T(8,128)(2,1)S(1)}, u32[]{:S(2)}, u32[]{:S(2)}) collective-permute-start(bf16[4,128,1280]{2,1,0:T(8,128)(2,1)} %get-tuple-element.8.refs_6_), channel_id=1, source_target_pairs={{0,1},{1,0},{2,3},{3,2},{4,5},{5,4},{6,7},{7,6},{8,9},{9,8},{10,11... | collective-permute-start | bytes 3932168 | tf_op jit(solution)/shard_map/ppermute | solution.py:244
  120.8 31.3 %copy-start.8 = (s32[2]{0:T(128)S(1)}, s32[2]{0:T(128)}, u32[]{:S(2)}) copy-start(s32[2]{0:T(128)} %param.14) | copy-start | bytes 28
  144.8 16.0 %all-to-all-start = ((bf16[32,16,256]{2,1,0:T(8,128)(2,1)}), bf16[32,16,256]{2,1,0:T(8,128)(2,1)S(1)}, u32[]{:S(2)}, u32[]{:S(2)}) async-start(bf16[32,16,256]{2,1,0:T(8,128)(2,1)} %bitcast.65), calls=%async_computation | async-start | bytes 524288 | tf_op jit(solution)/shard_map/all_to_all | solution.py:309
  (8 other events, 8.6 us)
Sparse Core Ops, SparseCore 0:
  27.3 25.0 all-gather.5
  56.2 51.9 all-gather.7

commit v4 on v3

--- a/solution.py
+++ b/solution.py
@@ -12,11 +12,11 @@
 QP = 1280
 W = 128
 CC = 16
-ROWS1, ROWS2, ROWS3 = 128, 160, 224
-FIRST = ((0, 1, 2, 4), (3, 5), (6, 7))
+ROWS1, ROWS2, ROWS3 = 96, 192, 224
+FIRST = ((0, 1, 2), (3, 4, 5), (6, 7))
 ANYWHERE = pl.BlockSpec(memory_space=pl.ANY)
 SCALARS = pl.BlockSpec(memory_space=pltpu.SMEM)
-LIMIT = 58 * 2**20
+LIMIT = 50 * 2**20
 
 
 def gate(values, after):
@@ -31,6 +31,7 @@
         in_specs=[ANYWHERE] * (count + len(after)),
         out_specs=[ANYWHERE] * count,
         input_output_aliases={k: k for k in range(count)},
+        compiler_params=pltpu.CompilerParams(vmem_limit_bytes=2**20),
         name="gate",
     )(*values, *after)
 
@@ -79,8 +80,8 @@
 
 
 def first_kernel(place, l0, l1, *refs):
-    rights, (xs, lbuf, rbuf, scr, xbuf, sems, out_sems) = refs[:4], refs[4:]
-    copies = [pltpu.make_async_copy(ref, lbuf.at[u], sems.at[4 + u]) for u, ref in enumerate((l0, l1))]
+    rights, (xs, lbuf, rbuf, scr, xbuf, sems, out_sems) = refs[:3], refs[3:]
+    copies = [pltpu.make_async_copy(ref, lbuf.at[u], sems.at[3 + u]) for u, ref in enumerate((l0, l1))]
     copies += [pltpu.make_async_copy(ref, rbuf.at[g], sems.at[g]) for g, ref in enumerate(rights)]
     for copy in copies:
         copy.start()
@@ -92,29 +93,29 @@
         pair_integrals(place, lbuf[...], rbuf[g], scr, ROWS1 + 8, g * 32)
         return carry
 
-    lax.fori_loop(0, 4, block, 0)
+    lax.fori_loop(0, 3, block, 0)
     round_out(scr, xbuf, xs, ROWS1, out_sems)
 
 
 def second_kernel(place, l0, l1, l2, *refs):
     rights, (xs, lbuf, rbuf, scr, xbuf, sems, out_sems) = refs[:6], refs[6:]
     copies = [pltpu.make_async_copy(ref, lbuf.at[u], sems.at[6 + u]) for u, ref in enumerate((l0, l1, l2))]
-    copies += [pltpu.make_async_copy(rights[g], rbuf.at[g], sems.at[g]) for g in (3, 5, 0, 1, 2, 4)]
+    copies += [pltpu.make_async_copy(rights[g], rbuf.at[g], sems.at[g]) for g in (3, 4, 5, 0, 1, 2)]
     for copy in copies:
         copy.start()
-    for copy in copies[:5]:
+    for copy in copies[:6]:
         copy.wait()
 
     def pairs(k, carry):
-        pair_integrals(place, lbuf[:2], rbuf[3 + 2 * k], scr, ROWS2 + 8, k * 32)
-        return carry
-
-    lax.fori_loop(0, 2, pairs, 0)
-    for copy in copies[5:]:
+        pair_integrals(place, lbuf[:2], rbuf[3 + k], scr, ROWS2 + 8, k * 32)
+        return carry
+
+    lax.fori_loop(0, 3, pairs, 0)
+    for copy in copies[6:]:
         copy.wait()
 
     def singles(g, carry):
-        single_integrals(place, lbuf[2], rbuf[g], place[4 + g], scr, ROWS2 + 8, 64 + (g // 2) * 32)
+        single_integrals(place, lbuf[2], rbuf[g], place[4 + g], scr, ROWS2 + 8, 96 + (g // 2) * 32)
         return carry
 
     lax.fori_loop(0, 6, singles, 0)
@@ -127,7 +128,7 @@
         kernel,
         out_shape=jax.ShapeDtypeStruct((W, rows, W), jnp.bfloat16),
         in_specs=[SCALARS] + [ANYWHERE] * (units + count),
-        out_specs=ANYWHERE,
+        out_specs=pl.BlockSpec(memory_space=pltpu.HBM),
         scratch_shapes=[
             pltpu.VMEM((units, 4, W, QP), jnp.bfloat16),
             pltpu.VMEM((count, 4, W, QP), jnp.bfloat16),
@@ -136,8 +137,8 @@
             pltpu.SemaphoreType.DMA((units + count,)),
             pltpu.SemaphoreType.DMA((4,)),
         ],
-        compiler_params=pltpu.CompilerParams(vmem_limit_bytes=LIMIT),
-        cost_estimate=pl.CostEstimate(flops=10 * 10**9, bytes_accessed=10**7, transcendentals=0),
+        compiler_params=pltpu.CompilerParams(vmem_limit_bytes=(26 if units == 2 else 34) * 2**20),
+        cost_estimate=pl.CostEstimate(flops=10**6, bytes_accessed=10**4, transcendentals=0),
         name="integrals%d" % units,
     )(place, *lefts, *rights)
 
@@ -256,7 +257,7 @@
 def lane_table():
     table = np.full((4, 4, 2, 512), -1, np.int32)
     group_of = {block: k for k, block in enumerate(FIRST[0])}
-    group_of.update({FIRST[1][k]: 4 + k for k in range(2)})
+    group_of.update({FIRST[1][k]: 3 + k for k in range(3)})
     group_of.update({FIRST[2][k]: 9 + k for k in range(2)})
     for y, x, far, zl, c, yb, zb, cb in np.ndindex(4, 4, 4, 2, 2, 4, 4, 2):
         step = (far - x) % 4
@@ -299,11 +300,11 @@
     cores = [core, 1 - core, core, 1 - core, 1 - core, core, core, 1 - core]
     zs = [(z + k) % 4 for k in RING]
     place = jnp.stack(zs + cores + [(k // 2) * 16 + (k % 2) * 4 for k in zs]).astype(jnp.int32)
-    x1 = integrals(first_kernel, ROWS1, place, (left, left_1), (right, right_s, right_1, right_1p))
+    x1 = integrals(first_kernel, ROWS1, place, (left, left_1), (right, right_s, right_1))
     right_1s = gate([right_1s], [x1])[0]
     rights = (right, right_s, right_1, right_1s, right_1p, swap(right_1s))
     x2 = integrals(second_kernel, ROWS2, place, (left, left_1, left_1s), rights)
-    right_2, x2 = gate([right_2, x2], [])
+    right_2 = gate([right_2], [x2])[0]
     rights = rights + (right_2, swap(right_2))
     partial = far_ladder(place, x1, x2, (left, left_1, left_1s, left_2), amps, rights)
     gathered = lax.all_to_all(partial.reshape(32, 16, 256), ("zh", "x", "zl", "c"), 0, 0, tiled=True)

time: 171 us -> 164 us (0.959)
  Pallas kernels: 52.7 us -> 47.9 us
  starting transfers between devices: 32.7 us -> 30.4 us
  other arithmetic: 5.31 us -> 3.18 us
  waiting for transfers between devices: 35.6 us -> 37.6 us
    pallas_call x2, Pallas kernels: 28.6 us -> 24.4 us  [integrals(): pl.pallas_call(kernel, out_shape=jax.ShapeDtypeStruct((W, rows, W), jnp.b...]
    all_gather x1, waiting for transfers between devices: 0.92 us -> 3.95 us  [shards(): amps = lax.all_gather(amps, 'y', axis=0)]
    ppermute x6, starting transfers between devices: 12.2 us -> 9.58 us  [onward(): return lax.ppermute(value, (axis, 'c'), pairs)]
    ppermute x3, waiting for transfers between devices: 11.9 us -> 14.4 us  [shift(): return lax.ppermute(value, axis, [(i, (i + step) % 4) for i in range(4)])]
    ppermute x5, waiting for transfers between devices: 4.86 us -> 2.57 us  [swap(): return lax.ppermute(value, 'c', [(0, 1), (1, 0)])]
    unnamed x34 -> x42, local copies, waits for them, and re-layouts: 10.6 us -> 11.6 us
  transfers between devices with their start and end apart: 17 -> 17, of which waited for: 9 -> 9; matrix products, arithmetic and copies ran while one was open for 6% -> 4% of each run, Pallas kernels for 17% -> 15%
where the time goes in v4:
time: 164 us; the launch traced here: 163 us
  Pallas kernels  47.9 us (29%)
  waiting for transfers between devices  37.6 us (23%)
  starting transfers between devices  30.4 us (19%)
  local copies, waits for them, and re-layouts  17.6 us (11%)
  between operations  15 us (9%)
  blocking collectives  10.8 us (7%)
  other arithmetic  3.18 us (2%)
    pallas_call x2, Pallas kernels, integrals(): pl.pallas_call(kernel, out_shape=jax.ShapeDtypeStruct((W, rows, W), jnp.b...  24.4 us
    pallas_call x1, Pallas kernels, far_ladder(): pl.pallas_call(far_kernel, out_shape=jax.ShapeDtypeStruct((2, 16, 16, 256...  23.5 us
    ppermute x3, waiting for transfers between devices, shift(): return lax.ppermute(value, axis, [(i, (i + step) % 4) for i in range(4)])  14.4 us
    unnamed x42, local copies, waits for them, and re-layouts  11.6 us
    ppermute x6, waiting for transfers between devices, onward(): return lax.ppermute(value, (axis, 'c'), pairs)  11.3 us
    all_gather x1, blocking collectives, shards(): amps = lax.all_gather(jnp.transpose(amplitudes, (1, 0, 2)), 'x', axis=0)  10.8 us
    ppermute x6, starting transfers between devices, onward(): return lax.ppermute(value, (axis, 'c'), pairs)  9.58 us
    ppermute x3, starting transfers between devices, shift(): return lax.ppermute(value, axis, [(i, (i + step) % 4) for i in range(4)])  7.53 us
  transfers between devices with their start and end apart: 17, of which 9 were waited for; matrix products, arithmetic and copies ran while one was open for 4% of the time, Pallas kernels for 15%

profile of v4, /device:TPU:1, one launch (start us, length us, event | category | flops | bytes accessed | tf_op | source)
XLA Modules:
  0.0 163.3 jit_solution(5709412065597337972)
XLA Ops:
  6.5 1.9 %fusion.5 = bf16[2,5120,128]{2,1,0:T(8,128)(2,1)S(1)} fusion(bf16[1,5000,128]{2,1,0:T(8,128)(2,1)} %bitcast.62, bf16[1,5000,128]{2,1,0:T(8,128)(2,1)} %bitcast.63), kind=kLoop, calls=%fused_computation.6 | loop fusion | flops 9175040 | bytes 5181440 | tf_op jit(solution)/shard_map/stack | solution.py:283
  9.7 2.5 %collective-permute-start = (bf16[2,128,1280]{2,1,0:T(8,128)(2,1)}, bf16[2,128,1280]{2,1,0:T(8,128)(2,1)S(1)}, u32[]{:S(2)}, u32[]{:S(2)}) collective-permute-start(bf16[2,128,1280]{2,1,0:T(8,128)(2,1)} %bitcast.19), channel_id=1, source_target_pairs={{0,2},{2,16},{16,18},{18,0},{1,3},{3,17},{17,19},{19,1},{4,6},{6,2... | collective-permute-start | bytes 1966088 | tf_op jit(solution)/shard_map/ppermute | solution.py:249
  13.4 2.1 %collective-permute-start.1 = (bf16[2,128,1280]{2,1,0:T(8,128)(2,1)}, bf16[2,128,1280]{2,1,0:T(8,128)(2,1)S(1)}, u32[]{:S(2)}, u32[]{:S(2)}) collective-permute-start(bf16[2,128,1280]{2,1,0:T(8,128)(2,1)} %bitcast.21), channel_id=1, source_target_pairs={{0,18},{2,0},{16,2},{18,16},{1,19},{3,1},{17,3},{19,17},{4,22},{6,... | collective-permute-start | bytes 1966088 | tf_op jit(solution)/shard_map/ppermute | solution.py:249
  15.5 10.8 %all-gather = bf16[64,16,128]{2,0,1:T(8,128)(2,1)S(1)} all-gather(bf16[16,16,128]{2,0,1:T(8,128)(2,1)S(1)} %bitcast.67), channel_id=2, replica_groups=mesh['y'=4,'zh'=2,'x'=4,'zl'=2,'c'=2] {'x'}, dimensions={0}, use_global_device_ids=true | all-gather | bytes 327680 | tf_op jit(solution)/shard_map/all_gather | solution.py:288
  29.2 2.9 %collective-permute-start.2 = (bf16[2,128,1280]{2,1,0:T(8,128)(2,1)S(1)}, bf16[2,128,1280]{2,1,0:T(8,128)(2,1)S(1)}, u32[]{:S(2)}, u32[]{:S(2)}) collective-permute-start(bf16[2,128,1280]{2,1,0:T(8,128)(2,1)S(1)} %gate.4), channel_id=1, source_target_pairs={{0,16},{2,18},{16,0},{18,2},{1,17},{3,19},{17,1},{19,3},{4,20},{6,... | collective-permute-start | bytes 1966088 | tf_op jit(solution)/shard_map/ppermute | solution.py:249
  32.3 13.0 %collective-permute-done.2 = bf16[2,128,1280]{2,1,0:T(8,128)(2,1)S(1)} collective-permute-done((bf16[2,128,1280]{2,1,0:T(8,128)(2,1)S(1)}, bf16[2,128,1280]{2,1,0:T(8,128)(2,1)S(1)}, u32[]{:S(2)}, u32[]{:S(2)}) %collective-permute-start.2) | collective-permute-done | bytes 655392 | tf_op jit(solution)/shard_map/ppermute | solution.py:249
  45.5 2.7 %collective-permute-start.4 = (bf16[4,128,1280]{2,1,0:T(8,128)(2,1)S(1)}, bf16[4,128,1280]{2,1,0:T(8,128)(2,1)}, u32[]{:S(2)}, u32[]{:S(2)}) collective-permute-start(bf16[4,128,1280]{2,1,0:T(8,128)(2,1)S(1)} %pad_maximum_fusion.1.refs_0_), channel_id=1, source_target_pairs={{0,1},{1,0},{2,3},{3,2},{4,5},{5,4},{6,7},{7,6},{8,9},{9,8},{10,11... | collective-permute-start | bytes 3932168 | tf_op jit(solution)/shard_map/ppermute | solution.py:245
  48.5 4.0 %all-gather.6.cloned.1.call-done = bf16[16,16,16,128]{3,2,1,0:T(8,128)(2,1)} async-done(((bf16[4,16,16,128]{3,2,1,0:T(8,128)(2,1)}), bf16[16,16,16,128]{3,2,1,0:T(8,128)(2,1)}) %all-gather.6.cloned.1.call-update) | async-done | bytes 1048592 | tf_op jit(solution)/shard_map/all_gather | solution.py:291
  55.1 2.8 %collective-permute-start.5 = (bf16[4,128,1280]{2,1,0:T(8,128)(2,1)S(1)}, bf16[4,128,1280]{2,1,0:T(8,128)(2,1)}, u32[]{:S(2)}, u32[]{:S(2)}) collective-permute-start(bf16[4,128,1280]{2,1,0:T(8,128)(2,1)S(1)} %pad_maximum_fusion.1.refs_0_), channel_id=1, source_target_pairs={{0,32},{1,97},{32,64},{33,1},{64,96},{65,33},{96,0},{97,65},{2,34}... | collective-permute-start | bytes 3932168 | tf_op jit(solution)/shard_map/ppermute | solution.py:254
  57.9 2.5 %collective-permute-start.3 = (bf16[4,128,1280]{2,1,0:T(8,128)(2,1)S(1)}, bf16[4,128,1280]{2,1,0:T(8,128)(2,1)}, u32[]{:S(2)}, u32[]{:S(2)}) collective-permute-start(bf16[4,128,1280]{2,1,0:T(8,128)(2,1)S(1)} %pad_maximum_fusion.l0), channel_id=1, source_target_pairs={{0,4},{1,13},{4,8},{5,1},{8,12},{9,5},{12,0},{13,9},{2,6},{3,15},{... | collective-permute-start | bytes 3932168 | tf_op jit(solution)/shard_map/ppermute | solution.py:254
  61.6 10.9 %collective-permute-done.5.refs_2_ = bf16[4,128,1280]{2,1,0:T(8,128)(2,1)} collective-permute-done((bf16[4,128,1280]{2,1,0:T(8,128)(2,1)S(1)}, bf16[4,128,1280]{2,1,0:T(8,128)(2,1)}, u32[]{:S(2)}, u32[]{:S(2)}) %collective-permute-start.5) | collective-permute-done | bytes 1310752 | tf_op jit(solution)/shard_map/ppermute | solution.py:254
  72.4 2.8 %collective-permute-start.9 = (bf16[4,128,1280]{2,1,0:T(8,128)(2,1)}, bf16[4,128,1280]{2,1,0:T(8,128)(2,1)S(1)}, u32[]{:S(2)}, u32[]{:S(2)}) collective-permute-start(bf16[4,128,1280]{2,1,0:T(8,128)(2,1)} %collective-permute-done.5.refs_2_), channel_id=1, source_target_pairs={{0,1},{1,0},{2,3},{3,2},{4,5},{5,4},{6,7},{7,6},{8,9},{9,8},{10,11... | collective-permute-start | bytes 3932168 | tf_op jit(solution)/shard_map/ppermute | solution.py:245
  75.2 1.3 copy-done.4
  76.6 1.3 copy-done.7
  77.9 8.3 %integrals2.1.refs_1_.x1 = bf16[128,96,128]{2,1,0:T(8,128)(2,1)S(1)} custom-call(s32[16]{0:T(128)S(1)} %stack.58.place, bf16[4,128,1280]{2,1,0:T(8,128)(2,1)S(1)} %copy-done.7, bf16[4,128,1280]{2,1,0:T(8,128)(2,1)} %collective-permute-done.3.l1, bf16[4,128,1280]{2,1,0:T(8,128)(2,1)S(1)} %copy-done.4, ...), custom_call_target="tpu_custom_call" | custom-call | flops 1000000 | bytes 10000 | tf_op jit(solution)/shard_map/integrals2/pallas_call | solution.py:127
  87.8 1.5 collective-permute-start.10
  89.3 1.5 collective-permute-start.12
  90.8 1.7 %collective-permute-start.11 = (bf16[4,128,1280]{2,1,0:T(8,128)(2,1)}, bf16[4,128,1280]{2,1,0:T(8,128)(2,1)}, u32[]{:S(2)}, u32[]{:S(2)}) collective-permute-start(bf16[4,128,1280]{2,1,0:T(8,128)(2,1)} %collective-permute-done.3.l1), channel_id=1, source_target_pairs={{0,4},{1,13},{4,8},{5,1},{8,12},{9,5},{12,0},{13,9},{2,6},{3,15},{... | collective-permute-start | bytes 3932168 | tf_op jit(solution)/shard_map/ppermute | solution.py:254
  92.6 16.1 %integrals3.1.refs_1_.x2 = bf16[128,192,128]{2,1,0:T(8,128)(2,1)S(1)} custom-call(s32[16]{0:T(128)S(1)} %stack.58.place, bf16[4,128,1280]{2,1,0:T(8,128)(2,1)S(1)} %copy-done.8, bf16[4,128,1280]{2,1,0:T(8,128)(2,1)} %collective-permute-done.3.l1, bf16[4,128,1280]{2,1,0:T(8,128)(2,1)S(1)} %collective-permute-done.7.l2, bf16[4,128,1280]{2,1,0:T(8,128)(2,1)S(1)} %copy-done.5, ...), custom_call_target="tpu_custom_call" | custom-call | flops 1000000 | bytes 10000 | tf_op jit(solution)/shard_map/integrals3/pallas_call | solution.py:127
  108.8 2.7 %copy-done.1 = bf16[128,192,128]{2,1,0:T(8,128)(2,1)} copy-done((bf16[128,192,128]{2,1,0:T(8,128)(2,1)}, bf16[128,192,128]{2,1,0:T(8,128)(2,1)S(1)}, u32[]{:S(2)}) %copy-start.1) | copy-done | bytes 6291480
  112.5 2.1 %collective-permute-done.13.refs_7_ = bf16[4,128,1280]{2,1,0:T(8,128)(2,1)} collective-permute-done((bf16[4,128,1280]{2,1,0:T(8,128)(2,1)S(1)}, bf16[4,128,1280]{2,1,0:T(8,128)(2,1)}, u32[]{:S(2)}, u32[]{:S(2)}) %collective-permute-start.13) | collective-permute-done | bytes 1310752 | tf_op jit(solution)/shard_map/ppermute | solution.py:245
  114.6 23.5 %far_ladder.1 = bf16[2,16,16,256]{3,2,1,0:T(8,128)(2,1)} custom-call(s32[16]{0:T(128)S(1)} %stack.58.place, bf16[128,96,128]{2,1,0:T(8,128)(2,1)} %copy-done.2, bf16[128,192,128]{2,1,0:T(8,128)(2,1)} %copy-done.1, bf16[4,128,1280]{2,1,0:T(8,128)(2,1)S(1)} %copy-done.9, bf16[4,128,1280]{2,1,0:T(8,128)(2,1)} %collective-permute-done.3.l1, ...), custom_call_target="tpu_custom_call" | custom-call | flops 15000000512 | bytes 10000000 | tf_op jit(solution)/shard_map/far_ladder/pallas_call | solution.py:223
  138.1 6.2 %all-to-all-start = ((bf16[32,16,256]{2,1,0:T(8,128)(2,1)}), bf16[32,16,256]{2,1,0:T(8,128)(2,1)S(1)}, u32[]{:S(2)}, u32[]{:S(2)}) async-start(bf16[32,16,256]{2,1,0:T(8,128)(2,1)} %bitcast.29), calls=%async_computation | async-start | bytes 524288 | tf_op jit(solution)/shard_map/all_to_all | solution.py:310
  147.9 5.3 %all-to-all-done = bf16[32,16,256]{2,1,0:T(8,128)(2,1)S(1)} async-done(((bf16[32,16,256]{2,1,0:T(8,128)(2,1)}), bf16[32,16,256]{2,1,0:T(8,128)(2,1)S(1)}, u32[]{:S(2)}, u32[]{:S(2)}) %all-to-all-start) | async-done | bytes 262176 | tf_op jit(solution)/shard_map/all_to_all | solution.py:310
  (84 shorter events, 17.8 us)
Async XLA Ops:
  6.5 104.9 %copy-start = (s32[256,2]{0,1:T(2,128)S(1)}, s32[256,2]{0,1:T(2,128)}, u32[]{:S(2)}) copy-start(s32[256,2]{0,1:T(2,128)} %param.13) | copy-start | bytes 6148
  6.5 45.9 %all-gather.6.cloned.1.call-start = ((), (), s32[]{:S(2)}) async-start(), calls=%async_computation.1 | async-start | bytes 1310720 | tf_op jit(solution)/shard_map/all_gather | solution.py:291
  9.7 19.3 %collective-permute-start = (bf16[2,128,1280]{2,1,0:T(8,128)(2,1)}, bf16[2,128,1280]{2,1,0:T(8,128)(2,1)S(1)}, u32[]{:S(2)}, u32[]{:S(2)}) collective-permute-start(bf16[2,128,1280]{2,1,0:T(8,128)(2,1)} %bitcast.19), channel_id=1, source_target_pairs={{0,2},{2,16},{16,18},{18,0},{1,3},{3,17},{17,19},{19,1},{4,6},{6,2... | collective-permute-start | bytes 1966088 | tf_op jit(solution)/shard_map/ppermute | solution.py:249
  13.4 15.9 %collective-permute-start.1 = (bf16[2,128,1280]{2,1,0:T(8,128)(2,1)}, bf16[2,128,1280]{2,1,0:T(8,128)(2,1)S(1)}, u32[]{:S(2)}, u32[]{:S(2)}) collective-permute-start(bf16[2,128,1280]{2,1,0:T(8,128)(2,1)} %bitcast.21), channel_id=1, source_target_pairs={{0,18},{2,0},{16,2},{18,16},{1,19},{3,1},{17,3},{19,17},{4,22},{6,... | collective-permute-start | bytes 1966088 | tf_op jit(solution)/shard_map/ppermute | solution.py:249
  27.2 87.4 %all-gather.8.cloned.1.call-start = ((), (), s32[]{:S(2)}) async-start(), calls=%async_computation.2 | async-start | bytes 9437184 | tf_op jit(solution)/shard_map/all_gather | solution.py:295
  29.2 16.1 %collective-permute-start.2 = (bf16[2,128,1280]{2,1,0:T(8,128)(2,1)S(1)}, bf16[2,128,1280]{2,1,0:T(8,128)(2,1)S(1)}, u32[]{:S(2)}, u32[]{:S(2)}) collective-permute-start(bf16[2,128,1280]{2,1,0:T(8,128)(2,1)S(1)} %gate.4), channel_id=1, source_target_pairs={{0,16},{2,18},{16,0},{18,2},{1,17},{3,19},{17,1},{19,3},{4,20},{6,... | collective-permute-start | bytes 1966088 | tf_op jit(solution)/shard_map/ppermute | solution.py:249
  45.5 9.6 %copy-start.3 = (bf16[4,128,1280]{2,1,0:T(8,128)(2,1)}, bf16[4,128,1280]{2,1,0:T(8,128)(2,1)S(1)}, u32[]{:S(2)}) copy-start(bf16[4,128,1280]{2,1,0:T(8,128)(2,1)S(1)} %pad_maximum_fusion.1.refs_0_) | copy-start | bytes 3932164
  45.5 6.9 %collective-permute-start.4 = (bf16[4,128,1280]{2,1,0:T(8,128)(2,1)S(1)}, bf16[4,128,1280]{2,1,0:T(8,128)(2,1)}, u32[]{:S(2)}, u32[]{:S(2)}) collective-permute-start(bf16[4,128,1280]{2,1,0:T(8,128)(2,1)S(1)} %pad_maximum_fusion.1.refs_0_), channel_id=1, source_target_pairs={{0,1},{1,0},{2,3},{3,2},{4,5},{5,4},{6,7},{7,6},{8,9},{9,8},{10,11... | collective-permute-start | bytes 3932168 | tf_op jit(solution)/shard_map/ppermute | solution.py:245
  48.3 9.6 %copy-start.6 = (bf16[4,128,1280]{2,1,0:T(8,128)(2,1)}, bf16[4,128,1280]{2,1,0:T(8,128)(2,1)S(1)}, u32[]{:S(2)}) copy-start(bf16[4,128,1280]{2,1,0:T(8,128)(2,1)S(1)} %pad_maximum_fusion.l0) | copy-start | bytes 3932164
  48.4 4.5 %collective-permute-start.6 = (bf16[4,128,1280]{2,1,0:T(8,128)(2,1)S(1)}, bf16[4,128,1280]{2,1,0:T(8,128)(2,1)}, u32[]{:S(2)}, u32[]{:S(2)}) collective-permute-start(bf16[4,128,1280]{2,1,0:T(8,128)(2,1)S(1)} %pad_maximum_fusion.l0), channel_id=1, source_target_pairs={{0,1},{1,0},{2,3},{3,2},{4,5},{5,4},{6,7},{7,6},{8,9},{9,8},{10,11... | collective-permute-start | bytes 3932168 | tf_op jit(solution)/shard_map/ppermute | solution.py:245
  55.1 17.4 %collective-permute-start.5 = (bf16[4,128,1280]{2,1,0:T(8,128)(2,1)S(1)}, bf16[4,128,1280]{2,1,0:T(8,128)(2,1)}, u32[]{:S(2)}, u32[]{:S(2)}) collective-permute-start(bf16[4,128,1280]{2,1,0:T(8,128)(2,1)S(1)} %pad_maximum_fusion.1.refs_0_), channel_id=1, source_target_pairs={{0,32},{1,97},{32,64},{33,1},{64,96},{65,33},{96,0},{97,65},{2,34}... | collective-permute-start | bytes 3932168 | tf_op jit(solution)/shard_map/ppermute | solution.py:254
  57.9 17.3 %collective-permute-start.3 = (bf16[4,128,1280]{2,1,0:T(8,128)(2,1)S(1)}, bf16[4,128,1280]{2,1,0:T(8,128)(2,1)}, u32[]{:S(2)}, u32[]{:S(2)}) collective-permute-start(bf16[4,128,1280]{2,1,0:T(8,128)(2,1)S(1)} %pad_maximum_fusion.l0), channel_id=1, source_target_pairs={{0,4},{1,13},{4,8},{5,1},{8,12},{9,5},{12,0},{13,9},{2,6},{3,15},{... | collective-permute-start | bytes 3932168 | tf_op jit(solution)/shard_map/ppermute | solution.py:254
  60.4 26.2 %collective-permute-start.8 = (bf16[4,128,1280]{2,1,0:T(8,128)(2,1)}, bf16[4,128,1280]{2,1,0:T(8,128)(2,1)}, u32[]{:S(2)}, u32[]{:S(2)}) collective-permute-start(bf16[4,128,1280]{2,1,0:T(8,128)(2,1)} %collective-permute-done.4.refs_1_.refs_2_), channel_id=1, source_target_pairs={{0,32},{1,97},{32,64},{33,1},{64,96},{65,33},{96,0},{97,65},{2,34}... | collective-permute-start | bytes 3932168 | tf_op jit(solution)/shard_map/ppermute | solution.py:254
  60.9 31.6 %collective-permute-start.7 = (bf16[4,128,1280]{2,1,0:T(8,128)(2,1)}, bf16[4,128,1280]{2,1,0:T(8,128)(2,1)S(1)}, u32[]{:S(2)}, u32[]{:S(2)}) collective-permute-start(bf16[4,128,1280]{2,1,0:T(8,128)(2,1)} %collective-permute-done.6.refs_1_), channel_id=1, source_target_pairs={{0,4},{1,13},{4,8},{5,1},{8,12},{9,5},{12,0},{13,9},{2,6},{3,15},{... | collective-permute-start | bytes 3932168 | tf_op jit(solution)/shard_map/ppermute | solution.py:254
  72.4 20.1 %collective-permute-start.9 = (bf16[4,128,1280]{2,1,0:T(8,128)(2,1)}, bf16[4,128,1280]{2,1,0:T(8,128)(2,1)S(1)}, u32[]{:S(2)}, u32[]{:S(2)}) collective-permute-start(bf16[4,128,1280]{2,1,0:T(8,128)(2,1)} %collective-permute-done.5.refs_2_), channel_id=1, source_target_pairs={{0,1},{1,0},{2,3},{3,2},{4,5},{5,4},{6,7},{7,6},{8,9},{9,8},{10,11... | collective-permute-start | bytes 3932168 | tf_op jit(solution)/shard_map/ppermute | solution.py:245
  87.8 4.7 %collective-permute-start.10 = (bf16[4,128,1280]{2,1,0:T(8,128)(2,1)}, bf16[4,128,1280]{2,1,0:T(8,128)(2,1)S(1)}, u32[]{:S(2)}, u32[]{:S(2)}) collective-permute-start(bf16[4,128,1280]{2,1,0:T(8,128)(2,1)} %gate.5.refs_3_), channel_id=1, source_target_pairs={{0,1},{1,0},{2,3},{3,2},{4,5},{5,4},{6,7},{7,6},{8,9},{9,8},{10,11... | collective-permute-start | bytes 3932168 | tf_op jit(solution)/shard_map/ppermute | solution.py:245
  89.3 19.5 %collective-permute-start.12 = (bf16[4,128,1280]{2,1,0:T(8,128)(2,1)}, bf16[4,128,1280]{2,1,0:T(8,128)(2,1)S(1)}, u32[]{:S(2)}, u32[]{:S(2)}) collective-permute-start(bf16[4,128,1280]{2,1,0:T(8,128)(2,1)} %collective-permute-done.5.refs_2_), channel_id=1, source_target_pairs={{0,32},{1,97},{32,64},{33,1},{64,96},{65,33},{96,0},{97,65},{2,34}... | collective-permute-start | bytes 3932168 | tf_op jit(solution)/shard_map/ppermute | solution.py:254
  90.8 21.7 %collective-permute-start.11 = (bf16[4,128,1280]{2,1,0:T(8,128)(2,1)}, bf16[4,128,1280]{2,1,0:T(8,128)(2,1)}, u32[]{:S(2)}, u32[]{:S(2)}) collective-permute-start(bf16[4,128,1280]{2,1,0:T(8,128)(2,1)} %collective-permute-done.3.l1), channel_id=1, source_target_pairs={{0,4},{1,13},{4,8},{5,1},{8,12},{9,5},{12,0},{13,9},{2,6},{3,15},{... | collective-permute-start | bytes 3932168 | tf_op jit(solution)/shard_map/ppermute | solution.py:254
  92.5 16.2 %copy-start.14 = (bf16[4,128,1280]{2,1,0:T(8,128)(2,1)}, bf16[4,128,1280]{2,1,0:T(8,128)(2,1)S(1)}, u32[]{:S(2)}) copy-start(bf16[4,128,1280]{2,1,0:T(8,128)(2,1)S(1)} %collective-permute-done.9.refs_4_) | copy-start | bytes 3932164
  92.5 16.2 %copy-start.13 = (bf16[4,128,1280]{2,1,0:T(8,128)(2,1)}, bf16[4,128,1280]{2,1,0:T(8,128)(2,1)S(1)}, u32[]{:S(2)}) copy-start(bf16[4,128,1280]{2,1,0:T(8,128)(2,1)S(1)} %collective-permute-done.7.l2) | copy-start | bytes 3932164
  92.6 16.2 %copy-start.15 = (bf16[4,128,1280]{2,1,0:T(8,128)(2,1)}, bf16[4,128,1280]{2,1,0:T(8,128)(2,1)S(1)}, u32[]{:S(2)}) copy-start(bf16[4,128,1280]{2,1,0:T(8,128)(2,1)S(1)} %collective-permute-done.10.refs_5_) | copy-start | bytes 3932164
  111.5 3.2 %collective-permute-start.13 = (bf16[4,128,1280]{2,1,0:T(8,128)(2,1)S(1)}, bf16[4,128,1280]{2,1,0:T(8,128)(2,1)}, u32[]{:S(2)}, u32[]{:S(2)}) collective-permute-start(bf16[4,128,1280]{2,1,0:T(8,128)(2,1)S(1)} %gate.7.refs_6_), channel_id=1, source_target_pairs={{0,1},{1,0},{2,3},{3,2},{4,5},{5,4},{6,7},{7,6},{8,9},{9,8},{10,11... | collective-permute-start | bytes 3932168 | tf_op jit(solution)/shard_map/ppermute | solution.py:245
  114.6 29.7 %copy-start.17 = (s32[2]{0:T(128)S(1)}, s32[2]{0:T(128)}, u32[]{:S(2)}) copy-start(s32[2]{0:T(128)} %param.14) | copy-start | bytes 28
  138.1 15.1 %all-to-all-start = ((bf16[32,16,256]{2,1,0:T(8,128)(2,1)}), bf16[32,16,256]{2,1,0:T(8,128)(2,1)S(1)}, u32[]{:S(2)}, u32[]{:S(2)}) async-start(bf16[32,16,256]{2,1,0:T(8,128)(2,1)} %bitcast.29), calls=%async_computation | async-start | bytes 524288 | tf_op jit(solution)/shard_map/all_to_all | solution.py:310
  (12 other events, 41.4 us)
Sparse Core Ops, SparseCore 0:
  27.3 25.0 all-gather.5
  55.2 51.9 all-gather.7

commit v5 on v4

--- a/solution.py
+++ b/solution.py
@@ -11,15 +11,15 @@
 RING = (0, 3, 1, 2)
 QP = 1280
 W = 128
-CC = 16
+CC = 32
 ROWS1, ROWS2, ROWS3 = 96, 192, 224
 FIRST = ((0, 1, 2), (3, 4, 5), (6, 7))
 ANYWHERE = pl.BlockSpec(memory_space=pl.ANY)
 SCALARS = pl.BlockSpec(memory_space=pltpu.SMEM)
-LIMIT = 50 * 2**20
-
-
-def gate(values, after):
+LIMIT = 55 * 2**20
+
+
+def gate(values, after, limit=2**20):
     count = len(values)
 
     def nothing(*refs):
@@ -31,7 +31,7 @@
         in_specs=[ANYWHERE] * (count + len(after)),
         out_specs=[ANYWHERE] * count,
         input_output_aliases={k: k for k in range(count)},
-        compiler_params=pltpu.CompilerParams(vmem_limit_bytes=2**20),
+        compiler_params=pltpu.CompilerParams(vmem_limit_bytes=limit),
         name="gate",
     )(*values, *after)
 
@@ -292,7 +292,7 @@
     left = jnp.stack([piece[0] for piece in pieces])
     right = jnp.stack([piece[1] for piece in pieces])
     left_s, right_s = swap(left), swap(right)
-    amps = lax.all_gather(gate([amps], [left_s, right_s])[0], ("zh", "zl", "c"), axis=0)
+    amps = lax.all_gather(gate([amps], [left_s, right_s], 58 * 2**20)[0], ("zh", "zl", "c"), axis=0)
     left_1, right_1 = onward(left, "x"), onward(right, "y")
     left_1s, right_1s = onward(left_s, "x"), onward(right_s, "y")
     right_1p = swap(right_1)

time: 164 us -> 163 us (level)
    unnamed x42 -> x40, local copies, waits for them, and re-layouts: 11.6 us -> 10.2 us
  transfers between devices with their start and end apart: 17 -> 17, of which waited for: 9 -> 8; matrix products, arithmetic and copies ran while one was open for 4% -> 5% of each run, Pallas kernels for 15% -> 15%
where the time goes in v5:
time: 163 us; the launch traced here: 162 us
  Pallas kernels  48.1 us (30%)
  waiting for transfers between devices  36.3 us (22%)
  starting transfers between devices  30.6 us (19%)
  local copies, waits for them, and re-layouts  16.3 us (10%)
  between operations  15 us (9%)
  blocking collectives  10.8 us (7%)
  other arithmetic  4.25 us (3%)
    pallas_call x2, Pallas kernels, integrals(): pl.pallas_call(kernel, out_shape=jax.ShapeDtypeStruct((W, rows, W), jnp.b...  25 us
    pallas_call x1, Pallas kernels, far_ladder(): pl.pallas_call(far_kernel, out_shape=jax.ShapeDtypeStruct((2, 16, 16, 256...  23.1 us
    ppermute x3, waiting for transfers between devices, shift(): return lax.ppermute(value, axis, [(i, (i + step) % 4) for i in range(4)])  14.4 us
    ppermute x6, waiting for transfers between devices, onward(): return lax.ppermute(value, (axis, 'c'), pairs)  10.9 us
    all_gather x1, blocking collectives, shards(): amps = lax.all_gather(jnp.transpose(amplitudes, (1, 0, 2)), 'x', axis=0)  10.8 us
    unnamed x40, local copies, waits for them, and re-layouts  10.2 us
    ppermute x6, starting transfers between devices, onward(): return lax.ppermute(value, (axis, 'c'), pairs)  9.27 us
    ppermute x5, starting transfers between devices, swap(): return lax.ppermute(value, 'c', [(0, 1), (1, 0)])  7.65 us
  transfers between devices with their start and end apart: 17, of which 8 were waited for; matrix products, arithmetic and copies ran while one was open for 5% of the time, Pallas kernels for 15%

profile of v5, /device:TPU:1, one launch (start us, length us, event | category | flops | bytes accessed | tf_op | source)
XLA Modules:
  0.0 162.1 jit_solution(5806826940700674133)
XLA Ops:
  6.5 1.9 %fusion.5 = bf16[2,5120,128]{2,1,0:T(8,128)(2,1)S(1)} fusion(bf16[1,5000,128]{2,1,0:T(8,128)(2,1)} %bitcast.62, bf16[1,5000,128]{2,1,0:T(8,128)(2,1)} %bitcast.63), kind=kLoop, calls=%fused_computation.6 | loop fusion | flops 9175040 | bytes 5181440 | tf_op jit(solution)/shard_map/stack | solution.py:283
  9.7 2.5 %collective-permute-start = (bf16[2,128,1280]{2,1,0:T(8,128)(2,1)}, bf16[2,128,1280]{2,1,0:T(8,128)(2,1)S(1)}, u32[]{:S(2)}, u32[]{:S(2)}) collective-permute-start(bf16[2,128,1280]{2,1,0:T(8,128)(2,1)} %bitcast.19), channel_id=1, source_target_pairs={{0,2},{2,16},{16,18},{18,0},{1,3},{3,17},{17,19},{19,1},{4,6},{6,2... | collective-permute-start | bytes 1966088 | tf_op jit(solution)/shard_map/ppermute | solution.py:249
  13.3 2.1 %collective-permute-start.1 = (bf16[2,128,1280]{2,1,0:T(8,128)(2,1)}, bf16[2,128,1280]{2,1,0:T(8,128)(2,1)S(1)}, u32[]{:S(2)}, u32[]{:S(2)}) collective-permute-start(bf16[2,128,1280]{2,1,0:T(8,128)(2,1)} %bitcast.21), channel_id=1, source_target_pairs={{0,18},{2,0},{16,2},{18,16},{1,19},{3,1},{17,3},{19,17},{4,22},{6,... | collective-permute-start | bytes 1966088 | tf_op jit(solution)/shard_map/ppermute | solution.py:249
  15.5 10.8 %all-gather = bf16[64,16,128]{2,0,1:T(8,128)(2,1)S(1)} all-gather(bf16[16,16,128]{2,0,1:T(8,128)(2,1)S(1)} %bitcast.68), channel_id=2, replica_groups=mesh['y'=4,'zh'=2,'x'=4,'zl'=2,'c'=2] {'x'}, dimensions={0}, use_global_device_ids=true | all-gather | bytes 327680 | tf_op jit(solution)/shard_map/all_gather | solution.py:288
  29.2 2.9 %collective-permute-start.2 = (bf16[2,128,1280]{2,1,0:T(8,128)(2,1)S(1)}, bf16[2,128,1280]{2,1,0:T(8,128)(2,1)S(1)}, u32[]{:S(2)}, u32[]{:S(2)}) collective-permute-start(bf16[2,128,1280]{2,1,0:T(8,128)(2,1)S(1)} %gate.4), channel_id=1, source_target_pairs={{0,16},{2,18},{16,0},{18,2},{1,17},{3,19},{17,1},{19,3},{4,20},{6,... | collective-permute-start | bytes 1966088 | tf_op jit(solution)/shard_map/ppermute | solution.py:249
  32.2 13.0 %collective-permute-done.2 = bf16[2,128,1280]{2,1,0:T(8,128)(2,1)S(1)} collective-permute-done((bf16[2,128,1280]{2,1,0:T(8,128)(2,1)S(1)}, bf16[2,128,1280]{2,1,0:T(8,128)(2,1)S(1)}, u32[]{:S(2)}, u32[]{:S(2)}) %collective-permute-start.2) | collective-permute-done | bytes 655392 | tf_op jit(solution)/shard_map/ppermute | solution.py:249
  45.5 2.7 %collective-permute-start.4 = (bf16[4,128,1280]{2,1,0:T(8,128)(2,1)S(1)}, bf16[4,128,1280]{2,1,0:T(8,128)(2,1)S(1)}, u32[]{:S(2)}, u32[]{:S(2)}) collective-permute-start(bf16[4,128,1280]{2,1,0:T(8,128)(2,1)S(1)} %pad_maximum_fusion.1.refs_0_), channel_id=1, source_target_pairs={{0,1},{1,0},{2,3},{3,2},{4,5},{5,4},{6,7},{7,6},{8,9},{9,8},{10,11... | collective-permute-start | bytes 3932168 | tf_op jit(solution)/shard_map/ppermute | solution.py:245
  49.6 2.8 %all-gather.6.cloned.1.call-done = bf16[16,16,16,128]{3,2,1,0:T(8,128)(2,1)} async-done(((bf16[4,16,16,128]{3,2,1,0:T(8,128)(2,1)}), bf16[16,16,16,128]{3,2,1,0:T(8,128)(2,1)}) %all-gather.6.cloned.1.call-update) | async-done | bytes 1048592 | tf_op jit(solution)/shard_map/all_gather | solution.py:291
  53.5 2.4 %collective-permute-start.5 = (bf16[4,128,1280]{2,1,0:T(8,128)(2,1)S(1)}, bf16[4,128,1280]{2,1,0:T(8,128)(2,1)}, u32[]{:S(2)}, u32[]{:S(2)}) collective-permute-start(bf16[4,128,1280]{2,1,0:T(8,128)(2,1)S(1)} %pad_maximum_fusion.1.refs_0_), channel_id=1, source_target_pairs={{0,32},{1,97},{32,64},{33,1},{64,96},{65,33},{96,0},{97,65},{2,34}... | collective-permute-start | bytes 3932168 | tf_op jit(solution)/shard_map/ppermute | solution.py:254
  55.9 2.5 %collective-permute-start.3 = (bf16[4,128,1280]{2,1,0:T(8,128)(2,1)}, bf16[4,128,1280]{2,1,0:T(8,128)(2,1)}, u32[]{:S(2)}, u32[]{:S(2)}) collective-permute-start(bf16[4,128,1280]{2,1,0:T(8,128)(2,1)} %pad_maximum_fusion.l0), channel_id=1, source_target_pairs={{0,4},{1,13},{4,8},{5,1},{8,12},{9,5},{12,0},{13,9},{2,6},{3,15},{... | collective-permute-start | bytes 3932168 | tf_op jit(solution)/shard_map/ppermute | solution.py:254
  59.6 10.9 %collective-permute-done.5.refs_2_ = bf16[4,128,1280]{2,1,0:T(8,128)(2,1)} collective-permute-done((bf16[4,128,1280]{2,1,0:T(8,128)(2,1)S(1)}, bf16[4,128,1280]{2,1,0:T(8,128)(2,1)}, u32[]{:S(2)}, u32[]{:S(2)}) %collective-permute-start.5) | collective-permute-done | bytes 1310752 | tf_op jit(solution)/shard_map/ppermute | solution.py:254
  70.5 3.6 %collective-permute-start.9 = (bf16[4,128,1280]{2,1,0:T(8,128)(2,1)}, bf16[4,128,1280]{2,1,0:T(8,128)(2,1)S(1)}, u32[]{:S(2)}, u32[]{:S(2)}) collective-permute-start(bf16[4,128,1280]{2,1,0:T(8,128)(2,1)} %collective-permute-done.5.refs_2_), channel_id=1, source_target_pairs={{0,1},{1,0},{2,3},{3,2},{4,5},{5,4},{6,7},{7,6},{8,9},{9,8},{10,11... | collective-permute-start | bytes 3932168 | tf_op jit(solution)/shard_map/ppermute | solution.py:245
  74.1 1.3 copy-done.4
  75.4 1.3 copy-done.7
  76.8 8.6 %integrals2.1.refs_1_.x1 = bf16[128,96,128]{2,1,0:T(8,128)(2,1)S(1)} custom-call(s32[16]{0:T(128)S(1)} %stack.58.place, bf16[4,128,1280]{2,1,0:T(8,128)(2,1)} %pad_maximum_fusion.l0, bf16[4,128,1280]{2,1,0:T(8,128)(2,1)} %collective-permute-done.3.l1, bf16[4,128,1280]{2,1,0:T(8,128)(2,1)S(1)} %copy-done.7, bf16[4,128,1280]{2,1,0:T(8,128)(2,1)S(1)} %copy-done.4, ...), custom_call_target="tpu_custom_call" | custom-call | flops 1000000 | bytes 10000 | tf_op jit(solution)/shard_map/integrals2/pallas_call | solution.py:127
  85.4 1.6 copy-done.2
  88.2 2.0 %collective-permute-start.12 = (bf16[4,128,1280]{2,1,0:T(8,128)(2,1)}, bf16[4,128,1280]{2,1,0:T(8,128)(2,1)S(1)}, u32[]{:S(2)}, u32[]{:S(2)}) collective-permute-start(bf16[4,128,1280]{2,1,0:T(8,128)(2,1)} %collective-permute-done.5.refs_2_), channel_id=1, source_target_pairs={{0,32},{1,97},{32,64},{33,1},{64,96},{65,33},{96,0},{97,65},{2,34}... | collective-permute-start | bytes 3932168 | tf_op jit(solution)/shard_map/ppermute | solution.py:254
  90.2 1.3 collective-permute-start.11
  91.6 16.5 %integrals3.1.refs_1_.x2 = bf16[128,192,128]{2,1,0:T(8,128)(2,1)S(1)} custom-call(s32[16]{0:T(128)S(1)} %stack.58.place, bf16[4,128,1280]{2,1,0:T(8,128)(2,1)} %pad_maximum_fusion.l0, bf16[4,128,1280]{2,1,0:T(8,128)(2,1)} %collective-permute-done.3.l1, bf16[4,128,1280]{2,1,0:T(8,128)(2,1)S(1)} %collective-permute-done.7.l2, ...), custom_call_target="tpu_custom_call" | custom-call | flops 1000000 | bytes 10000 | tf_op jit(solution)/shard_map/integrals3/pallas_call | solution.py:127
  108.1 2.7 %copy-done.1 = bf16[128,192,128]{2,1,0:T(8,128)(2,1)} copy-done((bf16[128,192,128]{2,1,0:T(8,128)(2,1)}, bf16[128,192,128]{2,1,0:T(8,128)(2,1)S(1)}, u32[]{:S(2)}) %copy-start.1) | copy-done | bytes 6291480
  111.8 2.1 %collective-permute-done.13.refs_7_ = bf16[4,128,1280]{2,1,0:T(8,128)(2,1)} collective-permute-done((bf16[4,128,1280]{2,1,0:T(8,128)(2,1)S(1)}, bf16[4,128,1280]{2,1,0:T(8,128)(2,1)}, u32[]{:S(2)}, u32[]{:S(2)}) %collective-permute-start.13) | collective-permute-done | bytes 1310752 | tf_op jit(solution)/shard_map/ppermute | solution.py:245
  114.0 23.1 %far_ladder.1 = bf16[2,16,16,256]{3,2,1,0:T(8,128)(2,1)} custom-call(s32[16]{0:T(128)} %copy-done.13, bf16[128,96,128]{2,1,0:T(8,128)(2,1)} %copy-done.2, bf16[128,192,128]{2,1,0:T(8,128)(2,1)} %copy-done.1, bf16[4,128,1280]{2,1,0:T(8,128)(2,1)} %pad_maximum_fusion.l0, bf16[4,128,1280]{2,1,0:T(8,128)(2,1)} %collective-permute-done.3.l1, ...), custom_call_target="tpu_custom_call" | custom-call | flops 15000000512 | bytes 10000000 | tf_op jit(solution)/shard_map/far_ladder/pallas_call | solution.py:223
  137.1 6.1 %all-to-all-start = ((bf16[32,16,256]{2,1,0:T(8,128)(2,1)}), bf16[32,16,256]{2,1,0:T(8,128)(2,1)S(1)}, u32[]{:S(2)}, u32[]{:S(2)}) async-start(bf16[32,16,256]{2,1,0:T(8,128)(2,1)} %bitcast.65), calls=%async_computation | async-start | bytes 524288 | tf_op jit(solution)/shard_map/all_to_all | solution.py:310
  146.7 5.3 %all-to-all-done = bf16[32,16,256]{2,1,0:T(8,128)(2,1)S(1)} async-done(((bf16[32,16,256]{2,1,0:T(8,128)(2,1)}), bf16[32,16,256]{2,1,0:T(8,128)(2,1)S(1)}, u32[]{:S(2)}, u32[]{:S(2)}) %all-to-all-start) | async-done | bytes 262176 | tf_op jit(solution)/shard_map/all_to_all | solution.py:310
  (82 shorter events, 17.0 us)
Async XLA Ops:
  6.5 104.3 %copy-start = (s32[256,2]{0,1:T(2,128)S(1)}, s32[256,2]{0,1:T(2,128)}, u32[]{:S(2)}) copy-start(s32[256,2]{0,1:T(2,128)} %param.13) | copy-start | bytes 6148
  6.5 45.9 %all-gather.6.cloned.1.call-start = ((), (), s32[]{:S(2)}) async-start(), calls=%async_computation.1 | async-start | bytes 1310720 | tf_op jit(solution)/shard_map/all_gather | solution.py:291
  9.7 19.3 %collective-permute-start = (bf16[2,128,1280]{2,1,0:T(8,128)(2,1)}, bf16[2,128,1280]{2,1,0:T(8,128)(2,1)S(1)}, u32[]{:S(2)}, u32[]{:S(2)}) collective-permute-start(bf16[2,128,1280]{2,1,0:T(8,128)(2,1)} %bitcast.19), channel_id=1, source_target_pairs={{0,2},{2,16},{16,18},{18,0},{1,3},{3,17},{17,19},{19,1},{4,6},{6,2... | collective-permute-start | bytes 1966088 | tf_op jit(solution)/shard_map/ppermute | solution.py:249
  13.3 15.9 %collective-permute-start.1 = (bf16[2,128,1280]{2,1,0:T(8,128)(2,1)}, bf16[2,128,1280]{2,1,0:T(8,128)(2,1)S(1)}, u32[]{:S(2)}, u32[]{:S(2)}) collective-permute-start(bf16[2,128,1280]{2,1,0:T(8,128)(2,1)} %bitcast.21), channel_id=1, source_target_pairs={{0,18},{2,0},{16,2},{18,16},{1,19},{3,1},{17,3},{19,17},{4,22},{6,... | collective-permute-start | bytes 1966088 | tf_op jit(solution)/shard_map/ppermute | solution.py:249
  27.2 86.8 %all-gather.8.cloned.1.call-start = ((), (), s32[]{:S(2)}) async-start(), calls=%async_computation.2 | async-start | bytes 9437184 | tf_op jit(solution)/shard_map/all_gather | solution.py:295
  29.2 16.1 %collective-permute-start.2 = (bf16[2,128,1280]{2,1,0:T(8,128)(2,1)S(1)}, bf16[2,128,1280]{2,1,0:T(8,128)(2,1)S(1)}, u32[]{:S(2)}, u32[]{:S(2)}) collective-permute-start(bf16[2,128,1280]{2,1,0:T(8,128)(2,1)S(1)} %gate.4), channel_id=1, source_target_pairs={{0,16},{2,18},{16,0},{18,2},{1,17},{3,19},{17,1},{19,3},{4,20},{6,... | collective-permute-start | bytes 1966088 | tf_op jit(solution)/shard_map/ppermute | solution.py:249
  45.5 8.0 %copy-start.6 = (bf16[4,128,1280]{2,1,0:T(8,128)(2,1)}, bf16[4,128,1280]{2,1,0:T(8,128)(2,1)S(1)}, u32[]{:S(2)}) copy-start(bf16[4,128,1280]{2,1,0:T(8,128)(2,1)S(1)} %pad_maximum_fusion.1.refs_0_) | copy-start | bytes 3932164
  45.5 6.9 %collective-permute-start.4 = (bf16[4,128,1280]{2,1,0:T(8,128)(2,1)S(1)}, bf16[4,128,1280]{2,1,0:T(8,128)(2,1)S(1)}, u32[]{:S(2)}, u32[]{:S(2)}) collective-permute-start(bf16[4,128,1280]{2,1,0:T(8,128)(2,1)S(1)} %pad_maximum_fusion.1.refs_0_), channel_id=1, source_target_pairs={{0,1},{1,0},{2,3},{3,2},{4,5},{5,4},{6,7},{7,6},{8,9},{9,8},{10,11... | collective-permute-start | bytes 3932168 | tf_op jit(solution)/shard_map/ppermute | solution.py:245
  49.4 3.7 %collective-permute-start.6 = (bf16[4,128,1280]{2,1,0:T(8,128)(2,1)}, bf16[4,128,1280]{2,1,0:T(8,128)(2,1)}, u32[]{:S(2)}, u32[]{:S(2)}) collective-permute-start(bf16[4,128,1280]{2,1,0:T(8,128)(2,1)} %pad_maximum_fusion.l0), channel_id=1, source_target_pairs={{0,1},{1,0},{2,3},{3,2},{4,5},{5,4},{6,7},{7,6},{8,9},{9,8},{10,11... | collective-permute-start | bytes 3932168 | tf_op jit(solution)/shard_map/ppermute | solution.py:245
  53.5 16.9 %collective-permute-start.5 = (bf16[4,128,1280]{2,1,0:T(8,128)(2,1)S(1)}, bf16[4,128,1280]{2,1,0:T(8,128)(2,1)}, u32[]{:S(2)}, u32[]{:S(2)}) collective-permute-start(bf16[4,128,1280]{2,1,0:T(8,128)(2,1)S(1)} %pad_maximum_fusion.1.refs_0_), channel_id=1, source_target_pairs={{0,32},{1,97},{32,64},{33,1},{64,96},{65,33},{96,0},{97,65},{2,34}... | collective-permute-start | bytes 3932168 | tf_op jit(solution)/shard_map/ppermute | solution.py:254
  55.9 18.2 %collective-permute-start.3 = (bf16[4,128,1280]{2,1,0:T(8,128)(2,1)}, bf16[4,128,1280]{2,1,0:T(8,128)(2,1)}, u32[]{:S(2)}, u32[]{:S(2)}) collective-permute-start(bf16[4,128,1280]{2,1,0:T(8,128)(2,1)} %pad_maximum_fusion.l0), channel_id=1, source_target_pairs={{0,4},{1,13},{4,8},{5,1},{8,12},{9,5},{12,0},{13,9},{2,6},{3,15},{... | collective-permute-start | bytes 3932168 | tf_op jit(solution)/shard_map/ppermute | solution.py:254
  58.4 27.0 %collective-permute-start.8 = (bf16[4,128,1280]{2,1,0:T(8,128)(2,1)}, bf16[4,128,1280]{2,1,0:T(8,128)(2,1)}, u32[]{:S(2)}, u32[]{:S(2)}) collective-permute-start(bf16[4,128,1280]{2,1,0:T(8,128)(2,1)} %copy-done.3), channel_id=1, source_target_pairs={{0,32},{1,97},{32,64},{33,1},{64,96},{65,33},{96,0},{97,65},{2,34}... | collective-permute-start | bytes 3932168 | tf_op jit(solution)/shard_map/ppermute | solution.py:254
  58.9 32.6 %copy-start.13 = (s32[16]{0:T(128)}, s32[16]{0:T(128)S(1)}, u32[]{:S(2)}) copy-start(s32[16]{0:T(128)S(1)} %stack.58.place) | copy-start | bytes 196
  58.9 32.6 %collective-permute-start.7 = (bf16[4,128,1280]{2,1,0:T(8,128)(2,1)}, bf16[4,128,1280]{2,1,0:T(8,128)(2,1)S(1)}, u32[]{:S(2)}, u32[]{:S(2)}) collective-permute-start(bf16[4,128,1280]{2,1,0:T(8,128)(2,1)} %collective-permute-done.6.refs_1_), channel_id=1, source_target_pairs={{0,4},{1,13},{4,8},{5,1},{8,12},{9,5},{12,0},{13,9},{2,6},{3,15},{... | collective-permute-start | bytes 3932168 | tf_op jit(solution)/shard_map/ppermute | solution.py:254
  70.5 21.0 %collective-permute-start.9 = (bf16[4,128,1280]{2,1,0:T(8,128)(2,1)}, bf16[4,128,1280]{2,1,0:T(8,128)(2,1)S(1)}, u32[]{:S(2)}, u32[]{:S(2)}) collective-permute-start(bf16[4,128,1280]{2,1,0:T(8,128)(2,1)} %collective-permute-done.5.refs_2_), channel_id=1, source_target_pairs={{0,1},{1,0},{2,3},{3,2},{4,5},{5,4},{6,7},{7,6},{8,9},{9,8},{10,11... | collective-permute-start | bytes 3932168 | tf_op jit(solution)/shard_map/ppermute | solution.py:245
  87.0 4.5 %collective-permute-start.10 = (bf16[4,128,1280]{2,1,0:T(8,128)(2,1)}, bf16[4,128,1280]{2,1,0:T(8,128)(2,1)S(1)}, u32[]{:S(2)}, u32[]{:S(2)}) collective-permute-start(bf16[4,128,1280]{2,1,0:T(8,128)(2,1)} %gate.5.refs_3_), channel_id=1, source_target_pairs={{0,1},{1,0},{2,3},{3,2},{4,5},{5,4},{6,7},{7,6},{8,9},{9,8},{10,11... | collective-permute-start | bytes 3932168 | tf_op jit(solution)/shard_map/ppermute | solution.py:245
  88.2 19.9 %collective-permute-start.12 = (bf16[4,128,1280]{2,1,0:T(8,128)(2,1)}, bf16[4,128,1280]{2,1,0:T(8,128)(2,1)S(1)}, u32[]{:S(2)}, u32[]{:S(2)}) collective-permute-start(bf16[4,128,1280]{2,1,0:T(8,128)(2,1)} %collective-permute-done.5.refs_2_), channel_id=1, source_target_pairs={{0,32},{1,97},{32,64},{33,1},{64,96},{65,33},{96,0},{97,65},{2,34}... | collective-permute-start | bytes 3932168 | tf_op jit(solution)/shard_map/ppermute | solution.py:254
  90.2 21.7 %collective-permute-start.11 = (bf16[4,128,1280]{2,1,0:T(8,128)(2,1)}, bf16[4,128,1280]{2,1,0:T(8,128)(2,1)S(1)}, u32[]{:S(2)}, u32[]{:S(2)}) collective-permute-start(bf16[4,128,1280]{2,1,0:T(8,128)(2,1)} %collective-permute-done.3.l1), channel_id=1, source_target_pairs={{0,4},{1,13},{4,8},{5,1},{8,12},{9,5},{12,0},{13,9},{2,6},{3,15},{... | collective-permute-start | bytes 3932168 | tf_op jit(solution)/shard_map/ppermute | solution.py:254
  91.5 16.5 %copy-start.11 = (bf16[4,128,1280]{2,1,0:T(8,128)(2,1)}, bf16[4,128,1280]{2,1,0:T(8,128)(2,1)S(1)}, u32[]{:S(2)}) copy-start(bf16[4,128,1280]{2,1,0:T(8,128)(2,1)S(1)} %collective-permute-done.9.refs_4_) | copy-start | bytes 3932164
  91.5 16.5 %copy-start.10 = (bf16[4,128,1280]{2,1,0:T(8,128)(2,1)}, bf16[4,128,1280]{2,1,0:T(8,128)(2,1)S(1)}, u32[]{:S(2)}) copy-start(bf16[4,128,1280]{2,1,0:T(8,128)(2,1)S(1)} %collective-permute-done.7.l2) | copy-start | bytes 3932164
  91.6 16.5 %copy-start.12 = (bf16[4,128,1280]{2,1,0:T(8,128)(2,1)}, bf16[4,128,1280]{2,1,0:T(8,128)(2,1)S(1)}, u32[]{:S(2)}) copy-start(bf16[4,128,1280]{2,1,0:T(8,128)(2,1)S(1)} %collective-permute-done.10.refs_5_) | copy-start | bytes 3932164
  110.8 3.2 %collective-permute-start.13 = (bf16[4,128,1280]{2,1,0:T(8,128)(2,1)S(1)}, bf16[4,128,1280]{2,1,0:T(8,128)(2,1)}, u32[]{:S(2)}, u32[]{:S(2)}) collective-permute-start(bf16[4,128,1280]{2,1,0:T(8,128)(2,1)S(1)} %gate.7.refs_6_), channel_id=1, source_target_pairs={{0,1},{1,0},{2,3},{3,2},{4,5},{5,4},{6,7},{7,6},{8,9},{9,8},{10,11... | collective-permute-start | bytes 3932168 | tf_op jit(solution)/shard_map/ppermute | solution.py:245
  114.0 29.2 %copy-start.15 = (s32[2]{0:T(128)S(1)}, s32[2]{0:T(128)}, u32[]{:S(2)}) copy-start(s32[2]{0:T(128)} %param.14) | copy-start | bytes 28
  137.1 15.0 %all-to-all-start = ((bf16[32,16,256]{2,1,0:T(8,128)(2,1)}), bf16[32,16,256]{2,1,0:T(8,128)(2,1)S(1)}, u32[]{:S(2)}, u32[]{:S(2)}) async-start(bf16[32,16,256]{2,1,0:T(8,128)(2,1)} %bitcast.65), calls=%async_computation | async-start | bytes 524288 | tf_op jit(solution)/shard_map/all_to_all | solution.py:310
  (11 other events, 36.2 us)
Sparse Core Ops, SparseCore 0:
  27.3 25.0 all-gather.5
  54.1 51.5 all-gather.7

commit v6 on v5

--- a/solution.py
+++ b/solution.py
@@ -73,7 +73,7 @@
             xbuf[c] = scr[pl.ds(start, rows), :].astype(jnp.bfloat16)
             return carry
 
-        lax.fori_loop(k * quarter, (k + 1) * quarter, convert, 0, unroll=8)
+        lax.fori_loop(k * quarter, (k + 1) * quarter, convert, 0, unroll=16)
         stores[k].start()
     for store in stores:
         store.wait()

time: 163 us -> 163 us (level)
  no operation moved by 1% of the time
where the time goes in v6:
time: 163 us; the launch traced here: 162 us
  Pallas kernels  48.1 us (30%)
  waiting for transfers between devices  36.2 us (22%)
  starting transfers between devices  30.6 us (19%)
  local copies, waits for them, and re-layouts  16.3 us (10%)
  between operations  15 us (9%)
  blocking collectives  10.8 us (7%)
  other arithmetic  4.25 us (3%)
    pallas_call x2, Pallas kernels, integrals(): pl.pallas_call(kernel, out_shape=jax.ShapeDtypeStruct((W, rows, W), jnp.b...  25 us
    pallas_call x1, Pallas kernels, far_ladder(): pl.pallas_call(far_kernel, out_shape=jax.ShapeDtypeStruct((2, 16, 16, 256...  23.1 us
    ppermute x3, waiting for transfers between devices, shift(): return lax.ppermute(value, axis, [(i, (i + step) % 4) for i in range(4)])  14.4 us
    ppermute x6, waiting for transfers between devices, onward(): return lax.ppermute(value, (axis, 'c'), pairs)  10.9 us
    all_gather x1, blocking collectives, shards(): amps = lax.all_gather(jnp.transpose(amplitudes, (1, 0, 2)), 'x', axis=0)  10.8 us
    unnamed x40, local copies, waits for them, and re-layouts  10.2 us
    ppermute x6, starting transfers between devices, onward(): return lax.ppermute(value, (axis, 'c'), pairs)  9.24 us
    ppermute x5, starting transfers between devices, swap(): return lax.ppermute(value, 'c', [(0, 1), (1, 0)])  7.68 us
  transfers between devices with their start and end apart: 17, of which 8 were waited for; matrix products, arithmetic and copies ran while one was open for 5% of the time, Pallas kernels for 15%

profile of v6, /device:TPU:1, one launch (start us, length us, event | category | flops | bytes accessed | tf_op | source)
XLA Modules:
  0.0 162.0 jit_solution(1966055899391507725)
XLA Ops:
  6.5 1.9 %fusion.5 = bf16[2,5120,128]{2,1,0:T(8,128)(2,1)S(1)} fusion(bf16[1,5000,128]{2,1,0:T(8,128)(2,1)} %bitcast.62, bf16[1,5000,128]{2,1,0:T(8,128)(2,1)} %bitcast.63), kind=kLoop, calls=%fused_computation.6 | loop fusion | flops 9175040 | bytes 5181440 | tf_op jit(solution)/shard_map/stack | solution.py:283
  9.7 2.5 %collective-permute-start = (bf16[2,128,1280]{2,1,0:T(8,128)(2,1)}, bf16[2,128,1280]{2,1,0:T(8,128)(2,1)S(1)}, u32[]{:S(2)}, u32[]{:S(2)}) collective-permute-start(bf16[2,128,1280]{2,1,0:T(8,128)(2,1)} %bitcast.19), channel_id=1, source_target_pairs={{0,2},{2,16},{16,18},{18,0},{1,3},{3,17},{17,19},{19,1},{4,6},{6,2... | collective-permute-start | bytes 1966088 | tf_op jit(solution)/shard_map/ppermute | solution.py:249
  13.3 2.1 %collective-permute-start.1 = (bf16[2,128,1280]{2,1,0:T(8,128)(2,1)}, bf16[2,128,1280]{2,1,0:T(8,128)(2,1)S(1)}, u32[]{:S(2)}, u32[]{:S(2)}) collective-permute-start(bf16[2,128,1280]{2,1,0:T(8,128)(2,1)} %bitcast.21), channel_id=1, source_target_pairs={{0,18},{2,0},{16,2},{18,16},{1,19},{3,1},{17,3},{19,17},{4,22},{6,... | collective-permute-start | bytes 1966088 | tf_op jit(solution)/shard_map/ppermute | solution.py:249
  15.5 10.8 %all-gather = bf16[64,16,128]{2,0,1:T(8,128)(2,1)S(1)} all-gather(bf16[16,16,128]{2,0,1:T(8,128)(2,1)S(1)} %bitcast.68), channel_id=2, replica_groups=mesh['y'=4,'zh'=2,'x'=4,'zl'=2,'c'=2] {'x'}, dimensions={0}, use_global_device_ids=true | all-gather | bytes 327680 | tf_op jit(solution)/shard_map/all_gather | solution.py:288
  29.2 2.9 %collective-permute-start.2 = (bf16[2,128,1280]{2,1,0:T(8,128)(2,1)S(1)}, bf16[2,128,1280]{2,1,0:T(8,128)(2,1)S(1)}, u32[]{:S(2)}, u32[]{:S(2)}) collective-permute-start(bf16[2,128,1280]{2,1,0:T(8,128)(2,1)S(1)} %gate.4), channel_id=1, source_target_pairs={{0,16},{2,18},{16,0},{18,2},{1,17},{3,19},{17,1},{19,3},{4,20},{6,... | collective-permute-start | bytes 1966088 | tf_op jit(solution)/shard_map/ppermute | solution.py:249
  32.2 13.0 %collective-permute-done.2 = bf16[2,128,1280]{2,1,0:T(8,128)(2,1)S(1)} collective-permute-done((bf16[2,128,1280]{2,1,0:T(8,128)(2,1)S(1)}, bf16[2,128,1280]{2,1,0:T(8,128)(2,1)S(1)}, u32[]{:S(2)}, u32[]{:S(2)}) %collective-permute-start.2) | collective-permute-done | bytes 655392 | tf_op jit(solution)/shard_map/ppermute | solution.py:249
  45.5 2.7 %collective-permute-start.4 = (bf16[4,128,1280]{2,1,0:T(8,128)(2,1)S(1)}, bf16[4,128,1280]{2,1,0:T(8,128)(2,1)S(1)}, u32[]{:S(2)}, u32[]{:S(2)}) collective-permute-start(bf16[4,128,1280]{2,1,0:T(8,128)(2,1)S(1)} %pad_maximum_fusion.1.refs_0_), channel_id=1, source_target_pairs={{0,1},{1,0},{2,3},{3,2},{4,5},{5,4},{6,7},{7,6},{8,9},{9,8},{10,11... | collective-permute-start | bytes 3932168 | tf_op jit(solution)/shard_map/ppermute | solution.py:245
  49.6 2.8 %all-gather.6.cloned.1.call-done = bf16[16,16,16,128]{3,2,1,0:T(8,128)(2,1)} async-done(((bf16[4,16,16,128]{3,2,1,0:T(8,128)(2,1)}), bf16[16,16,16,128]{3,2,1,0:T(8,128)(2,1)}) %all-gather.6.cloned.1.call-update) | async-done | bytes 1048592 | tf_op jit(solution)/shard_map/all_gather | solution.py:291
  53.5 2.4 %collective-permute-start.5 = (bf16[4,128,1280]{2,1,0:T(8,128)(2,1)S(1)}, bf16[4,128,1280]{2,1,0:T(8,128)(2,1)}, u32[]{:S(2)}, u32[]{:S(2)}) collective-permute-start(bf16[4,128,1280]{2,1,0:T(8,128)(2,1)S(1)} %pad_maximum_fusion.1.refs_0_), channel_id=1, source_target_pairs={{0,32},{1,97},{32,64},{33,1},{64,96},{65,33},{96,0},{97,65},{2,34}... | collective-permute-start | bytes 3932168 | tf_op jit(solution)/shard_map/ppermute | solution.py:254
  55.9 2.5 %collective-permute-start.3 = (bf16[4,128,1280]{2,1,0:T(8,128)(2,1)}, bf16[4,128,1280]{2,1,0:T(8,128)(2,1)}, u32[]{:S(2)}, u32[]{:S(2)}) collective-permute-start(bf16[4,128,1280]{2,1,0:T(8,128)(2,1)} %pad_maximum_fusion.l0), channel_id=1, source_target_pairs={{0,4},{1,13},{4,8},{5,1},{8,12},{9,5},{12,0},{13,9},{2,6},{3,15},{... | collective-permute-start | bytes 3932168 | tf_op jit(solution)/shard_map/ppermute | solution.py:254
  59.6 10.9 %collective-permute-done.5.refs_2_ = bf16[4,128,1280]{2,1,0:T(8,128)(2,1)} collective-permute-done((bf16[4,128,1280]{2,1,0:T(8,128)(2,1)S(1)}, bf16[4,128,1280]{2,1,0:T(8,128)(2,1)}, u32[]{:S(2)}, u32[]{:S(2)}) %collective-permute-start.5) | collective-permute-done | bytes 1310752 | tf_op jit(solution)/shard_map/ppermute | solution.py:254
  70.5 3.6 %collective-permute-start.9 = (bf16[4,128,1280]{2,1,0:T(8,128)(2,1)}, bf16[4,128,1280]{2,1,0:T(8,128)(2,1)S(1)}, u32[]{:S(2)}, u32[]{:S(2)}) collective-permute-start(bf16[4,128,1280]{2,1,0:T(8,128)(2,1)} %collective-permute-done.5.refs_2_), channel_id=1, source_target_pairs={{0,1},{1,0},{2,3},{3,2},{4,5},{5,4},{6,7},{7,6},{8,9},{9,8},{10,11... | collective-permute-start | bytes 3932168 | tf_op jit(solution)/shard_map/ppermute | solution.py:245
  74.1 1.3 copy-done.4
  75.4 1.3 copy-done.7
  76.8 8.5 %integrals2.1.refs_1_.x1 = bf16[128,96,128]{2,1,0:T(8,128)(2,1)S(1)} custom-call(s32[16]{0:T(128)S(1)} %stack.58.place, bf16[4,128,1280]{2,1,0:T(8,128)(2,1)} %pad_maximum_fusion.l0, bf16[4,128,1280]{2,1,0:T(8,128)(2,1)} %collective-permute-done.3.l1, bf16[4,128,1280]{2,1,0:T(8,128)(2,1)S(1)} %copy-done.7, bf16[4,128,1280]{2,1,0:T(8,128)(2,1)S(1)} %copy-done.4, ...), custom_call_target="tpu_custom_call" | custom-call | flops 1000000 | bytes 10000 | tf_op jit(solution)/shard_map/integrals2/pallas_call | solution.py:127
  85.4 1.6 copy-done.2
  88.2 2.0 %collective-permute-start.12 = (bf16[4,128,1280]{2,1,0:T(8,128)(2,1)}, bf16[4,128,1280]{2,1,0:T(8,128)(2,1)S(1)}, u32[]{:S(2)}, u32[]{:S(2)}) collective-permute-start(bf16[4,128,1280]{2,1,0:T(8,128)(2,1)} %collective-permute-done.5.refs_2_), channel_id=1, source_target_pairs={{0,32},{1,97},{32,64},{33,1},{64,96},{65,33},{96,0},{97,65},{2,34}... | collective-permute-start | bytes 3932168 | tf_op jit(solution)/shard_map/ppermute | solution.py:254
  90.1 1.3 collective-permute-start.11
  91.5 16.4 %integrals3.1.refs_1_.x2 = bf16[128,192,128]{2,1,0:T(8,128)(2,1)S(1)} custom-call(s32[16]{0:T(128)S(1)} %stack.58.place, bf16[4,128,1280]{2,1,0:T(8,128)(2,1)} %pad_maximum_fusion.l0, bf16[4,128,1280]{2,1,0:T(8,128)(2,1)} %collective-permute-done.3.l1, bf16[4,128,1280]{2,1,0:T(8,128)(2,1)S(1)} %collective-permute-done.7.l2, ...), custom_call_target="tpu_custom_call" | custom-call | flops 1000000 | bytes 10000 | tf_op jit(solution)/shard_map/integrals3/pallas_call | solution.py:127
  108.1 2.7 %copy-done.1 = bf16[128,192,128]{2,1,0:T(8,128)(2,1)} copy-done((bf16[128,192,128]{2,1,0:T(8,128)(2,1)}, bf16[128,192,128]{2,1,0:T(8,128)(2,1)S(1)}, u32[]{:S(2)}) %copy-start.1) | copy-done | bytes 6291480
  111.8 2.1 %collective-permute-done.13.refs_7_ = bf16[4,128,1280]{2,1,0:T(8,128)(2,1)} collective-permute-done((bf16[4,128,1280]{2,1,0:T(8,128)(2,1)S(1)}, bf16[4,128,1280]{2,1,0:T(8,128)(2,1)}, u32[]{:S(2)}, u32[]{:S(2)}) %collective-permute-start.13) | collective-permute-done | bytes 1310752 | tf_op jit(solution)/shard_map/ppermute | solution.py:245
  113.9 23.1 %far_ladder.1 = bf16[2,16,16,256]{3,2,1,0:T(8,128)(2,1)} custom-call(s32[16]{0:T(128)} %copy-done.13, bf16[128,96,128]{2,1,0:T(8,128)(2,1)} %copy-done.2, bf16[128,192,128]{2,1,0:T(8,128)(2,1)} %copy-done.1, bf16[4,128,1280]{2,1,0:T(8,128)(2,1)} %pad_maximum_fusion.l0, bf16[4,128,1280]{2,1,0:T(8,128)(2,1)} %collective-permute-done.3.l1, ...), custom_call_target="tpu_custom_call" | custom-call | flops 15000000512 | bytes 10000000 | tf_op jit(solution)/shard_map/far_ladder/pallas_call | solution.py:223
  137.0 6.1 %all-to-all-start = ((bf16[32,16,256]{2,1,0:T(8,128)(2,1)}), bf16[32,16,256]{2,1,0:T(8,128)(2,1)S(1)}, u32[]{:S(2)}, u32[]{:S(2)}) async-start(bf16[32,16,256]{2,1,0:T(8,128)(2,1)} %bitcast.65), calls=%async_computation | async-start | bytes 524288 | tf_op jit(solution)/shard_map/all_to_all | solution.py:310
  146.7 5.3 %all-to-all-done = bf16[32,16,256]{2,1,0:T(8,128)(2,1)S(1)} async-done(((bf16[32,16,256]{2,1,0:T(8,128)(2,1)}), bf16[32,16,256]{2,1,0:T(8,128)(2,1)S(1)}, u32[]{:S(2)}, u32[]{:S(2)}) %all-to-all-start) | async-done | bytes 262176 | tf_op jit(solution)/shard_map/all_to_all | solution.py:310
  (82 shorter events, 17.0 us)
Async XLA Ops:
  6.5 104.2 %copy-start = (s32[256,2]{0,1:T(2,128)S(1)}, s32[256,2]{0,1:T(2,128)}, u32[]{:S(2)}) copy-start(s32[256,2]{0,1:T(2,128)} %param.13) | copy-start | bytes 6148
  6.5 45.9 %all-gather.6.cloned.1.call-start = ((), (), s32[]{:S(2)}) async-start(), calls=%async_computation.1 | async-start | bytes 1310720 | tf_op jit(solution)/shard_map/all_gather | solution.py:291
  9.7 19.3 %collective-permute-start = (bf16[2,128,1280]{2,1,0:T(8,128)(2,1)}, bf16[2,128,1280]{2,1,0:T(8,128)(2,1)S(1)}, u32[]{:S(2)}, u32[]{:S(2)}) collective-permute-start(bf16[2,128,1280]{2,1,0:T(8,128)(2,1)} %bitcast.19), channel_id=1, source_target_pairs={{0,2},{2,16},{16,18},{18,0},{1,3},{3,17},{17,19},{19,1},{4,6},{6,2... | collective-permute-start | bytes 1966088 | tf_op jit(solution)/shard_map/ppermute | solution.py:249
  13.3 15.9 %collective-permute-start.1 = (bf16[2,128,1280]{2,1,0:T(8,128)(2,1)}, bf16[2,128,1280]{2,1,0:T(8,128)(2,1)S(1)}, u32[]{:S(2)}, u32[]{:S(2)}) collective-permute-start(bf16[2,128,1280]{2,1,0:T(8,128)(2,1)} %bitcast.21), channel_id=1, source_target_pairs={{0,18},{2,0},{16,2},{18,16},{1,19},{3,1},{17,3},{19,17},{4,22},{6,... | collective-permute-start | bytes 1966088 | tf_op jit(solution)/shard_map/ppermute | solution.py:249
  27.2 86.7 %all-gather.8.cloned.1.call-start = ((), (), s32[]{:S(2)}) async-start(), calls=%async_computation.2 | async-start | bytes 9437184 | tf_op jit(solution)/shard_map/all_gather | solution.py:295
  29.2 16.1 %collective-permute-start.2 = (bf16[2,128,1280]{2,1,0:T(8,128)(2,1)S(1)}, bf16[2,128,1280]{2,1,0:T(8,128)(2,1)S(1)}, u32[]{:S(2)}, u32[]{:S(2)}) collective-permute-start(bf16[2,128,1280]{2,1,0:T(8,128)(2,1)S(1)} %gate.4), channel_id=1, source_target_pairs={{0,16},{2,18},{16,0},{18,2},{1,17},{3,19},{17,1},{19,3},{4,20},{6,... | collective-permute-start | bytes 1966088 | tf_op jit(solution)/shard_map/ppermute | solution.py:249
  45.5 8.0 %copy-start.6 = (bf16[4,128,1280]{2,1,0:T(8,128)(2,1)}, bf16[4,128,1280]{2,1,0:T(8,128)(2,1)S(1)}, u32[]{:S(2)}) copy-start(bf16[4,128,1280]{2,1,0:T(8,128)(2,1)S(1)} %pad_maximum_fusion.1.refs_0_) | copy-start | bytes 3932164
  45.5 6.9 %collective-permute-start.4 = (bf16[4,128,1280]{2,1,0:T(8,128)(2,1)S(1)}, bf16[4,128,1280]{2,1,0:T(8,128)(2,1)S(1)}, u32[]{:S(2)}, u32[]{:S(2)}) collective-permute-start(bf16[4,128,1280]{2,1,0:T(8,128)(2,1)S(1)} %pad_maximum_fusion.1.refs_0_), channel_id=1, source_target_pairs={{0,1},{1,0},{2,3},{3,2},{4,5},{5,4},{6,7},{7,6},{8,9},{9,8},{10,11... | collective-permute-start | bytes 3932168 | tf_op jit(solution)/shard_map/ppermute | solution.py:245
  49.4 3.7 %collective-permute-start.6 = (bf16[4,128,1280]{2,1,0:T(8,128)(2,1)}, bf16[4,128,1280]{2,1,0:T(8,128)(2,1)}, u32[]{:S(2)}, u32[]{:S(2)}) collective-permute-start(bf16[4,128,1280]{2,1,0:T(8,128)(2,1)} %pad_maximum_fusion.l0), channel_id=1, source_target_pairs={{0,1},{1,0},{2,3},{3,2},{4,5},{5,4},{6,7},{7,6},{8,9},{9,8},{10,11... | collective-permute-start | bytes 3932168 | tf_op jit(solution)/shard_map/ppermute | solution.py:245
  53.5 16.9 %collective-permute-start.5 = (bf16[4,128,1280]{2,1,0:T(8,128)(2,1)S(1)}, bf16[4,128,1280]{2,1,0:T(8,128)(2,1)}, u32[]{:S(2)}, u32[]{:S(2)}) collective-permute-start(bf16[4,128,1280]{2,1,0:T(8,128)(2,1)S(1)} %pad_maximum_fusion.1.refs_0_), channel_id=1, source_target_pairs={{0,32},{1,97},{32,64},{33,1},{64,96},{65,33},{96,0},{97,65},{2,34}... | collective-permute-start | bytes 3932168 | tf_op jit(solution)/shard_map/ppermute | solution.py:254
  55.9 18.2 %collective-permute-start.3 = (bf16[4,128,1280]{2,1,0:T(8,128)(2,1)}, bf16[4,128,1280]{2,1,0:T(8,128)(2,1)}, u32[]{:S(2)}, u32[]{:S(2)}) collective-permute-start(bf16[4,128,1280]{2,1,0:T(8,128)(2,1)} %pad_maximum_fusion.l0), channel_id=1, source_target_pairs={{0,4},{1,13},{4,8},{5,1},{8,12},{9,5},{12,0},{13,9},{2,6},{3,15},{... | collective-permute-start | bytes 3932168 | tf_op jit(solution)/shard_map/ppermute | solution.py:254
  58.4 27.0 %collective-permute-start.8 = (bf16[4,128,1280]{2,1,0:T(8,128)(2,1)}, bf16[4,128,1280]{2,1,0:T(8,128)(2,1)}, u32[]{:S(2)}, u32[]{:S(2)}) collective-permute-start(bf16[4,128,1280]{2,1,0:T(8,128)(2,1)} %copy-done.3), channel_id=1, source_target_pairs={{0,32},{1,97},{32,64},{33,1},{64,96},{65,33},{96,0},{97,65},{2,34}... | collective-permute-start | bytes 3932168 | tf_op jit(solution)/shard_map/ppermute | solution.py:254
  58.9 32.6 %copy-start.13 = (s32[16]{0:T(128)}, s32[16]{0:T(128)S(1)}, u32[]{:S(2)}) copy-start(s32[16]{0:T(128)S(1)} %stack.58.place) | copy-start | bytes 196
  58.9 32.5 %collective-permute-start.7 = (bf16[4,128,1280]{2,1,0:T(8,128)(2,1)}, bf16[4,128,1280]{2,1,0:T(8,128)(2,1)S(1)}, u32[]{:S(2)}, u32[]{:S(2)}) collective-permute-start(bf16[4,128,1280]{2,1,0:T(8,128)(2,1)} %collective-permute-done.6.refs_1_), channel_id=1, source_target_pairs={{0,4},{1,13},{4,8},{5,1},{8,12},{9,5},{12,0},{13,9},{2,6},{3,15},{... | collective-permute-start | bytes 3932168 | tf_op jit(solution)/shard_map/ppermute | solution.py:254
  70.5 21.0 %collective-permute-start.9 = (bf16[4,128,1280]{2,1,0:T(8,128)(2,1)}, bf16[4,128,1280]{2,1,0:T(8,128)(2,1)S(1)}, u32[]{:S(2)}, u32[]{:S(2)}) collective-permute-start(bf16[4,128,1280]{2,1,0:T(8,128)(2,1)} %collective-permute-done.5.refs_2_), channel_id=1, source_target_pairs={{0,1},{1,0},{2,3},{3,2},{4,5},{5,4},{6,7},{7,6},{8,9},{9,8},{10,11... | collective-permute-start | bytes 3932168 | tf_op jit(solution)/shard_map/ppermute | solution.py:245
  87.0 4.5 %collective-permute-start.10 = (bf16[4,128,1280]{2,1,0:T(8,128)(2,1)}, bf16[4,128,1280]{2,1,0:T(8,128)(2,1)S(1)}, u32[]{:S(2)}, u32[]{:S(2)}) collective-permute-start(bf16[4,128,1280]{2,1,0:T(8,128)(2,1)} %gate.5.refs_3_), channel_id=1, source_target_pairs={{0,1},{1,0},{2,3},{3,2},{4,5},{5,4},{6,7},{7,6},{8,9},{9,8},{10,11... | collective-permute-start | bytes 3932168 | tf_op jit(solution)/shard_map/ppermute | solution.py:245
  88.2 19.9 %collective-permute-start.12 = (bf16[4,128,1280]{2,1,0:T(8,128)(2,1)}, bf16[4,128,1280]{2,1,0:T(8,128)(2,1)S(1)}, u32[]{:S(2)}, u32[]{:S(2)}) collective-permute-start(bf16[4,128,1280]{2,1,0:T(8,128)(2,1)} %collective-permute-done.5.refs_2_), channel_id=1, source_target_pairs={{0,32},{1,97},{32,64},{33,1},{64,96},{65,33},{96,0},{97,65},{2,34}... | collective-permute-start | bytes 3932168 | tf_op jit(solution)/shard_map/ppermute | solution.py:254
  90.1 21.6 %collective-permute-start.11 = (bf16[4,128,1280]{2,1,0:T(8,128)(2,1)}, bf16[4,128,1280]{2,1,0:T(8,128)(2,1)S(1)}, u32[]{:S(2)}, u32[]{:S(2)}) collective-permute-start(bf16[4,128,1280]{2,1,0:T(8,128)(2,1)} %collective-permute-done.3.l1), channel_id=1, source_target_pairs={{0,4},{1,13},{4,8},{5,1},{8,12},{9,5},{12,0},{13,9},{2,6},{3,15},{... | collective-permute-start | bytes 3932168 | tf_op jit(solution)/shard_map/ppermute | solution.py:254
  91.5 16.5 %copy-start.11 = (bf16[4,128,1280]{2,1,0:T(8,128)(2,1)}, bf16[4,128,1280]{2,1,0:T(8,128)(2,1)S(1)}, u32[]{:S(2)}) copy-start(bf16[4,128,1280]{2,1,0:T(8,128)(2,1)S(1)} %collective-permute-done.9.refs_4_) | copy-start | bytes 3932164
  91.5 16.5 %copy-start.10 = (bf16[4,128,1280]{2,1,0:T(8,128)(2,1)}, bf16[4,128,1280]{2,1,0:T(8,128)(2,1)S(1)}, u32[]{:S(2)}) copy-start(bf16[4,128,1280]{2,1,0:T(8,128)(2,1)S(1)} %collective-permute-done.7.l2) | copy-start | bytes 3932164
  91.5 16.5 %copy-start.12 = (bf16[4,128,1280]{2,1,0:T(8,128)(2,1)}, bf16[4,128,1280]{2,1,0:T(8,128)(2,1)S(1)}, u32[]{:S(2)}) copy-start(bf16[4,128,1280]{2,1,0:T(8,128)(2,1)S(1)} %collective-permute-done.10.refs_5_) | copy-start | bytes 3932164
  110.7 3.2 %collective-permute-start.13 = (bf16[4,128,1280]{2,1,0:T(8,128)(2,1)S(1)}, bf16[4,128,1280]{2,1,0:T(8,128)(2,1)}, u32[]{:S(2)}, u32[]{:S(2)}) collective-permute-start(bf16[4,128,1280]{2,1,0:T(8,128)(2,1)S(1)} %gate.7.refs_6_), channel_id=1, source_target_pairs={{0,1},{1,0},{2,3},{3,2},{4,5},{5,4},{6,7},{7,6},{8,9},{9,8},{10,11... | collective-permute-start | bytes 3932168 | tf_op jit(solution)/shard_map/ppermute | solution.py:245
  113.9 29.2 %copy-start.15 = (s32[2]{0:T(128)S(1)}, s32[2]{0:T(128)}, u32[]{:S(2)}) copy-start(s32[2]{0:T(128)} %param.14) | copy-start | bytes 28
  137.0 15.0 %all-to-all-start = ((bf16[32,16,256]{2,1,0:T(8,128)(2,1)}), bf16[32,16,256]{2,1,0:T(8,128)(2,1)S(1)}, u32[]{:S(2)}, u32[]{:S(2)}) async-start(bf16[32,16,256]{2,1,0:T(8,128)(2,1)} %bitcast.65), calls=%async_computation | async-start | bytes 524288 | tf_op jit(solution)/shard_map/all_to_all | solution.py:310
  (11 other events, 36.2 us)
Sparse Core Ops, SparseCore 0:
  27.3 25.0 all-gather.5
  54.1 51.5 all-gather.7
